TPU v7x, 32 devices: a whole 2x2x4 slice. The times are simulated.
32 devices in a mesh: bead: 8 (over y, x, core), dom: 4 (over z).
Axes of the slice: x: 2, y: 2, z: 4, core: 2. Of those that a mesh axis runs over, the one named last changes fastest.
Arguments:
- positions: float32 [8, 3, 4096], P('bead', None, 'dom')
- momenta: float32 [8, 3, 4096], P('bead', None, 'dom'), may hold values from -6 to 6
- features: float32 [64, 4096], P(None, 'dom'), may hold values from -6 to 6
- masses: float32 [4096], P('dom'), may hold values from 1 to 16
- radial_width: float32 [4], replicated, may hold values from 1 to 4
- msg_weight: bfloat16 [4, 64, 64], replicated, may hold values from -0.75 to 0.75
- update_weight: bfloat16 [64, 64], replicated, may hold values from -0.75 to 0.75
- mix_weight: bfloat16 [64, 64], replicated, may hold values from -0.75 to 0.75
- out_weight: bfloat16 [64], replicated, may hold values from -4 to 4
- counts: int32 [32], P('dom'), may hold values from 0 to 128, as said below
- pairs: int32 [2, 480], P(None, 'dom'), may hold values from 0 to 23, as said below
- npairs: int32 [4], P('dom'), may hold values from 0 to 120
- leaving: int32 [2, 256], P(None, 'dom'), may hold values from -1 to 1023, as said below
Outputs:
- forces: float32 [8, 3, 4096], P('bead', None, 'dom')
- positions_new: float32 [8, 3, 4096], P('bead', None, 'dom')
- momenta_new: float32 [8, 3, 4096], P('bead', None, 'dom')
- arrivals: float32 [8, 6, 512], P('bead', None, 'dom')
Inputs may be any that keep to these rules, and one draw needn't show every extreme that they name: Each block holds atoms in its first counts slots; the first block of every domain is full, and at least one domain has all blocks holding atoms. `pairs`: the first npairs[d] columns of domain d name a local block (row 0, 0 to 7) and an extended block (row 1) numbered over the blocks of d - 1, d, d + 1; both hold atoms and no pair appears twice; later columns are zero. Row 0 names slots of atoms leaving through the lower face, row 1 through the upper face; only occupied slots, no slot twice in a domain, both rows of a domain equally long, -1 after the used entries.
All inputs are finite; a program needn't handle non-finite values.
Results may differ from a plain program's by a relative error of at most 0.0048.
Values sent between devices are 32-bit elements; how exact they have to be, the bound alone decides.
No kernel may reach another device: no remote copies, remote signals or barrier semaphores. Data moves between devices by JAX's collectives and lax.ppermute only.
A program may use at most 64 MiB of HBM per device.

v0:
```python
from functools import partial

import jax
import jax.numpy as jnp
from jax import lax
from jax.sharding import PartitionSpec as P

F = 64
BLK = 128
MIG = 64
GROUP = 8
CELLS = 8


CUTOFF_SQUARE = 36.0
CELL_SIDE = 10.0
MESSAGE_SCALE = 0.25
SPRING_RATE = 0.2


def extended(cells, sides, width):
    for axis, dim in sides:
        count = lax.axis_size(axis)
        head = lax.slice_in_dim(cells, 0, width, axis=dim)
        tail = lax.slice_in_dim(cells, cells.shape[dim] - width, cells.shape[dim], axis=dim)
        cells = jnp.concatenate(
            [
                lax.ppermute(tail, axis, [(i, (i + 1) % count) for i in range(count)]),
                cells,
                lax.ppermute(head, axis, [((i + 1) % count, i) for i in range(count)]),
            ],
            axis=dim,
        )
    return cells


def radial_terms(squared, inverse_width):
    inside = squared < CUTOFF_SQUARE
    remain = 1.0 - squared / CUTOFF_SQUARE
    cutoff = jnp.where(inside, remain * remain, 0.0)[:, None]
    cutoff_slope = jnp.where(inside, -2.0 * remain / CUTOFF_SQUARE, 0.0)[:, None]
    widths = inverse_width[None, :, None, None]
    decays = jnp.exp(-squared[:, None] * widths)
    values = decays * cutoff
    slopes = decays * (cutoff_slope - cutoff * widths)
    return (values, slopes)


def pair_geometry(coords, row_index, column_index, same_block, weight):
    row_points = jnp.take(coords, row_index, axis=0, mode="clip")
    column_points = jnp.take(coords, column_index, axis=0, mode="clip")
    separation = row_points[:, :, :, None] - column_points[:, :, None, :]
    squared = jnp.sum(separation * separation, axis=1)
    block_size = row_points.shape[2]
    identity = (
        lax.broadcasted_iota(jnp.int32, (block_size, block_size), 0)
        == lax.broadcasted_iota(jnp.int32, (block_size, block_size), 1)
    ).astype(jnp.float32)
    keep_mask = weight[:, None, None] * (1.0 - same_block[:, None, None] * identity[None])
    return (separation, squared, keep_mask)


def clamp_index(index, limit):
    return jnp.clip(index, 0, limit - 1)


def message_group(
    coords, tables, inverse_width, summed, row_index, column_index, out_index, same_block, weight
):
    row_index = clamp_index(row_index, coords.shape[0])
    column_index = clamp_index(column_index, coords.shape[0])
    separation, squared, keep_mask = pair_geometry(
        coords, row_index, column_index, same_block, weight
    )
    values, slopes = radial_terms(squared, inverse_width)
    amplitude = (values * keep_mask[:, None]).astype(jnp.bfloat16)
    gathered = jnp.take(tables, column_index, axis=0, mode="clip")
    contrib = jnp.einsum("gfke,gkie->gfi", gathered, amplitude, preferred_element_type=jnp.float32)
    return summed.at[out_index].add(contrib)


def force_group(
    coords,
    tables,
    downstream,
    inverse_width,
    summed,
    row_index,
    column_index,
    out_index,
    same_block,
    weight,
):
    row_index = clamp_index(row_index, coords.shape[0])
    column_index = clamp_index(column_index, coords.shape[0])
    separation, squared, keep_mask = pair_geometry(
        coords, row_index, column_index, same_block, weight
    )
    values, slopes = radial_terms(squared, inverse_width)
    gathered = jnp.take(tables, column_index, axis=0, mode="clip")
    incoming = jnp.take(downstream, out_index, axis=0, mode="clip")
    pair_grad = jnp.einsum("gfi,gfke->gkie", incoming, gathered, preferred_element_type=jnp.float32)
    weighted = 2.0 * jnp.sum(pair_grad * slopes, axis=1) * keep_mask
    row_grad = jnp.sum(separation * weighted[:, None, :, :], axis=3)
    column_grad = -jnp.sum(separation * weighted[:, None, :, :], axis=2)
    return summed.at[row_index].add(row_grad).at[column_index].add(column_grad)


def tile_window(local_list, extended_list, first_tile, stop_tile, round_index):
    position = first_tile + round_index * GROUP + jnp.arange(GROUP, dtype=jnp.int32)
    weight = (position < stop_tile).astype(jnp.float32)
    clipped = jnp.minimum(position, local_list.shape[0] - 1)
    return (jnp.take(local_list, clipped), jnp.take(extended_list, clipped), weight)


def sweep(update, initial, local_list, extended_list, first_tile, stop_tile, row_base, column_base):
    rounds = (stop_tile - first_tile + GROUP - 1) // GROUP

    def advance(round_index, carried):
        local_rows, extended_columns, weight = tile_window(
            local_list, extended_list, first_tile, stop_tile, round_index
        )
        same_block = (extended_columns == local_rows + CELLS).astype(jnp.float32)
        return update(
            carried,
            local_rows + row_base,
            extended_columns + column_base,
            local_rows,
            same_block,
            weight,
        )

    return lax.fori_loop(0, rounds, advance, initial)


def project(feature_blocks, msg_weight):
    tables = jnp.einsum(
        "kgf,nfa->ngka",
        msg_weight.astype(jnp.float32),
        feature_blocks,
        precision=lax.Precision.HIGHEST,
    )
    return tables.astype(jnp.bfloat16)


def node_backward(message, own_features, occupied, update_weight, mix_weight, out_weight):
    scaled = (message * MESSAGE_SCALE).astype(jnp.bfloat16)
    first_pre = jnp.einsum("gf,cfa->cga", update_weight, scaled, preferred_element_type=jnp.float32)
    first_gate = jax.nn.sigmoid(first_pre)
    updated = (own_features + first_pre * first_gate).astype(jnp.bfloat16)
    second_pre = jnp.einsum("gf,cfa->cga", mix_weight, updated, preferred_element_type=jnp.float32)
    second_gate = jax.nn.sigmoid(second_pre)
    second_grad = (
        out_weight.astype(jnp.float32)[None, :, None]
        * second_gate
        * (1.0 + second_pre * (1.0 - second_gate))
        * occupied[:, None, :]
    ).astype(jnp.bfloat16)
    update_grad = jnp.einsum(
        "gf,cga->cfa", mix_weight, second_grad, preferred_element_type=jnp.float32
    )
    first_grad = (update_grad * first_gate * (1.0 + first_pre * (1.0 - first_gate))).astype(
        jnp.bfloat16
    )
    return (
        MESSAGE_SCALE
        * jnp.einsum("gf,cga->cfa", update_weight, first_grad, preferred_element_type=jnp.float32)
    ).astype(jnp.bfloat16)


def body(
    positions,
    momenta,
    features,
    masses,
    radial_width,
    msg_weight,
    update_weight,
    mix_weight,
    out_weight,
    counts,
    pairs,
    npairs,
    leaving,
):
    slot_index = lax.broadcasted_iota(jnp.int32, (CELLS, BLK), 1)
    occupied = (slot_index < counts[:, None]).astype(jnp.float32)
    own_features = jnp.transpose(features.reshape(F, CELLS, BLK), (1, 0, 2)) * occupied[:, None, :]
    current = positions[0]
    own_coords = jnp.transpose(current.reshape(3, CELLS, BLK), (1, 0, 2))
    vertical = jnp.array([0.0, 0.0, CELL_SIDE], dtype=jnp.float32)[:, None]
    padded = extended(own_coords, (("dom", 0),), CELLS)
    coord_ext = jnp.concatenate(
        [padded[:CELLS] - vertical, own_coords, padded[2 * CELLS :] + vertical], axis=0
    )
    widened = extended(own_features, (("dom", 0),), CELLS)
    below_features = widened[:CELLS]
    above_features = widened[2 * CELLS :]
    own_tables = project(own_features, msg_weight)
    table_ext = jnp.concatenate(
        [project(below_features, msg_weight), own_tables, project(above_features, msg_weight)],
        axis=0,
    )
    inverse_width = 1.0 / (radial_width * radial_width)
    local_list = pairs[0]
    extended_list = pairs[1]
    tile_count = npairs[0]
    empty_message = jnp.zeros((CELLS, F, BLK), jnp.float32)
    empty_ext = jnp.zeros((3 * CELLS, 3, BLK), jnp.float32)
    message = sweep(
        partial(message_group, coord_ext, table_ext, inverse_width),
        empty_message,
        local_list,
        extended_list,
        0,
        tile_count,
        CELLS,
        0,
    )
    downstream = node_backward(
        message, own_features, occupied, update_weight, mix_weight, out_weight
    )
    grad_ext = sweep(
        partial(force_group, coord_ext, table_ext, downstream, inverse_width),
        empty_ext,
        local_list,
        extended_list,
        0,
        tile_count,
        CELLS,
        0,
    )
    grad_local = grad_ext[CELLS : 2 * CELLS]
    ghost_part = jnp.concatenate([grad_ext[:CELLS], grad_ext[2 * CELLS :]], axis=0)
    returned = extended(ghost_part, (("dom", 0),), CELLS)
    own_grad = grad_local + returned[:CELLS] + returned[3 * CELLS :]
    physical = -jnp.transpose(own_grad, (1, 0, 2)).reshape(3, CELLS * BLK)
    neighbours = extended(positions, (("bead", 0),), 1)
    spring = -SPRING_RATE * masses[None, :] * (2.0 * current - neighbours[0] - neighbours[2])
    forces = physical + spring
    momenta_new = momenta[0] + forces
    positions_new = current + momenta_new / masses[None, :]
    packet = jnp.concatenate([positions_new, momenta_new], axis=0)
    movers = leaving.reshape(-1)
    present = (movers >= 0).astype(jnp.float32)
    picked = jnp.take(packet, jnp.maximum(movers, 0), axis=1)
    face_shift = jnp.where(jnp.arange(movers.shape[0]) < MIG, CELL_SIDE, -CELL_SIDE)
    height_row = (jnp.arange(6) == 2).astype(jnp.float32)
    picked = (picked + height_row[:, None] * face_shift[None, :]) * present[None, :]
    received = extended(picked[None], (("dom", 2),), MIG)
    arrivals = jnp.concatenate([received[:, :, :MIG], received[:, :, 3 * MIG :]], axis=2)
    return (forces[None], positions_new[None], momenta_new[None], arrivals)


def solution(mesh):
    in_specs = (
        P("bead", None, "dom"),
        P("bead", None, "dom"),
        P(None, "dom"),
        P("dom"),
        P(),
        P(),
        P(),
        P(),
        P(),
        P("dom"),
        P(None, "dom"),
        P("dom"),
        P(None, "dom"),
    )
    out_specs = (
        P("bead", None, "dom"),
        P("bead", None, "dom"),
        P("bead", None, "dom"),
        P("bead", None, "dom"),
    )
    return jax.shard_map(body, mesh=mesh, in_specs=in_specs, out_specs=out_specs, check_vma=False)
```

profile of v0, /device:TPU:0, one launch (start us, length us, event | category | flops | bytes accessed | tf_op | source)
XLA Modules:
  0.0 479.3 jit_solution(1266541214780585495)
XLA Ops:
  1.6 3.1 collective-permute-start.2
  6.8 3.8 collective-permute-start.1
  20.6 2.6 collective-permute-start.7
  29.0 52.8 %while.22 = (s32[]{:T(128)}, f32[8,64,128]{2,1,0:T(8,128)}, s32[]{:T(128)}, s32[120]{0:T(128)S(1)}, s32[120]{0:T(128)S(1)}, /*index=5*/bf16[24,64,4,128]{3,2,1,0...) while((s32[]{:T(128)}, f32[8,64,128]{2,1,0:T(8,128)}, ...), condition=%wide.region_3.5_spmd, body=%wide.region_0.4_spmd.sunk | while | flops 71535896 | bytes 7033785 | solution.py:133
  34.7 2.4 convolution_bitcast_fusion.5
  37.1 2.5 scatter_fusion
  45.2 2.4 convolution_bitcast_fusion.5
  47.6 2.5 scatter_fusion
  55.8 2.4 convolution_bitcast_fusion.5
  58.2 2.5 scatter_fusion
  66.3 2.4 convolution_bitcast_fusion.5
  68.8 2.5 scatter_fusion
  76.9 2.4 convolution_bitcast_fusion.5
  79.3 2.4 scatter_fusion
  84.2 92.6 %while.23 = (s32[]{:T(128)}, f32[24,3,128]{2,1,0:T(4,128)S(1)}, s32[]{:T(128)}, s32[120]{0:T(128)S(1)}, f32[24,3,128]{2,1,0:T(4,128)S(1)}, /*index=5*/s32[120]{0...) while((s32[]{:T(128)}, f32[24,3,128]{2,1,0:T(4,128)S(1)}, ...), condition=%wide.region_11.13_spmd, body=%wide.region_4.12_spmd.sunk | while | flops 74489136 | bytes 17016584 | solution.py:133
  93.5 2.1 gather_fusion.10
  97.4 2.3 fusion.77
  112.1 2.1 gather_fusion.10
  115.9 2.3 fusion.77
  134.5 2.3 fusion.77
  153.0 2.3 fusion.77
  171.5 2.3 fusion.77
  176.9 201.9 %collective-permute-start.4 = (f32[8,3,128]{2,1,0:T(4,128)S(1)}, f32[8,3,128]{2,1,0:T(4,128)S(1)}, u32[]{:S(2)}, u32[]{:S(2)}) collective-permute-start(f32[8,3,128]{2,1,0:T(4,128)S(1)} %get-tuple-element.362), channel_id=1, source_target_pairs={{0,1},{1,2},{2,3},{3,0},{4,5},{5,6},{6,7},{7,4},{8,9},{9,10},{10,1... | collective-permute-start | bytes 36872 | tf_op jit(solution)/shard_map/ppermute | solution.py:28
  382.5 86.8 %collective-permute-done.5 = f32[8,3,128]{2,1,0:T(4,128)S(1)} collective-permute-done((f32[8,3,128]{2,1,0:T(4,128)S(1)}, f32[8,3,128]{2,1,0:T(4,128)S(1)}, u32[]{:S(2)}, u32[]{:S(2)}) %collective-permute-start.5) | collective-permute-done | bytes 12320 | tf_op jit(solution)/shard_map/ppermute | solution.py:30
  (331 shorter events, 138.4 us)
Async XLA Ops:
  0.6 24.8 %copy-start.3 = (bf16[4,64,64]{2,1,0:T(8,128)(2,1)S(1)}, bf16[4,64,64]{2,1,0:T(8,128)(2,1)}, u32[]{:S(2)}) copy-start(bf16[4,64,64]{2,1,0:T(8,128)(2,1)} %param.25) | copy-start | bytes 98308
  1.6 23.8 %collective-permute-start.2 = (f32[8,64,128]{2,1,0:T(8,128)S(1)}, f32[8,64,128]{2,1,0:T(8,128)S(1)}, u32[]{:S(2)}, u32[]{:S(2)}) collective-permute-start(f32[8,64,128]{2,1,0:T(8,128)S(1)} %fusion.27), channel_id=1, source_target_pairs={{0,1},{1,2},{2,3},{3,0},{4,5},{5,6},{6,7},{7,4},{8,9},{9,10},{10,1... | collective-permute-start | bytes 786440 | tf_op jit(solution)/shard_map/ppermute | solution.py:28
  4.7 21.3 %collective-permute-start.3 = (f32[8,64,128]{2,1,0:T(8,128)S(1)}, f32[8,64,128]{2,1,0:T(8,128)S(1)}, u32[]{:S(2)}, u32[]{:S(2)}) collective-permute-start(f32[8,64,128]{2,1,0:T(8,128)S(1)} %fusion.27), channel_id=1, source_target_pairs={{1,0},{2,1},{3,2},{0,3},{5,4},{6,5},{7,6},{4,7},{9,8},{10,9},{11,1... | collective-permute-start | bytes 786440 | tf_op jit(solution)/shard_map/ppermute | solution.py:30
  6.8 13.8 %collective-permute-start = (f32[8,3,128]{2,0,1:T(8,128)}, f32[8,3,128]{2,0,1:T(8,128)S(1)}, u32[]{:S(2)}, u32[]{:S(2)}) collective-permute-start(f32[8,3,128]{2,0,1:T(8,128)} %bitcast.154), channel_id=1, source_target_pairs={{0,1},{1,2},{2,3},{3,0},{4,5},{5,6},{6,7},{7,4},{8,9},{9,10},{10,1... | collective-permute-start | bytes 36872 | tf_op jit(solution)/shard_map/ppermute | solution.py:28
  6.8 17.2 %collective-permute-start.1 = (f32[8,3,128]{2,0,1:T(8,128)}, f32[8,3,128]{2,0,1:T(8,128)S(1)}, u32[]{:S(2)}, u32[]{:S(2)}) collective-permute-start(f32[8,3,128]{2,0,1:T(8,128)} %bitcast.155), channel_id=1, source_target_pairs={{1,0},{2,1},{3,2},{0,3},{5,4},{6,5},{7,6},{4,7},{9,8},{10,9},{11,1... | collective-permute-start | bytes 36872 | tf_op jit(solution)/shard_map/ppermute | solution.py:30
  12.0 370.3 %collective-permute-start.6 = (f32[1,3,1024]{2,1,0:T(4,128)}, f32[1,3,1024]{2,1,0:T(4,128)}, u32[]{:S(2)}, u32[]{:S(2)}) collective-permute-start(f32[1,3,1024]{2,1,0:T(4,128)} %copy.118), channel_id=1, source_target_pairs={{0,4},{4,8},{8,12},{12,16},{16,20},{20,24},{24,28},{28,0},{1,5},{5... | collective-permute-start | bytes 36872 | tf_op jit(solution)/shard_map/ppermute | solution.py:28
  20.6 361.7 %collective-permute-start.7 = (f32[1,3,1024]{2,1,0:T(4,128)}, f32[1,3,1024]{2,1,0:T(4,128)}, u32[]{:S(2)}, u32[]{:S(2)}) collective-permute-start(f32[1,3,1024]{2,1,0:T(4,128)} %copy.118), channel_id=1, source_target_pairs={{4,0},{8,4},{12,8},{16,12},{20,16},{24,20},{28,24},{0,28},{5,1},{9... | collective-permute-start | bytes 36872 | tf_op jit(solution)/shard_map/ppermute | solution.py:30
  29.0 52.8 %copy-start.7 = (bf16[64,64]{1,0:T(8,128)(2,1)S(1)}, bf16[64,64]{1,0:T(8,128)(2,1)}, u32[]{:S(2)}) copy-start(bf16[64,64]{1,0:T(8,128)(2,1)} %param.26) | copy-start | bytes 24580
  29.0 53.9 %copy-start.9 = (bf16[64,64]{1,0:T(8,128)(2,1)S(1)}, bf16[64,64]{1,0:T(8,128)(2,1)}, u32[]{:S(2)}) copy-start(bf16[64,64]{1,0:T(8,128)(2,1)} %param.27) | copy-start | bytes 24580
  90.8 6.6 %copy-start.1 = (f32[8,128,128]{1,2,0:T(8,128)S(1)}, f32[8,128,128]{1,2,0:T(8,128)}, u32[]{:S(2)}) copy-start(f32[8,128,128]{1,2,0:T(8,128)} %copy.174) | copy-start | bytes 1572868 | tf_op jit(solution)/shard_map/while
  91.8 5.6 %copy-start.2 = (f32[8,128,128]{1,2,0:T(8,128)S(1)}, f32[8,128,128]{1,2,0:T(8,128)}, u32[]{:S(2)}) copy-start(f32[8,128,128]{1,2,0:T(8,128)} %copy.175) | copy-start | bytes 1572868 | tf_op jit(solution)/shard_map/while
  97.4 2.5 copy-start.4
  109.4 6.6 %copy-start.1 = (f32[8,128,128]{1,2,0:T(8,128)S(1)}, f32[8,128,128]{1,2,0:T(8,128)}, u32[]{:S(2)}) copy-start(f32[8,128,128]{1,2,0:T(8,128)} %copy.174) | copy-start | bytes 1572868 | tf_op jit(solution)/shard_map/while
  110.4 5.6 %copy-start.2 = (f32[8,128,128]{1,2,0:T(8,128)S(1)}, f32[8,128,128]{1,2,0:T(8,128)}, u32[]{:S(2)}) copy-start(f32[8,128,128]{1,2,0:T(8,128)} %copy.175) | copy-start | bytes 1572868 | tf_op jit(solution)/shard_map/while
  127.9 6.6 %copy-start.1 = (f32[8,128,128]{1,2,0:T(8,128)S(1)}, f32[8,128,128]{1,2,0:T(8,128)}, u32[]{:S(2)}) copy-start(f32[8,128,128]{1,2,0:T(8,128)} %copy.174) | copy-start | bytes 1572868 | tf_op jit(solution)/shard_map/while
  128.9 5.6 %copy-start.2 = (f32[8,128,128]{1,2,0:T(8,128)S(1)}, f32[8,128,128]{1,2,0:T(8,128)}, u32[]{:S(2)}) copy-start(f32[8,128,128]{1,2,0:T(8,128)} %copy.175) | copy-start | bytes 1572868 | tf_op jit(solution)/shard_map/while
  146.4 6.6 %copy-start.1 = (f32[8,128,128]{1,2,0:T(8,128)S(1)}, f32[8,128,128]{1,2,0:T(8,128)}, u32[]{:S(2)}) copy-start(f32[8,128,128]{1,2,0:T(8,128)} %copy.174) | copy-start | bytes 1572868 | tf_op jit(solution)/shard_map/while
  147.4 5.6 %copy-start.2 = (f32[8,128,128]{1,2,0:T(8,128)S(1)}, f32[8,128,128]{1,2,0:T(8,128)}, u32[]{:S(2)}) copy-start(f32[8,128,128]{1,2,0:T(8,128)} %copy.175) | copy-start | bytes 1572868 | tf_op jit(solution)/shard_map/while
  164.9 6.6 %copy-start.1 = (f32[8,128,128]{1,2,0:T(8,128)S(1)}, f32[8,128,128]{1,2,0:T(8,128)}, u32[]{:S(2)}) copy-start(f32[8,128,128]{1,2,0:T(8,128)} %copy.174) | copy-start | bytes 1572868 | tf_op jit(solution)/shard_map/while
  165.9 5.6 %copy-start.2 = (f32[8,128,128]{1,2,0:T(8,128)S(1)}, f32[8,128,128]{1,2,0:T(8,128)}, u32[]{:S(2)}) copy-start(f32[8,128,128]{1,2,0:T(8,128)} %copy.175) | copy-start | bytes 1572868 | tf_op jit(solution)/shard_map/while
  176.9 205.6 %collective-permute-start.4 = (f32[8,3,128]{2,1,0:T(4,128)S(1)}, f32[8,3,128]{2,1,0:T(4,128)S(1)}, u32[]{:S(2)}, u32[]{:S(2)}) collective-permute-start(f32[8,3,128]{2,1,0:T(4,128)S(1)} %get-tuple-element.362), channel_id=1, source_target_pairs={{0,1},{1,2},{2,3},{3,0},{4,5},{5,6},{6,7},{7,4},{8,9},{9,10},{10,1... | collective-permute-start | bytes 36872 | tf_op jit(solution)/shard_map/ppermute | solution.py:28
  378.7 90.5 %collective-permute-start.5 = (f32[8,3,128]{2,1,0:T(4,128)S(1)}, f32[8,3,128]{2,1,0:T(4,128)S(1)}, u32[]{:S(2)}, u32[]{:S(2)}) collective-permute-start(f32[8,3,128]{2,1,0:T(4,128)S(1)} %get-tuple-element.363), channel_id=1, source_target_pairs={{1,0},{2,1},{3,2},{0,3},{5,4},{6,5},{7,6},{4,7},{9,8},{10,9},{11,1... | collective-permute-start | bytes 36872 | tf_op jit(solution)/shard_map/ppermute | solution.py:30
  471.9 6.5 %collective-permute-start.8 = (f32[1,6,64]{1,2,0:T(8,128)S(1)}, f32[1,6,64]{1,2,0:T(8,128)S(1)}, u32[]{:S(2)}, u32[]{:S(2)}) collective-permute-start(f32[1,6,64]{1,2,0:T(8,128)S(1)} %get-tuple-element.360), channel_id=1, source_target_pairs={{0,1},{1,2},{2,3},{3,0},{4,5},{5,6},{6,7},{7,4},{8,9},{9,10},{10,1... | collective-permute-start | bytes 4616 | tf_op jit(solution)/shard_map/ppermute | solution.py:28
  474.0 4.5 collective-permute-start.9
  (21 other events, 39.7 us)
where the time goes:
time: 482 us; the launch traced here: 479 us
  starting transfers between devices  219 us (45%)
  waiting for transfers between devices  87 us (18%)
  local copies, waits for them, and re-layouts  77.7 us (16%)
  other arithmetic  63.9 us (13%)
  matrix products  28.6 us (6%)
    ppermute x5, starting transfers between devices, extended(): lax.ppermute(tail, axis, [(i, (i + 1) % count) for i in range(count)])  207 us
    ppermute x5, waiting for transfers between devices, extended(): lax.ppermute(head, axis, [((i + 1) % count, i) for i in range(count)])  86.8 us
    ppermute x5, starting transfers between devices, extended(): lax.ppermute(head, axis, [((i + 1) % count, i) for i in range(count)])  12.5 us
    scatter-add x5, other arithmetic, message_group(): return summed.at[out_index].add(contrib)  12.3 us
    dot_general x5, matrix products, message_group(): jnp.einsum('gfke,gkie->gfi', gathered, amplitude, preferred_element_type=...  12.1 us
    dot_general x5, matrix products, force_group(): jnp.einsum('gfi,gfke->gkie', incoming, gathered, preferred_element_type=j...  11.4 us
    gather x5, local copies, waits for them, and re-layouts, force_group(): incoming = jnp.take(downstream, out_index, axis=0, mode='clip')  10.6 us
  transfers between devices with their start and end apart: 10, of which 2 were waited for; matrix products, arithmetic and copies ran while one was open for 35% of the time, Pallas kernels for 0%

commit v1 on v0

v1 whole, which is shorter than its diff:
```python
from functools import partial

import jax
import jax.numpy as jnp
from jax import lax
from jax.experimental import pallas as pl
from jax.experimental.pallas import tpu as pltpu
from jax.sharding import PartitionSpec as P

F = 64
RAD = 4
BLK = 128
MIG = 64
CELLS = 8
ATOMS_DEV = CELLS * BLK
PACK = 72

CUTOFF_SQUARE = 36.0
CELL_SIDE = 10.0
MESSAGE_SCALE = 0.25
SPRING_RATE = 0.2
LOG2E = 1.4426950408889634
FAR = 1.0e9
CHUNK = 16

f32 = jnp.float32
bf16 = jnp.bfloat16
VMEM = pl.BlockSpec(memory_space=pltpu.VMEM)
SMEM = pl.BlockSpec(memory_space=pltpu.SMEM)
PARAMS = pltpu.CompilerParams(vmem_limit_bytes=48 * 1024 * 1024)


def dot(a, b, dims=((1,), (0,))):
    return lax.dot_general(a, b, (dims, ((), ())), preferred_element_type=f32)


def halves(x):
    high = x.astype(bf16)
    return high, (x - high.astype(f32)).astype(bf16)


def block_lanes(x, b):
    return x[:, b * BLK : (b + 1) * BLK]


def pack_kernel(features, positions, counts, packed):
    lane = lax.broadcasted_iota(jnp.int32, (1, BLK), 1)
    for b in range(CELLS):
        cols = slice(b * BLK, (b + 1) * BLK)
        keep = (lane < counts[b]).astype(f32)
        packed[0:F, cols] = features[:, cols] * keep
        packed[F : F + 3, cols] = positions[0, :, cols]
        packed[F + 3 : PACK, cols] = jnp.zeros((PACK - F - 3, BLK), f32)


def split_lists(pairs, npairs, own_list, ghost_list, tallies):
    def step(p, carry):
        own, ghost = carry
        i = pairs[0, p]
        j = pairs[1, p]
        mine = jnp.logical_and(j >= CELLS, j < 2 * CELLS)
        shifted = jnp.where(mine, j - CELLS, jnp.where(j >= 2 * CELLS, j - CELLS, j))
        code = i * 16 + shifted
        own_list[own] = code
        ghost_list[ghost] = code
        taken = mine.astype(jnp.int32)
        return own + taken, ghost + 1 - taken

    own, ghost = lax.fori_loop(0, npairs[0], step, (jnp.int32(0), jnp.int32(0)))
    for extra in range(4):
        own_list[own + extra] = CELLS * 16
        ghost_list[ghost + extra] = CELLS * 16
    tallies[0] = own
    tallies[1] = ghost


def fill_tables(packed, weight, tables, base):
    high, low = halves(packed[0:F, :])
    stacked = jnp.concatenate([high, low], axis=0)
    result = dot(weight, stacked)
    for b in range(CELLS):
        for k in range(RAD):
            tables[base + b, :, k * BLK : (k + 1) * BLK] = block_lanes(
                result[k * F : (k + 1) * F], b
            ).astype(bf16)


def fill_transposed(packed, turned, base):
    x = packed[0:F, :]
    high = x.astype(bf16).astype(f32)
    stacked = jnp.concatenate([high, x - high], axis=0)
    for b in range(CELLS):
        turned[base + b] = block_lanes(stacked, b).T.astype(bf16)


def fill_rows(packed, rows):
    for b in range(CELLS):
        rows[b, 0:3, :] = packed[F : F + 3, b * BLK : (b + 1) * BLK]
    rows[CELLS] = jnp.zeros((8, BLK), f32)


def fill_columns(sources, columns):
    pieces = []
    for packed, shift in sources:
        third = lax.broadcasted_iota(jnp.int32, (3, BLK), 0) == 2
        for b in range(CELLS):
            piece = packed[F : F + 3, b * BLK : (b + 1) * BLK]
            if shift:
                piece = piece + jnp.where(third, shift, 0.0)
            pieces.append(piece)
    used = 3 * len(pieces)
    pieces.append(jnp.zeros((BLK - used, BLK), f32))
    turned = jnp.concatenate(pieces, axis=0).T
    for n in range(used):
        columns[n // 3, n % 3] = jnp.broadcast_to(turned[:, n : n + 1], (BLK, BLK))


def fill_penalty(penalty):
    same = lax.broadcasted_iota(jnp.int32, (BLK, BLK), 0) == lax.broadcasted_iota(
        jnp.int32, (BLK, BLK), 1
    )
    penalty[0] = jnp.zeros((BLK, BLK), f32)
    penalty[1] = jnp.where(same, FAR, 0.0)


def inverse_widths(radial_width):
    return [1.0 / (radial_width[k] * radial_width[k]) for k in range(RAD)]


def decode(pair_list, p):
    code = pair_list[p]
    return lax.shift_right_logical(code, 4), lax.bitwise_and(code, 15)


def separation(rows, columns, penalty, i, j, place):
    parts = [rows[i, c : c + 1, :] - columns[j, c, place, :] for c in range(3)]
    squared = parts[0] * parts[0] + parts[1] * parts[1] + parts[2] * parts[2]
    if penalty is not None:
        squared = squared + penalty[(i == j).astype(jnp.int32), place, :]
    remain = jnp.maximum(1.0 - squared * (1.0 / CUTOFF_SQUARE), 0.0)
    return parts, squared, remain


def message_pass(pair_list, count, rows, columns, penalty, rates, tables, amps, message):
    def amplitudes(p, amp):
        i, j = decode(pair_list, p)
        for r in range(BLK // CHUNK):
            place = slice(r * CHUNK, (r + 1) * CHUNK)
            _, squared, remain = separation(rows, columns, penalty, i, j, place)
            cutoff = remain * remain
            for k in range(RAD):
                value = jnp.exp2(squared * rates[k]) * cutoff
                amp[k * BLK + r * CHUNK : k * BLK + (r + 1) * CHUNK, :] = value.astype(bf16)

    def multiply(p, amp):
        i, j = decode(pair_list, p)
        message[i] += dot(tables[j], amp[...])

    amp_a, amp_b = amps

    @pl.when(count > 0)
    def _():
        amplitudes(0, amp_a)

    def step(t, carry):
        multiply(2 * t, amp_a)
        amplitudes(2 * t + 1, amp_b)
        multiply(2 * t + 1, amp_b)
        amplitudes(2 * t + 2, amp_a)
        return carry

    lax.fori_loop(0, (count + 1) // 2, step, 0)


def force_pass(
    pair_list, count, rows, columns, penalty, rates, doubled, turned, down, grads, row_sum, column_sum
):
    lane = lax.broadcasted_iota(jnp.int32, (CHUNK, BLK), 1)

    def products(p, grad):
        i, j = decode(pair_list, p)
        right = down[i]
        grad[...] = dot(turned[j], jnp.concatenate([right, right], axis=0))

    def apply(p, grad):
        i, j = decode(pair_list, p)
        marks = [lane == 3 * j + c for c in range(3)]
        sums = [jnp.zeros((CHUNK, BLK), f32) for _ in range(3)]
        for r in range(BLK // CHUNK):
            place = slice(r * CHUNK, (r + 1) * CHUNK)
            parts, squared, remain = separation(rows, columns, penalty, i, j, place)
            plain = None
            scaled = None
            for k in range(RAD):
                term = jnp.exp2(squared * rates[k]) * grad[place, k * BLK : (k + 1) * BLK]
                plain = term if plain is None else plain + term
                term = term * doubled[k]
                scaled = term if scaled is None else scaled + term
            weighted = remain * (plain + remain * scaled)
            pulls = [weighted * part for part in parts]
            sums = [s + pull for s, pull in zip(sums, pulls)]
            totals = [jnp.sum(pull, axis=1, keepdims=True) for pull in pulls]
            placed = jnp.where(
                marks[0],
                totals[0],
                jnp.where(marks[1], totals[1], jnp.where(marks[2], totals[2], 0.0)),
            )
            column_sum[place, :] += placed
        for c in range(3):
            row_sum[i, c] += sums[c]

    grad_a, grad_b = grads

    @pl.when(count > 0)
    def _():
        products(0, grad_a)

    def step(t, carry):
        products(2 * t + 1, grad_b)
        apply(2 * t, grad_a)
        products(2 * t + 2, grad_a)
        apply(2 * t + 1, grad_b)
        return carry

    lax.fori_loop(0, (count + 1) // 2, step, 0)


def own_message_kernel(
    packed,
    pairs,
    npairs,
    radial_width,
    weight,
    message,
    own_list,
    ghost_list,
    tallies,
    tables,
    rows,
    columns,
    penalty,
    amp_a,
    amp_b,
):
    split_lists(pairs, npairs, own_list, ghost_list, tallies)
    fill_tables(packed, jnp.concatenate([weight[...], weight[...]], axis=1), tables, 0)
    fill_rows(packed, rows)
    fill_columns([(packed, 0.0)], columns)
    fill_penalty(penalty)
    message[...] = jnp.zeros(message.shape, f32)
    rates = [-LOG2E * inverse for inverse in inverse_widths(radial_width)]
    message_pass(
        own_list, tallies[0], rows, columns, penalty, rates, tables, (amp_a, amp_b), message
    )


def node_backward(
    message, packed, counts, weight, update_weight, mix_weight, out_weight, down
):
    whole = jnp.concatenate([message[b] for b in range(CELLS)], axis=1)
    scaled = (whole * MESSAGE_SCALE).astype(bf16)
    first_pre = dot(update_weight[...], scaled)
    first_gate = jax.nn.sigmoid(first_pre)
    updated = (packed[0:F, :] + first_pre * first_gate).astype(bf16)
    second_pre = dot(mix_weight[...], updated)
    second_gate = jax.nn.sigmoid(second_pre)
    lane = lax.broadcasted_iota(jnp.int32, (1, BLK), 1)
    occupied = jnp.concatenate([(lane < counts[b]).astype(f32) for b in range(CELLS)], axis=1)
    second_grad = (
        out_weight[...].astype(f32)
        * second_gate
        * (1.0 + second_pre * (1.0 - second_gate))
        * occupied
    ).astype(bf16)
    update_grad = dot(mix_weight[...], second_grad, ((0,), (0,)))
    first_grad = (update_grad * first_gate * (1.0 + first_pre * (1.0 - first_gate))).astype(bf16)
    downstream = (MESSAGE_SCALE * dot(update_weight[...], first_grad, ((0,), (0,)))).astype(bf16)
    for k in range(RAD):
        mixed = dot(weight[k * F : (k + 1) * F, :], downstream, ((0,), (0,)))
        mixed = (mixed * (4.0 / CUTOFF_SQUARE)).astype(bf16)
        for b in range(CELLS):
            down[b, :, k * BLK : (k + 1) * BLK] = block_lanes(mixed, b)
    down[CELLS] = jnp.zeros((F, RAD * BLK), bf16)


def doubled_rates(inverse):
    return [value * (0.5 * CUTOFF_SQUARE) for value in inverse]


def collect_rows(row_sum, out, start=None):
    for b in range(CELLS):
        for c in range(3):
            total = jnp.sum(row_sum[b, c], axis=0, keepdims=True)
            n = 3 * b + c
            out[n : n + 1, :] = total if start is None else total + start[n : n + 1, :]


def ghost_kernel(
    packed,
    below,
    above,
    own_message,
    ghost_list,
    tallies,
    counts,
    radial_width,
    weight,
    update_weight,
    mix_weight,
    out_weight,
    row_force,
    ghost_below,
    ghost_above,
    down,
    message,
    tables,
    turned,
    rows,
    columns,
    amp_a,
    amp_b,
    grad_a,
    grad_b,
    row_sum,
    column_sum,
):
    doubled_weight = jnp.concatenate([weight[...], weight[...]], axis=1)
    fill_tables(below, doubled_weight, tables, 0)
    fill_tables(above, doubled_weight, tables, CELLS)
    fill_rows(packed, rows)
    fill_columns([(below, -CELL_SIDE), (above, CELL_SIDE)], columns)
    message[...] = own_message[...]
    inverse = inverse_widths(radial_width)
    rates = [-LOG2E * value for value in inverse]
    count = tallies[1]
    message_pass(
        ghost_list, count, rows, columns, None, rates, tables, (amp_a, amp_b), message
    )
    fill_transposed(below, turned, 0)
    fill_transposed(above, turned, CELLS)
    node_backward(message, packed, counts, weight, update_weight, mix_weight, out_weight, down)
    row_sum[...] = jnp.zeros(row_sum.shape, f32)
    column_sum[...] = jnp.zeros(column_sum.shape, f32)
    force_pass(
        ghost_list,
        count,
        rows,
        columns,
        None,
        rates,
        doubled_rates(inverse),
        turned,
        down,
        (grad_a, grad_b),
        row_sum,
        column_sum,
    )
    collect_rows(row_sum, row_force)
    flat = column_sum[...].T
    ghost_below[...] = flat[0:24]
    ghost_above[...] = flat[24:48]


def own_force_kernel(
    packed,
    row_force,
    down,
    own_list,
    tallies,
    radial_width,
    force,
    turned,
    rows,
    columns,
    penalty,
    grad_a,
    grad_b,
    row_sum,
    column_sum,
):
    fill_rows(packed, rows)
    fill_columns([(packed, 0.0)], columns)
    fill_penalty(penalty)
    fill_transposed(packed, turned, 0)
    row_sum[...] = jnp.zeros(row_sum.shape, f32)
    column_sum[...] = jnp.zeros(column_sum.shape, f32)
    inverse = inverse_widths(radial_width)
    rates = [-LOG2E * value for value in inverse]
    force_pass(
        own_list,
        tallies[0],
        rows,
        columns,
        penalty,
        rates,
        doubled_rates(inverse),
        turned,
        down,
        (grad_a, grad_b),
        row_sum,
        column_sum,
    )
    collect_rows(row_sum, force, row_force[...] - column_sum[...].T[0:24])


def finish_kernel(
    force,
    from_above,
    from_below,
    positions,
    momenta,
    before,
    after,
    masses,
    leaving,
    forces,
    positions_new,
    momenta_new,
    upward,
    downward,
):
    pair_force = force[...] - from_above[...] - from_below[...]
    physical = jnp.concatenate([pair_force[3 * b : 3 * b + 3, :] for b in range(CELLS)], axis=1)
    mass = masses[...]
    current = positions[0]
    spring = -SPRING_RATE * mass * (2.0 * current - before[0] - after[0])
    total = physical + spring
    moved = momenta[0] + total
    placed = current + moved / mass
    forces[0] = total
    momenta_new[0] = moved
    positions_new[0] = placed
    movers = jnp.concatenate([leaving[1:2, :], leaving[0:1, :]], axis=1)
    slot = lax.broadcasted_iota(jnp.int32, (ATOMS_DEV, 2 * MIG), 0)
    chosen = (slot == movers).astype(f32).astype(bf16)
    packet = jnp.concatenate([placed, moved, jnp.zeros((2, ATOMS_DEV), f32)], axis=0)
    high = packet.astype(bf16)
    middle, third = halves(packet - high.astype(f32))
    picked = dot(high, chosen) + (dot(middle, chosen) + dot(third, chosen))
    lane = lax.broadcasted_iota(jnp.int32, (8, 2 * MIG), 1)
    row = lax.broadcasted_iota(jnp.int32, (8, 2 * MIG), 0)
    shift = jnp.where(lane < MIG, -CELL_SIDE, CELL_SIDE)
    present = movers >= 0
    shifted = jnp.where(present, picked + jnp.where(row == 2, shift, 0.0), 0.0)
    upward[0] = jnp.where(lane < MIG, shifted, 0.0)[0:6]
    downward[0] = jnp.where(lane < MIG, 0.0, shifted)[0:6]


def shape(dims, kind=f32):
    return jax.ShapeDtypeStruct(dims, kind)


def body(
    positions,
    momenta,
    features,
    masses,
    radial_width,
    msg_weight,
    update_weight,
    mix_weight,
    out_weight,
    counts,
    pairs,
    npairs,
    leaving,
):
    def ring(axis, step):
        count = lax.axis_size(axis)
        return [(i, (i + step) % count) for i in range(count)]

    weight = msg_weight.reshape(RAD * F, F)
    packed = pl.pallas_call(
        pack_kernel,
        out_shape=shape((PACK, ATOMS_DEV)),
        in_specs=[VMEM, VMEM, SMEM],
        out_specs=VMEM,
        compiler_params=PARAMS,
    )(features, positions, counts)
    below = lax.ppermute(packed, "dom", ring("dom", 1))
    above = lax.ppermute(packed, "dom", ring("dom", -1))
    before = lax.ppermute(positions, "bead", ring("bead", 1))
    after = lax.ppermute(positions, "bead", ring("bead", -1))

    amp = pltpu.VMEM((RAD * BLK, BLK), bf16)
    grad = pltpu.VMEM((BLK, RAD * BLK), f32)
    rows = pltpu.VMEM((CELLS + 1, 8, BLK), f32)
    row_sum = pltpu.VMEM((CELLS + 1, 3, CHUNK, BLK), f32)
    column_sum = pltpu.VMEM((BLK, BLK), f32)
    penalty = pltpu.VMEM((2, BLK, BLK), f32)
    listed = shape((pairs.shape[1] + 8,), jnp.int32)

    def columns(blocks):
        return pltpu.VMEM((blocks, 3, BLK, BLK), f32)

    def tables(blocks):
        return pltpu.VMEM((blocks, F, RAD * BLK), bf16)

    def turned(blocks):
        return pltpu.VMEM((blocks, BLK, BLK), bf16)

    own_message, own_list, ghost_list, tallies = pl.pallas_call(
        own_message_kernel,
        out_shape=(shape((CELLS + 1, F, BLK)), listed, listed, shape((2,), jnp.int32)),
        in_specs=[VMEM, SMEM, SMEM, SMEM, VMEM],
        out_specs=(VMEM, SMEM, SMEM, SMEM),
        scratch_shapes=[tables(CELLS), rows, columns(CELLS), penalty, amp, amp],
        compiler_params=PARAMS,
    )(packed, pairs, npairs, radial_width, weight)
    row_force, ghost_below, ghost_above, down = pl.pallas_call(
        ghost_kernel,
        out_shape=(
            shape((24, BLK)),
            shape((24, BLK)),
            shape((24, BLK)),
            shape((CELLS + 1, F, RAD * BLK), bf16),
        ),
        in_specs=[VMEM] * 4 + [SMEM] * 4 + [VMEM] * 4,
        out_specs=(VMEM,) * 4,
        scratch_shapes=[
            pltpu.VMEM((CELLS + 1, F, BLK), f32),
            tables(2 * CELLS),
            turned(2 * CELLS),
            rows,
            columns(2 * CELLS),
            amp,
            amp,
            grad,
            grad,
            row_sum,
            column_sum,
        ],
        compiler_params=PARAMS,
    )(
        packed,
        below,
        above,
        own_message,
        ghost_list,
        tallies,
        counts,
        radial_width,
        weight,
        update_weight,
        mix_weight,
        out_weight.reshape(F, 1),
    )
    from_above = lax.ppermute(ghost_below, "dom", ring("dom", -1))
    from_below = lax.ppermute(ghost_above, "dom", ring("dom", 1))
    force = pl.pallas_call(
        own_force_kernel,
        out_shape=shape((24, BLK)),
        in_specs=[VMEM] * 3 + [SMEM] * 3,
        out_specs=VMEM,
        scratch_shapes=[
            turned(CELLS),
            rows,
            columns(CELLS),
            penalty,
            grad,
            grad,
            row_sum,
            column_sum,
        ],
        compiler_params=PARAMS,
    )(packed, row_force, down, own_list, tallies, radial_width)
    whole = shape((1, 3, ATOMS_DEV))
    packet = shape((1, 6, 2 * MIG))
    forces, positions_new, momenta_new, upward, downward = pl.pallas_call(
        finish_kernel,
        out_shape=(whole, whole, whole, packet, packet),
        in_specs=[VMEM] * 9,
        out_specs=(VMEM,) * 5,
        compiler_params=PARAMS,
    )(
        force,
        from_above,
        from_below,
        positions,
        momenta,
        before,
        after,
        masses.reshape(1, ATOMS_DEV),
        leaving,
    )
    arrivals = lax.ppermute(upward, "dom", ring("dom", 1)) + lax.ppermute(
        downward, "dom", ring("dom", -1)
    )
    return forces, positions_new, momenta_new, arrivals


def solution(mesh):
    split = P("bead", None, "dom")
    in_specs = (
        split,
        split,
        P(None, "dom"),
        P("dom"),
        P(),
        P(),
        P(),
        P(),
        P(),
        P("dom"),
        P(None, "dom"),
        P("dom"),
        P(None, "dom"),
    )
    out_specs = (split, split, split, split)
    return jax.shard_map(body, mesh=mesh, in_specs=in_specs, out_specs=out_specs, check_vma=False)
```

time: 482 us -> 65.5 us (0.14)
  starting transfers between devices: 219 us -> 25.2 us
  waiting for transfers between devices: 87 us -> 11.6 us
  local copies, waits for them, and re-layouts: 77.7 us -> 5.56 us
  other arithmetic: 63.9 us -> 0.01 us
  matrix products: 28.6 us -> 0 us
  Pallas kernels: 0 us -> 21.5 us
    ppermute x10 -> x8, starting transfers between devices: 219 us -> 25.2 us  [the longest x1 10.3 us: body(): from_above = lax.ppermute(ghost_below, 'dom', ring('dom', -1))]
    ppermute x10 -> x8, waiting for transfers between devices: 87 us -> 11.6 us  [the longest x1 6.48 us: body(): from_below = lax.ppermute(ghost_above, 'dom', ring('dom', 1))]
    gather x56 -> x0, local copies, waits for them, and re-layouts: 53.3 us -> none  [the longest x5 10.6 us: force_group(): incoming = jnp.take(downstream, out_index, axis=0, mode='clip')]
    dot_general x16 -> x0, matrix products: 28.6 us -> none  [the longest x5 12.1 us: message_group(): jnp.einsum('gfke,gkie->gfi', gathered, amplitude, preferred_element_type=...]
    pallas_call x0 -> x5, Pallas kernels: none -> 21.5 us  [the longest x1 14.2 us: body(): pl.pallas_call(ghost_kernel, out_shape=(shape((24, BLK)), shape((24, BLK)...]
    scatter-add x15 -> x0, other arithmetic: 20.1 us -> none  [the longest x5 12.3 us: message_group(): return summed.at[out_index].add(contrib)]
    convert_element_type x23 -> x0, other arithmetic: 11.6 us -> none  [the longest x10 9.51 us: advance(): same_block = (extended_columns == local_rows + CELLS).astype(jnp.float32)]
    select_n x10 -> x0, local copies, waits for them, and re-layouts: 9.95 us -> none  [the longest x5 4.99 us: radial_terms(): cutoff = jnp.where(inside, remain * remain, 0.0)[:, None]]
  transfers between devices with their start and end apart: 10 -> 8, of which waited for: 2 -> 3; matrix products, arithmetic and copies ran while one was open for 35% -> 3% of each run, Pallas kernels for 0% -> 32%
where the time goes in v1:
time: 65.5 us; the launch traced here: 65.3 us
  starting transfers between devices  25.2 us (38%)
  Pallas kernels  21.5 us (33%)
  waiting for transfers between devices  11.6 us (18%)
  local copies, waits for them, and re-layouts  5.56 us (8%)
  between operations  1.41 us (2%)
    pallas_call x1, Pallas kernels, body(): pl.pallas_call(ghost_kernel, out_shape=(shape((24, BLK)), shape((24, BLK)...  14.2 us
    ppermute x1, starting transfers between devices, body(): from_above = lax.ppermute(ghost_below, 'dom', ring('dom', -1))  10.3 us
    ppermute x1, waiting for transfers between devices, body(): from_below = lax.ppermute(ghost_above, 'dom', ring('dom', 1))  6.48 us
    ppermute x1, starting transfers between devices, body(): lax.ppermute(upward, 'dom', ring('dom', 1))  6.16 us
    unnamed x28, local copies, waits for them, and re-layouts  5.45 us
    ppermute x1, waiting for transfers between devices, body(): above = lax.ppermute(packed, 'dom', ring('dom', -1))  4.25 us
    pallas_call x1, Pallas kernels, body(): pl.pallas_call(own_message_kernel, out_shape=(shape((CELLS + 1, F, BLK)),...  3.66 us
    ppermute x1, starting transfers between devices, body(): below = lax.ppermute(packed, 'dom', ring('dom', 1))  3.08 us
  transfers between devices with their start and end apart: 8, of which 3 were waited for; matrix products, arithmetic and copies ran while one was open for 3% of the time, Pallas kernels for 32%

profile of v1, /device:TPU:0, one launch (start us, length us, event | category | flops | bytes accessed | tf_op | source)
XLA Modules:
  0.0 65.3 jit_solution(16363945789364500535)
XLA Ops:
  0.6 0.7 %copy.17.positions = f32[1,3,1024]{2,1,0:T(4,128)S(1)} copy(f32[1,3,1024]{2,0,1:T(1,128)} %param.13) | data formatting | bytes 24576 | tf_op args[0]
  1.4 0.9 %copy-done.1 = f32[64,1024]{1,0:T(8,128)S(1)} copy-done((f32[64,1024]{1,0:T(8,128)S(1)}, f32[64,1024]{1,0:T(8,128)}, u32[]{:S(2)}) %copy-start.1) | copy-done | bytes 262168
  2.3 0.6 shard_map.156.packed
  2.9 3.1 %collective-permute-start = (f32[72,1024]{1,0:T(8,128)S(1)}, f32[72,1024]{1,0:T(8,128)S(1)}, u32[]{:S(2)}, u32[]{:S(2)}) collective-permute-start(f32[72,1024]{1,0:T(8,128)S(1)} %shard_map.156.packed), channel_id=1, source_target_pairs={{0,1},{1,2},{2,3},{3,0},{4,5},{5,6},{6,7},{7,4},{8,9},{9,10},{10,1... | collective-permute-start | bytes 884744 | tf_op jit(solution)/shard_map/ppermute | solution.py:480
  6.0 2.1 %collective-permute-start.1 = (f32[72,1024]{1,0:T(8,128)S(1)}, f32[72,1024]{1,0:T(8,128)S(1)}, u32[]{:S(2)}, u32[]{:S(2)}) collective-permute-start(f32[72,1024]{1,0:T(8,128)S(1)} %shard_map.156.packed), channel_id=1, source_target_pairs={{0,3},{1,0},{2,1},{3,2},{4,7},{5,4},{6,5},{7,6},{8,11},{9,8},{10,9... | collective-permute-start | bytes 884744 | tf_op jit(solution)/shard_map/ppermute | solution.py:481
  8.1 2.6 %collective-permute-start.5 = (f32[1,3,1024]{2,1,0:T(4,128)S(1)}, f32[1,3,1024]{2,1,0:T(4,128)S(1)}, u32[]{:S(2)}, u32[]{:S(2)}) collective-permute-start(f32[1,3,1024]{2,1,0:T(4,128)S(1)} %copy.17.positions), channel_id=1, source_target_pairs={{0,28},{4,0},{8,4},{12,8},{16,12},{20,16},{24,20},{28,24},{1,29},{... | collective-permute-start | bytes 36872 | tf_op jit(solution)/shard_map/ppermute | solution.py:483
  11.4 0.6 copy-done.10
  12.0 0.1 copy.18.out_weight
  12.1 0.6 copy-done.4
  12.8 0.0 copy-done.7
  12.8 3.7 %shard_map.157 = (f32[9,64,128]{2,1,0:T(8,128)S(1)}, s32[128]{0:T(128)S(1)}, s32[128]{0:T(128)S(1)}, s32[2]{0:T(128)S(1)}) custom-call(f32[72,1024]{1,0:T(8,128)S(1)} %shard_map.156.packed, s32[2,120]{1,0:T(2,128)S(1)} %copy-done.7, s32[1]{0:T(128)S(6)} %copy.27.npairs, f32[4]{0:T(128)S(1)} %copy-done.4, bf16[256,64]{1,0:T(8,128)(2,1)S(1)} %bitcast.3), custom_call_target="tpu_custom_call" | custom-call | tf_op jit(solution)/shard_map/pallas_call | solution.py:502
  16.5 4.2 %collective-permute-done.1.above = f32[72,1024]{1,0:T(8,128)S(1)} collective-permute-done((f32[72,1024]{1,0:T(8,128)S(1)}, f32[72,1024]{1,0:T(8,128)S(1)}, u32[]{:S(2)}, u32[]{:S(2)}) %collective-permute-start.1) | collective-permute-done | bytes 294944 | tf_op jit(solution)/shard_map/ppermute | solution.py:481
  20.8 14.2 %shard_map.158 = (f32[24,128]{1,0:T(8,128)S(1)}, f32[24,128]{1,0:T(8,128)S(1)}, f32[24,128]{1,0:T(8,128)S(1)}, bf16[9,64,512]{2,1,0:T(8,128)(2,1)S(1)}) custom-call(f32[72,1024]{1,0:T(8,128)S(1)} %shard_map.156.packed, f32[72,1024]{1,0:T(8,128)S(1)} %collective-permute-done.below, f32[72,1024]{1,0:T(8,128)S(1)} %collective-permute-done.1.above, ...), custom_call_target="tpu_custom_call" | custom-call | tf_op jit(solution)/shard_map/pallas_call | solution.py:510
  34.9 10.3 %collective-permute-start.2 = (f32[24,128]{1,0:T(8,128)S(1)}, f32[24,128]{1,0:T(8,128)S(1)}, u32[]{:S(2)}, u32[]{:S(2)}) collective-permute-start(f32[24,128]{1,0:T(8,128)S(1)} %get-tuple-element.23), channel_id=1, source_target_pairs={{0,3},{1,0},{2,1},{3,2},{4,7},{5,4},{6,5},{7,6},{8,11},{9,8},{10,9... | collective-permute-start | bytes 36872 | tf_op jit(solution)/shard_map/ppermute | solution.py:548
  45.3 2.8 %shard_map.159.force = f32[24,128]{1,0:T(8,128)S(1)} custom-call(f32[72,1024]{1,0:T(8,128)S(1)} %shard_map.156.packed, f32[24,128]{1,0:T(8,128)S(1)} %get-tuple-element.20.row_force, bf16[9,64,512]{2,1,0:T(8,128)(2,1)S(1)} %get-tuple-element.21.down, s32[128]{0:T(128)S(1)} %get-tuple-element.22.own_list, s32[2]{0:T(128)S(1)} %get-tuple-element.19.tallies, ...), custom_call_target="tpu_custom_call" | custom-call | tf_op jit(solution)/shard_map/pallas_call | solution.py:550
  48.1 6.5 %collective-permute-done.3.from_below = f32[24,128]{1,0:T(8,128)S(1)} collective-permute-done((f32[24,128]{1,0:T(8,128)S(1)}, f32[24,128]{1,0:T(8,128)S(1)}, u32[]{:S(2)}, u32[]{:S(2)}) %collective-permute-start.3) | collective-permute-done | bytes 12320 | tf_op jit(solution)/shard_map/ppermute | solution.py:549
  54.6 0.3 shard_map.160
  54.9 6.2 %collective-permute-start.6 = (f32[1,6,128]{2,1,0:T(8,128)S(1)}, f32[1,6,128]{2,1,0:T(8,128)S(1)}, u32[]{:S(2)}, u32[]{:S(2)}) collective-permute-start(f32[1,6,128]{2,1,0:T(8,128)S(1)} %get-tuple-element.28), channel_id=1, source_target_pairs={{0,1},{1,2},{2,3},{3,0},{4,5},{5,6},{6,7},{7,4},{8,9},{9,10},{10,1... | collective-permute-start | bytes 9224 | tf_op jit(solution)/shard_map/ppermute | solution.py:586
  61.1 0.9 %collective-permute-start.7 = (f32[1,6,128]{2,1,0:T(8,128)S(1)}, f32[1,6,128]{2,1,0:T(8,128)S(1)}, u32[]{:S(2)}, u32[]{:S(2)}) collective-permute-start(f32[1,6,128]{2,1,0:T(8,128)S(1)} %get-tuple-element.29), channel_id=1, source_target_pairs={{0,3},{1,0},{2,1},{3,2},{4,7},{5,4},{6,5},{7,6},{8,11},{9,8},{10,9... | collective-permute-start | bytes 9224 | tf_op jit(solution)/shard_map/ppermute | solution.py:586
  62.0 0.6 copy.23
  62.6 0.6 copy.24
  63.2 0.6 copy.25
  63.8 0.9 %collective-permute-done.7 = f32[1,6,128]{2,1,0:T(8,128)S(1)} collective-permute-done((f32[1,6,128]{2,1,0:T(8,128)S(1)}, f32[1,6,128]{2,1,0:T(8,128)S(1)}, u32[]{:S(2)}, u32[]{:S(2)}) %collective-permute-start.7) | collective-permute-done | bytes 3104 | tf_op jit(solution)/shard_map/ppermute | solution.py:586
  64.7 0.6 copy.26
  (27 shorter events, 0.1 us)
Async XLA Ops:
  0.6 0.7 %copy-start.6 = (s32[8]{0:T(128)S(1)}, s32[8]{0:T(128)}, u32[]{:S(2)}) copy-start(s32[8]{0:T(128)} %counts.3) | copy-start | bytes 100
  1.4 1.0 %copy-start.1 = (f32[64,1024]{1,0:T(8,128)S(1)}, f32[64,1024]{1,0:T(8,128)}, u32[]{:S(2)}) copy-start(f32[64,1024]{1,0:T(8,128)} %features.1) | copy-start | bytes 786436
  2.3 9.8 %copy-start = (bf16[4,64,64]{2,1,0:T(8,128)(2,1)S(1)}, bf16[4,64,64]{2,1,0:T(8,128)(2,1)}, u32[]{:S(2)}) copy-start(bf16[4,64,64]{2,1,0:T(8,128)(2,1)} %param.18) | copy-start | bytes 98308
  2.9 13.6 %collective-permute-start = (f32[72,1024]{1,0:T(8,128)S(1)}, f32[72,1024]{1,0:T(8,128)S(1)}, u32[]{:S(2)}, u32[]{:S(2)}) collective-permute-start(f32[72,1024]{1,0:T(8,128)S(1)} %shard_map.156.packed), channel_id=1, source_target_pairs={{0,1},{1,2},{2,3},{3,0},{4,5},{5,6},{6,7},{7,4},{8,9},{9,10},{10,1... | collective-permute-start | bytes 884744 | tf_op jit(solution)/shard_map/ppermute | solution.py:480
  6.0 14.8 %collective-permute-start.1 = (f32[72,1024]{1,0:T(8,128)S(1)}, f32[72,1024]{1,0:T(8,128)S(1)}, u32[]{:S(2)}, u32[]{:S(2)}) collective-permute-start(f32[72,1024]{1,0:T(8,128)S(1)} %shard_map.156.packed), channel_id=1, source_target_pairs={{0,3},{1,0},{2,1},{3,2},{4,7},{5,4},{6,5},{7,6},{8,11},{9,8},{10,9... | collective-permute-start | bytes 884744 | tf_op jit(solution)/shard_map/ppermute | solution.py:481
  8.1 40.0 %collective-permute-start.4 = (f32[1,3,1024]{2,1,0:T(4,128)S(1)}, f32[1,3,1024]{2,1,0:T(4,128)S(1)}, u32[]{:S(2)}, u32[]{:S(2)}) collective-permute-start(f32[1,3,1024]{2,1,0:T(4,128)S(1)} %copy.17.positions), channel_id=1, source_target_pairs={{0,4},{4,8},{8,12},{12,16},{16,20},{20,24},{24,28},{28,0},{1,5},{5... | collective-permute-start | bytes 36872 | tf_op jit(solution)/shard_map/ppermute | solution.py:482
  8.1 40.0 %collective-permute-start.5 = (f32[1,3,1024]{2,1,0:T(4,128)S(1)}, f32[1,3,1024]{2,1,0:T(4,128)S(1)}, u32[]{:S(2)}, u32[]{:S(2)}) collective-permute-start(f32[1,3,1024]{2,1,0:T(4,128)S(1)} %copy.17.positions), channel_id=1, source_target_pairs={{0,28},{4,0},{8,4},{12,8},{16,12},{20,16},{24,20},{28,24},{1,29},{... | collective-permute-start | bytes 36872 | tf_op jit(solution)/shard_map/ppermute | solution.py:483
  11.4 0.7 %copy-start.10 = (bf16[64]{0:T(256)(128)(2,1)S(1)}, bf16[64]{0:T(256)(128)(2,1)}, u32[]{:S(2)}) copy-start(bf16[64]{0:T(256)(128)(2,1)} %param.21) | copy-start | bytes 388
  12.1 0.7 %copy-start.4 = (f32[4]{0:T(128)S(1)}, f32[4]{0:T(128)}, u32[]{:S(2)}) copy-start(f32[4]{0:T(128)} %radial_width.5) | copy-start | bytes 52
  12.1 0.7 %copy-start.7 = (s32[2,120]{1,0:T(2,128)S(1)}, s32[2,120]{1,0:T(2,128)}, u32[]{:S(2)}) copy-start(s32[2,120]{1,0:T(2,128)} %pairs.1) | copy-start | bytes 2884
  12.8 7.9 %copy-start.2 = (bf16[64,64]{1,0:T(8,128)(2,1)S(1)}, bf16[64,64]{1,0:T(8,128)(2,1)}, u32[]{:S(2)}) copy-start(bf16[64,64]{1,0:T(8,128)(2,1)} %update_weight.1) | copy-start | bytes 24580
  12.8 7.9 %copy-start.3 = (bf16[64,64]{1,0:T(8,128)(2,1)S(1)}, bf16[64,64]{1,0:T(8,128)(2,1)}, u32[]{:S(2)}) copy-start(bf16[64,64]{1,0:T(8,128)(2,1)} %mix_weight.1) | copy-start | bytes 24580
  20.8 24.5 %copy-start.9 = (f32[1,3,1024]{2,0,1:T(1,128)S(1)}, f32[1,3,1024]{2,0,1:T(1,128)}, u32[]{:S(2)}) copy-start(f32[1,3,1024]{2,0,1:T(1,128)} %param.14) | copy-start | bytes 36868
  34.9 13.2 %collective-permute-start.2 = (f32[24,128]{1,0:T(8,128)S(1)}, f32[24,128]{1,0:T(8,128)S(1)}, u32[]{:S(2)}, u32[]{:S(2)}) collective-permute-start(f32[24,128]{1,0:T(8,128)S(1)} %get-tuple-element.23), channel_id=1, source_target_pairs={{0,3},{1,0},{2,1},{3,2},{4,7},{5,4},{6,5},{7,6},{8,11},{9,8},{10,9... | collective-permute-start | bytes 36872 | tf_op jit(solution)/shard_map/ppermute | solution.py:548
  45.2 9.4 %collective-permute-start.3 = (f32[24,128]{1,0:T(8,128)S(1)}, f32[24,128]{1,0:T(8,128)S(1)}, u32[]{:S(2)}, u32[]{:S(2)}) collective-permute-start(f32[24,128]{1,0:T(8,128)S(1)} %get-tuple-element.24), channel_id=1, source_target_pairs={{0,1},{1,2},{2,3},{3,0},{4,5},{5,6},{6,7},{7,4},{8,9},{9,10},{10,1... | collective-permute-start | bytes 36872 | tf_op jit(solution)/shard_map/ppermute | solution.py:549
  45.2 9.4 %copy-start.5 = (f32[1024]{0:T(1024)S(1)}, f32[1024]{0:T(1024)}, u32[]{:S(2)}) copy-start(f32[1024]{0:T(1024)} %param.16) | copy-start | bytes 12292
  48.1 6.5 %copy-start.8 = (s32[2,64]{1,0:T(2,128)S(1)}, s32[2,64]{1,0:T(2,128)}, u32[]{:S(2)}) copy-start(s32[2,64]{1,0:T(2,128)} %leaving.1) | copy-start | bytes 1540
  54.9 8.9 %collective-permute-start.6 = (f32[1,6,128]{2,1,0:T(8,128)S(1)}, f32[1,6,128]{2,1,0:T(8,128)S(1)}, u32[]{:S(2)}, u32[]{:S(2)}) collective-permute-start(f32[1,6,128]{2,1,0:T(8,128)S(1)} %get-tuple-element.28), channel_id=1, source_target_pairs={{0,1},{1,2},{2,3},{3,0},{4,5},{5,6},{6,7},{7,4},{8,9},{9,10},{10,1... | collective-permute-start | bytes 9224 | tf_op jit(solution)/shard_map/ppermute | solution.py:586
  61.1 3.6 %collective-permute-start.7 = (f32[1,6,128]{2,1,0:T(8,128)S(1)}, f32[1,6,128]{2,1,0:T(8,128)S(1)}, u32[]{:S(2)}, u32[]{:S(2)}) collective-permute-start(f32[1,6,128]{2,1,0:T(8,128)S(1)} %get-tuple-element.29), channel_id=1, source_target_pairs={{0,3},{1,0},{2,1},{3,2},{4,7},{5,4},{6,5},{7,6},{8,11},{9,8},{10,9... | collective-permute-start | bytes 9224 | tf_op jit(solution)/shard_map/ppermute | solution.py:586

commit v2 on v1

--- a/solution.py
+++ b/solution.py
@@ -22,6 +22,7 @@
 LOG2E = 1.4426950408889634
 FAR = 1.0e9
 CHUNK = 16
+GROUP = 4
 
 f32 = jnp.float32
 bf16 = jnp.bfloat16
@@ -46,11 +47,10 @@
 def pack_kernel(features, positions, counts, packed):
     lane = lax.broadcasted_iota(jnp.int32, (1, BLK), 1)
     for b in range(CELLS):
-        cols = slice(b * BLK, (b + 1) * BLK)
         keep = (lane < counts[b]).astype(f32)
-        packed[0:F, cols] = features[:, cols] * keep
-        packed[F : F + 3, cols] = positions[0, :, cols]
-        packed[F + 3 : PACK, cols] = jnp.zeros((PACK - F - 3, BLK), f32)
+        packed[b, 0:F, :] = features[:, b * BLK : (b + 1) * BLK] * keep
+        place = [positions[c * CELLS + b : c * CELLS + b + 1, :] for c in range(3)]
+        packed[b, F:PACK, :] = jnp.concatenate(place + [jnp.zeros((5, BLK), f32)], axis=0)
 
 
 def split_lists(pairs, npairs, own_list, ghost_list, tallies):
@@ -67,15 +67,19 @@
         return own + taken, ghost + 1 - taken
 
     own, ghost = lax.fori_loop(0, npairs[0], step, (jnp.int32(0), jnp.int32(0)))
-    for extra in range(4):
+    for extra in range(2 * GROUP):
         own_list[own + extra] = CELLS * 16
         ghost_list[ghost + extra] = CELLS * 16
     tallies[0] = own
     tallies[1] = ghost
 
 
+def feature_rows(packed):
+    return jnp.concatenate([packed[b, 0:F, :] for b in range(CELLS)], axis=1)
+
+
 def fill_tables(packed, weight, tables, base):
-    high, low = halves(packed[0:F, :])
+    high, low = halves(feature_rows(packed))
     stacked = jnp.concatenate([high, low], axis=0)
     result = dot(weight, stacked)
     for b in range(CELLS):
@@ -86,33 +90,31 @@
 
 
 def fill_transposed(packed, turned, base):
-    x = packed[0:F, :]
-    high = x.astype(bf16).astype(f32)
-    stacked = jnp.concatenate([high, x - high], axis=0)
     for b in range(CELLS):
-        turned[base + b] = block_lanes(stacked, b).T.astype(bf16)
-
-
-def fill_rows(packed, rows):
-    for b in range(CELLS):
-        rows[b, 0:3, :] = packed[F : F + 3, b * BLK : (b + 1) * BLK]
-    rows[CELLS] = jnp.zeros((8, BLK), f32)
+        x = packed[b, 0:F, :]
+        high = x.astype(bf16).astype(f32)
+        stacked = jnp.concatenate([high, x - high], axis=0)
+        turned[base + b] = stacked.T.astype(bf16)
 
 
 def fill_columns(sources, columns):
     pieces = []
     for packed, shift in sources:
-        third = lax.broadcasted_iota(jnp.int32, (3, BLK), 0) == 2
         for b in range(CELLS):
-            piece = packed[F : F + 3, b * BLK : (b + 1) * BLK]
+            piece = packed[b, F:PACK, :]
             if shift:
+                third = lax.broadcasted_iota(jnp.int32, (PACK - F, BLK), 0) == 2
                 piece = piece + jnp.where(third, shift, 0.0)
             pieces.append(piece)
-    used = 3 * len(pieces)
-    pieces.append(jnp.zeros((BLK - used, BLK), f32))
+    blocks = len(pieces)
+    width = PACK - F
+    if width * blocks < BLK:
+        pieces.append(jnp.zeros((BLK - width * blocks, BLK), f32))
     turned = jnp.concatenate(pieces, axis=0).T
-    for n in range(used):
-        columns[n // 3, n % 3] = jnp.broadcast_to(turned[:, n : n + 1], (BLK, BLK))
+    for b in range(blocks):
+        for c in range(3):
+            n = width * b + c
+            columns[b, c] = jnp.broadcast_to(turned[:, n : n + 1], (BLK, BLK))
 
 
 def fill_penalty(penalty):
@@ -132,8 +134,8 @@
     return lax.shift_right_logical(code, 4), lax.bitwise_and(code, 15)
 
 
-def separation(rows, columns, penalty, i, j, place):
-    parts = [rows[i, c : c + 1, :] - columns[j, c, place, :] for c in range(3)]
+def separation(packed, columns, penalty, i, j, place):
+    parts = [packed[i & 7, F + c : F + c + 1, :] - columns[j, c, place, :] for c in range(3)]
     squared = parts[0] * parts[0] + parts[1] * parts[1] + parts[2] * parts[2]
     if penalty is not None:
         squared = squared + penalty[(i == j).astype(jnp.int32), place, :]
@@ -141,12 +143,12 @@
     return parts, squared, remain
 
 
-def message_pass(pair_list, count, rows, columns, penalty, rates, tables, amps, message):
+def message_pass(pair_list, count, packed, columns, penalty, rates, tables, amps, message):
     def amplitudes(p, amp):
         i, j = decode(pair_list, p)
         for r in range(BLK // CHUNK):
             place = slice(r * CHUNK, (r + 1) * CHUNK)
-            _, squared, remain = separation(rows, columns, penalty, i, j, place)
+            _, squared, remain = separation(packed, columns, penalty, i, j, place)
             cutoff = remain * remain
             for k in range(RAD):
                 value = jnp.exp2(squared * rates[k]) * cutoff
@@ -156,24 +158,23 @@
         i, j = decode(pair_list, p)
         message[i] += dot(tables[j], amp[...])
 
-    amp_a, amp_b = amps
-
     @pl.when(count > 0)
     def _():
-        amplitudes(0, amp_a)
+        for u, amp in enumerate(amps):
+            amplitudes(u, amp)
 
     def step(t, carry):
-        multiply(2 * t, amp_a)
-        amplitudes(2 * t + 1, amp_b)
-        multiply(2 * t + 1, amp_b)
-        amplitudes(2 * t + 2, amp_a)
+        for u, amp in enumerate(amps):
+            multiply(GROUP * t + u, amp)
+        for u, amp in enumerate(amps):
+            amplitudes(GROUP * t + GROUP + u, amp)
         return carry
 
-    lax.fori_loop(0, (count + 1) // 2, step, 0)
+    lax.fori_loop(0, (count + GROUP - 1) // GROUP, step, 0)
 
 
 def force_pass(
-    pair_list, count, rows, columns, penalty, rates, doubled, turned, down, grads, row_sum, column_sum
+    pair_list, count, packed, columns, penalty, rates, doubled, turned, down, grads, row_sum, column_sum
 ):
     lane = lax.broadcasted_iota(jnp.int32, (CHUNK, BLK), 1)
 
@@ -188,7 +189,7 @@
         sums = [jnp.zeros((CHUNK, BLK), f32) for _ in range(3)]
         for r in range(BLK // CHUNK):
             place = slice(r * CHUNK, (r + 1) * CHUNK)
-            parts, squared, remain = separation(rows, columns, penalty, i, j, place)
+            parts, squared, remain = separation(packed, columns, penalty, i, j, place)
             plain = None
             scaled = None
             for k in range(RAD):
@@ -209,20 +210,27 @@
         for c in range(3):
             row_sum[i, c] += sums[c]
 
-    grad_a, grad_b = grads
+    pairs_each = GROUP // 2
+    first, second = grads[:pairs_each], grads[pairs_each:]
 
     @pl.when(count > 0)
     def _():
-        products(0, grad_a)
+        for u, grad in enumerate(first):
+            products(u, grad)
 
     def step(t, carry):
-        products(2 * t + 1, grad_b)
-        apply(2 * t, grad_a)
-        products(2 * t + 2, grad_a)
-        apply(2 * t + 1, grad_b)
+        base = GROUP * t
+        for u, grad in enumerate(second):
+            products(base + pairs_each + u, grad)
+        for u, grad in enumerate(first):
+            apply(base + u, grad)
+        for u, grad in enumerate(first):
+            products(base + GROUP + u, grad)
+        for u, grad in enumerate(second):
+            apply(base + pairs_each + u, grad)
         return carry
 
-    lax.fori_loop(0, (count + 1) // 2, step, 0)
+    lax.fori_loop(0, (count + GROUP - 1) // GROUP, step, 0)
 
 
 def own_message_kernel(
@@ -236,22 +244,23 @@
     ghost_list,
     tallies,
     tables,
-    rows,
     columns,
     penalty,
-    amp_a,
-    amp_b,
+    *amps,
 ):
     split_lists(pairs, npairs, own_list, ghost_list, tallies)
     fill_tables(packed, jnp.concatenate([weight[...], weight[...]], axis=1), tables, 0)
-    fill_rows(packed, rows)
     fill_columns([(packed, 0.0)], columns)
     fill_penalty(penalty)
     message[...] = jnp.zeros(message.shape, f32)
     rates = [-LOG2E * inverse for inverse in inverse_widths(radial_width)]
-    message_pass(
-        own_list, tallies[0], rows, columns, penalty, rates, tables, (amp_a, amp_b), message
-    )
+    message_pass(own_list, tallies[0], packed, columns, penalty, rates, tables, amps, message)
+
+
+def as_column(row):
+    size = (row.shape[1], row.shape[1])
+    diagonal = lax.broadcasted_iota(jnp.int32, size, 0) == lax.broadcasted_iota(jnp.int32, size, 1)
+    return jnp.sum(jnp.where(diagonal, row, 0.0), axis=1, keepdims=True)
 
 
 def node_backward(
@@ -261,13 +270,13 @@
     scaled = (whole * MESSAGE_SCALE).astype(bf16)
     first_pre = dot(update_weight[...], scaled)
     first_gate = jax.nn.sigmoid(first_pre)
-    updated = (packed[0:F, :] + first_pre * first_gate).astype(bf16)
+    updated = (feature_rows(packed) + first_pre * first_gate).astype(bf16)
     second_pre = dot(mix_weight[...], updated)
     second_gate = jax.nn.sigmoid(second_pre)
     lane = lax.broadcasted_iota(jnp.int32, (1, BLK), 1)
     occupied = jnp.concatenate([(lane < counts[b]).astype(f32) for b in range(CELLS)], axis=1)
     second_grad = (
-        out_weight[...].astype(f32)
+        as_column(out_weight[...].astype(f32))
         * second_gate
         * (1.0 + second_pre * (1.0 - second_gate))
         * occupied
@@ -291,8 +300,9 @@
     for b in range(CELLS):
         for c in range(3):
             total = jnp.sum(row_sum[b, c], axis=0, keepdims=True)
-            n = 3 * b + c
-            out[n : n + 1, :] = total if start is None else total + start[n : n + 1, :]
+            n = CELLS * c + b
+            m = 3 * b + c
+            out[n : n + 1, :] = total if start is None else total - start[m : m + 1, :]
 
 
 def ghost_kernel(
@@ -315,27 +325,21 @@
     message,
     tables,
     turned,
-    rows,
     columns,
-    amp_a,
-    amp_b,
-    grad_a,
-    grad_b,
     row_sum,
     column_sum,
+    *buffers,
 ):
+    amps, grads = buffers[:GROUP], buffers[GROUP:]
     doubled_weight = jnp.concatenate([weight[...], weight[...]], axis=1)
     fill_tables(below, doubled_weight, tables, 0)
     fill_tables(above, doubled_weight, tables, CELLS)
-    fill_rows(packed, rows)
     fill_columns([(below, -CELL_SIDE), (above, CELL_SIDE)], columns)
     message[...] = own_message[...]
     inverse = inverse_widths(radial_width)
     rates = [-LOG2E * value for value in inverse]
     count = tallies[1]
-    message_pass(
-        ghost_list, count, rows, columns, None, rates, tables, (amp_a, amp_b), message
-    )
+    message_pass(ghost_list, count, packed, columns, None, rates, tables, amps, message)
     fill_transposed(below, turned, 0)
     fill_transposed(above, turned, CELLS)
     node_backward(message, packed, counts, weight, update_weight, mix_weight, out_weight, down)
@@ -344,14 +348,14 @@
     force_pass(
         ghost_list,
         count,
-        rows,
+        packed,
         columns,
         None,
         rates,
         doubled_rates(inverse),
         turned,
         down,
-        (grad_a, grad_b),
+        grads,
         row_sum,
         column_sum,
     )
@@ -370,15 +374,12 @@
     radial_width,
     force,
     turned,
-    rows,
     columns,
     penalty,
-    grad_a,
-    grad_b,
     row_sum,
     column_sum,
+    *grads,
 ):
-    fill_rows(packed, rows)
     fill_columns([(packed, 0.0)], columns)
     fill_penalty(penalty)
     fill_transposed(packed, turned, 0)
@@ -389,18 +390,25 @@
     force_pass(
         own_list,
         tallies[0],
-        rows,
+        packed,
         columns,
         penalty,
         rates,
         doubled_rates(inverse),
         turned,
         down,
-        (grad_a, grad_b),
+        grads,
         row_sum,
         column_sum,
     )
-    collect_rows(row_sum, force, row_force[...] - column_sum[...].T[0:24])
+    collect_rows(row_sum, force, column_sum[...].T)
+    force[...] += row_force[...]
+
+
+def by_component(flat):
+    return jnp.concatenate(
+        [flat[3 * b + c : 3 * b + c + 1, :] for c in range(3) for b in range(CELLS)], axis=0
+    )
 
 
 def finish_kernel(
@@ -418,32 +426,37 @@
     momenta_new,
     upward,
     downward,
+    packet,
 ):
-    pair_force = force[...] - from_above[...] - from_below[...]
-    physical = jnp.concatenate([pair_force[3 * b : 3 * b + 3, :] for b in range(CELLS)], axis=1)
-    mass = masses[...]
-    current = positions[0]
-    spring = -SPRING_RATE * mass * (2.0 * current - before[0] - after[0])
+    physical = force[...] - by_component(from_above[...] + from_below[...])
+    mass = jnp.concatenate([masses[...]] * 3, axis=0)
+    current = positions[...]
+    spring = -SPRING_RATE * mass * (2.0 * current - before[...] - after[...])
     total = physical + spring
-    moved = momenta[0] + total
+    moved = momenta[...] + total
     placed = current + moved / mass
-    forces[0] = total
-    momenta_new[0] = moved
-    positions_new[0] = placed
+    forces[...] = total
+    momenta_new[...] = moved
+    positions_new[...] = placed
+    packet[0:24, :] = placed
+    packet[24:48, :] = moved
+    packet[48:64, :] = jnp.zeros((16, BLK), f32)
     movers = jnp.concatenate([leaving[1:2, :], leaving[0:1, :]], axis=1)
     slot = lax.broadcasted_iota(jnp.int32, (ATOMS_DEV, 2 * MIG), 0)
     chosen = (slot == movers).astype(f32).astype(bf16)
-    packet = jnp.concatenate([placed, moved, jnp.zeros((2, ATOMS_DEV), f32)], axis=0)
-    high = packet.astype(bf16)
-    middle, third = halves(packet - high.astype(f32))
-    picked = dot(high, chosen) + (dot(middle, chosen) + dot(third, chosen))
+    values = jnp.concatenate([packet[pl.ds(b, 8, stride=CELLS), :] for b in range(CELLS)], axis=1)
+    high = values.astype(bf16)
+    middle, low = halves(values - high.astype(f32))
+    picked = dot(high, chosen) + (dot(middle, chosen) + dot(low, chosen))
     lane = lax.broadcasted_iota(jnp.int32, (8, 2 * MIG), 1)
     row = lax.broadcasted_iota(jnp.int32, (8, 2 * MIG), 0)
     shift = jnp.where(lane < MIG, -CELL_SIDE, CELL_SIDE)
-    present = movers >= 0
-    shifted = jnp.where(present, picked + jnp.where(row == 2, shift, 0.0), 0.0)
-    upward[0] = jnp.where(lane < MIG, shifted, 0.0)[0:6]
-    downward[0] = jnp.where(lane < MIG, 0.0, shifted)[0:6]
+    shifted = jnp.where(movers >= 0, picked + jnp.where(row == 2, shift, 0.0), 0.0)
+    up = jnp.where(lane < MIG, shifted, 0.0)
+    down = jnp.where(lane < MIG, 0.0, shifted)
+    for q in range(6):
+        upward[q] = up[q : q + 1, :]
+        downward[q] = down[q : q + 1, :]
 
 
 def shape(dims, kind=f32):
@@ -470,21 +483,21 @@
         return [(i, (i + step) % count) for i in range(count)]
 
     weight = msg_weight.reshape(RAD * F, F)
+    current = positions.reshape(3 * CELLS, BLK)
     packed = pl.pallas_call(
         pack_kernel,
-        out_shape=shape((PACK, ATOMS_DEV)),
+        out_shape=shape((CELLS, PACK, BLK)),
         in_specs=[VMEM, VMEM, SMEM],
         out_specs=VMEM,
         compiler_params=PARAMS,
-    )(features, positions, counts)
+    )(features, current, counts)
     below = lax.ppermute(packed, "dom", ring("dom", 1))
     above = lax.ppermute(packed, "dom", ring("dom", -1))
-    before = lax.ppermute(positions, "bead", ring("bead", 1))
-    after = lax.ppermute(positions, "bead", ring("bead", -1))
+    before = lax.ppermute(current, "bead", ring("bead", 1))
+    after = lax.ppermute(current, "bead", ring("bead", -1))
 
     amp = pltpu.VMEM((RAD * BLK, BLK), bf16)
     grad = pltpu.VMEM((BLK, RAD * BLK), f32)
-    rows = pltpu.VMEM((CELLS + 1, 8, BLK), f32)
     row_sum = pltpu.VMEM((CELLS + 1, 3, CHUNK, BLK), f32)
     column_sum = pltpu.VMEM((BLK, BLK), f32)
     penalty = pltpu.VMEM((2, BLK, BLK), f32)
@@ -504,7 +517,7 @@
         out_shape=(shape((CELLS + 1, F, BLK)), listed, listed, shape((2,), jnp.int32)),
         in_specs=[VMEM, SMEM, SMEM, SMEM, VMEM],
         out_specs=(VMEM, SMEM, SMEM, SMEM),
-        scratch_shapes=[tables(CELLS), rows, columns(CELLS), penalty, amp, amp],
+        scratch_shapes=[tables(CELLS), columns(CELLS), penalty] + [amp] * GROUP,
         compiler_params=PARAMS,
     )(packed, pairs, npairs, radial_width, weight)
     row_force, ghost_below, ghost_above, down = pl.pallas_call(
@@ -521,15 +534,12 @@
             pltpu.VMEM((CELLS + 1, F, BLK), f32),
             tables(2 * CELLS),
             turned(2 * CELLS),
-            rows,
             columns(2 * CELLS),
-            amp,
-            amp,
-            grad,
-            grad,
             row_sum,
             column_sum,
-        ],
+        ]
+        + [amp] * GROUP
+        + [grad] * GROUP,
         compiler_params=PARAMS,
     )(
         packed,
@@ -543,7 +553,7 @@
         weight,
         update_weight,
         mix_weight,
-        out_weight.reshape(F, 1),
+        out_weight.reshape(1, F),
     )
     from_above = lax.ppermute(ghost_below, "dom", ring("dom", -1))
     from_below = lax.ppermute(ghost_above, "dom", ring("dom", 1))
@@ -554,39 +564,39 @@
         out_specs=VMEM,
         scratch_shapes=[
             turned(CELLS),
-            rows,
             columns(CELLS),
             penalty,
-            grad,
-            grad,
             row_sum,
             column_sum,
-        ],
+        ]
+        + [grad] * GROUP,
         compiler_params=PARAMS,
     )(packed, row_force, down, own_list, tallies, radial_width)
-    whole = shape((1, 3, ATOMS_DEV))
-    packet = shape((1, 6, 2 * MIG))
+    whole = shape((3 * CELLS, BLK))
+    packet = shape((6, 1, 2 * MIG))
     forces, positions_new, momenta_new, upward, downward = pl.pallas_call(
         finish_kernel,
         out_shape=(whole, whole, whole, packet, packet),
         in_specs=[VMEM] * 9,
         out_specs=(VMEM,) * 5,
+        scratch_shapes=[pltpu.VMEM((64, BLK), f32)],
         compiler_params=PARAMS,
     )(
         force,
         from_above,
         from_below,
-        positions,
-        momenta,
+        current,
+        momenta.reshape(3 * CELLS, BLK),
         before,
         after,
-        masses.reshape(1, ATOMS_DEV),
+        masses.reshape(CELLS, BLK),
         leaving,
     )
     arrivals = lax.ppermute(upward, "dom", ring("dom", 1)) + lax.ppermute(
         downward, "dom", ring("dom", -1)
     )
-    return forces, positions_new, momenta_new, arrivals
+    result = tuple(x.reshape(1, 3, ATOMS_DEV) for x in (forces, positions_new, momenta_new))
+    return result + (arrivals.reshape(1, 6, 2 * MIG),)
 
 
 def solution(mesh):

time: 65.5 us -> 56.2 us (0.86)
  starting transfers between devices: 25.2 us -> 20.3 us
  Pallas kernels: 21.5 us -> 17.4 us
  local copies, waits for them, and re-layouts: 5.56 us -> 4.32 us
    pallas_call x1, Pallas kernels: 14.2 us -> 10.5 us  [body(): pl.pallas_call(ghost_kernel, out_shape=(shape((24, BLK)), shape((24, BLK)...]
    ppermute x1, starting transfers between devices: 10.3 us -> 7.18 us  [body(): from_above = lax.ppermute(ghost_below, 'dom', ring('dom', -1))]
    ppermute x1, waiting for transfers between devices: 6.48 us -> 3.62 us  [body(): from_below = lax.ppermute(ghost_above, 'dom', ring('dom', 1))]
    ppermute x1, starting transfers between devices: 6.16 us -> 4.44 us  [body(): lax.ppermute(upward, 'dom', ring('dom', 1))]
    ppermute x1, waiting for transfers between devices: 0.01 us -> 1.57 us  [body(): lax.ppermute(upward, 'dom', ring('dom', 1))]
    unnamed x28 -> x24, local copies, waits for them, and re-layouts: 5.45 us -> 4.32 us
    ppermute x1, waiting for transfers between devices: 0.01 us -> 0.68 us  [body(): below = lax.ppermute(packed, 'dom', ring('dom', 1))]
  transfers between devices with their start and end apart: 8 -> 8, of which waited for: 3 -> 5; matrix products, arithmetic and copies ran while one was open for 3% -> 0% of each run, Pallas kernels for 32% -> 29%
where the time goes in v2:
time: 56.2 us; the launch traced here: 55.9 us
  starting transfers between devices  20.3 us (36%)
  Pallas kernels  17.4 us (31%)
  waiting for transfers between devices  11.9 us (21%)
  local copies, waits for them, and re-layouts  4.32 us (8%)
  between operations  1.38 us (2%)
  other arithmetic  0.58 us (1%)
    pallas_call x1, Pallas kernels, body(): pl.pallas_call(ghost_kernel, out_shape=(shape((24, BLK)), shape((24, BLK)...  10.5 us
    ppermute x1, starting transfers between devices, body(): from_above = lax.ppermute(ghost_below, 'dom', ring('dom', -1))  7.18 us
    ppermute x1, waiting for transfers between devices, body(): above = lax.ppermute(packed, 'dom', ring('dom', -1))  4.88 us
    ppermute x1, starting transfers between devices, body(): lax.ppermute(upward, 'dom', ring('dom', 1))  4.44 us
    unnamed x24, local copies, waits for them, and re-layouts  4.32 us
    ppermute x1, waiting for transfers between devices, body(): from_below = lax.ppermute(ghost_above, 'dom', ring('dom', 1))  3.62 us
    pallas_call x1, Pallas kernels, body(): pl.pallas_call(own_message_kernel, out_shape=(shape((CELLS + 1, F, BLK)),...  3.13 us
    ppermute x1, starting transfers between devices, body(): below = lax.ppermute(packed, 'dom', ring('dom', 1))  3.08 us
  transfers between devices with their start and end apart: 8, of which 5 were waited for; matrix products, arithmetic and copies ran while one was open for 0% of the time, Pallas kernels for 29%

profile of v2, /device:TPU:0, one launch (start us, length us, event | category | flops | bytes accessed | tf_op | source)
XLA Modules:
  0.0 55.9 jit_solution(10921679315245311075)
XLA Ops:
  0.6 0.6 %copy-done.8 = s32[8]{0:T(128)S(1)} copy-done((s32[8]{0:T(128)S(1)}, s32[8]{0:T(128)}, u32[]{:S(2)}) %copy-start.8) | copy-done | bytes 56
  1.3 0.9 %copy-done.1 = f32[64,1024]{1,0:T(8,128)S(1)} copy-done((f32[64,1024]{1,0:T(8,128)S(1)}, f32[64,1024]{1,0:T(8,128)}, u32[]{:S(2)}) %copy-start.1) | copy-done | bytes 262168
  2.2 0.7 %copy-done.2 = f32[1,3,1024]{2,0,1:T(1,128)S(1)} copy-done((f32[1,3,1024]{2,0,1:T(1,128)S(1)}, f32[1,3,1024]{2,0,1:T(1,128)}, u32[]{:S(2)}) %copy-start.2) | copy-done | bytes 12312
  2.9 0.6 %shard_map.156.packed = f32[8,72,128]{2,1,0:T(8,128)S(1)} custom-call(f32[64,1024]{1,0:T(8,128)S(1)} %copy-done.1, f32[24,128]{1,0:T(8,128)S(1)} %bitcast.12, s32[8]{0:T(128)S(1)} %copy-done.8), custom_call_target="tpu_custom_call" | custom-call | tf_op jit(solution)/shard_map/pallas_call | solution.py:487
  3.5 3.1 %collective-permute-start = (f32[8,72,128]{2,1,0:T(8,128)S(1)}, f32[8,72,128]{2,1,0:T(8,128)S(1)}, u32[]{:S(2)}, u32[]{:S(2)}) collective-permute-start(f32[8,72,128]{2,1,0:T(8,128)S(1)} %shard_map.156.packed), channel_id=1, source_target_pairs={{0,1},{1,2},{2,3},{3,0},{4,5},{5,6},{6,7},{7,4},{8,9},{9,10},{10,1... | collective-permute-start | bytes 884744 | tf_op jit(solution)/shard_map/ppermute | solution.py:494
  6.6 2.1 %collective-permute-start.1 = (f32[8,72,128]{2,1,0:T(8,128)S(1)}, f32[8,72,128]{2,1,0:T(8,128)S(1)}, u32[]{:S(2)}, u32[]{:S(2)}) collective-permute-start(f32[8,72,128]{2,1,0:T(8,128)S(1)} %shard_map.156.packed), channel_id=1, source_target_pairs={{0,3},{1,0},{2,1},{3,2},{4,7},{5,4},{6,5},{7,6},{8,11},{9,8},{10,9... | collective-permute-start | bytes 884744 | tf_op jit(solution)/shard_map/ppermute | solution.py:495
  8.7 2.6 %collective-permute-start.5 = (f32[24,128]{1,0:T(8,128)S(1)}, f32[24,128]{1,0:T(8,128)S(1)}, u32[]{:S(2)}, u32[]{:S(2)}) collective-permute-start(f32[24,128]{1,0:T(8,128)S(1)} %bitcast.14), channel_id=1, source_target_pairs={{0,28},{4,0},{8,4},{12,8},{16,12},{20,16},{24,20},{28,24},{1,29},{... | collective-permute-start | bytes 36872 | tf_op jit(solution)/shard_map/ppermute | solution.py:497
  12.0 0.6 %copy-done.6 = f32[4]{0:T(128)S(1)} copy-done((f32[4]{0:T(128)S(1)}, f32[4]{0:T(128)}, u32[]{:S(2)}) %copy-start.6) | copy-done | bytes 40
  12.6 0.0 copy-done.9
  12.7 3.1 %shard_map.157 = (f32[9,64,128]{2,1,0:T(8,128)S(1)}, s32[128]{0:T(128)S(1)}, s32[128]{0:T(128)S(1)}, s32[2]{0:T(128)S(1)}) custom-call(f32[8,72,128]{2,1,0:T(8,128)S(1)} %shard_map.156.packed, s32[2,120]{1,0:T(2,128)S(1)} %copy-done.9, s32[1]{0:T(128)S(6)} %copy.23.npairs, f32[4]{0:T(128)S(1)} %copy-done.6, bf16[256,64]{1,0:T(8,128)(2,1)S(1)} %bitcast.10), custom_call_target="tpu_custom_call" | custom-call | tf_op jit(solution)/shard_map/pallas_call | solution.py:515
  15.8 0.7 %collective-permute-done.below = f32[8,72,128]{2,1,0:T(8,128)S(1)} collective-permute-done((f32[8,72,128]{2,1,0:T(8,128)S(1)}, f32[8,72,128]{2,1,0:T(8,128)S(1)}, u32[]{:S(2)}, u32[]{:S(2)}) %collective-permute-start) | collective-permute-done | bytes 294944 | tf_op jit(solution)/shard_map/ppermute | solution.py:494
  16.5 4.9 %collective-permute-done.1.above = f32[8,72,128]{2,1,0:T(8,128)S(1)} collective-permute-done((f32[8,72,128]{2,1,0:T(8,128)S(1)}, f32[8,72,128]{2,1,0:T(8,128)S(1)}, u32[]{:S(2)}, u32[]{:S(2)}) %collective-permute-start.1) | collective-permute-done | bytes 294944 | tf_op jit(solution)/shard_map/ppermute | solution.py:495
  21.4 0.6 %copy-done.11 = bf16[64]{0:T(256)(128)(2,1)S(1)} copy-done((bf16[64]{0:T(256)(128)(2,1)S(1)}, bf16[64]{0:T(256)(128)(2,1)}, u32[]{:S(2)}) %copy-start.11) | copy-done | bytes 152
  22.0 10.5 %shard_map.158 = (f32[24,128]{1,0:T(8,128)S(1)}, f32[24,128]{1,0:T(8,128)S(1)}, f32[24,128]{1,0:T(8,128)S(1)}, bf16[9,64,512]{2,1,0:T(8,128)(2,1)S(1)}) custom-call(f32[8,72,128]{2,1,0:T(8,128)S(1)} %shard_map.156.packed, f32[8,72,128]{2,1,0:T(8,128)S(1)} %collective-permute-done.below, f32[8,72,128]{2,1,0:T(8,128)S(1)} %collective-permute-done.1.above, ...), custom_call_target="tpu_custom_call" | custom-call | tf_op jit(solution)/shard_map/pallas_call | solution.py:523
  32.5 7.2 %collective-permute-start.2 = (f32[24,128]{1,0:T(8,128)S(1)}, f32[24,128]{1,0:T(8,128)S(1)}, u32[]{:S(2)}, u32[]{:S(2)}) collective-permute-start(f32[24,128]{1,0:T(8,128)S(1)} %get-tuple-element.23), channel_id=1, source_target_pairs={{0,3},{1,0},{2,1},{3,2},{4,7},{5,4},{6,5},{7,6},{8,11},{9,8},{10,9... | collective-permute-start | bytes 36872 | tf_op jit(solution)/shard_map/ppermute | solution.py:558
  39.7 2.6 %shard_map.159.force = f32[24,128]{1,0:T(8,128)S(1)} custom-call(f32[8,72,128]{2,1,0:T(8,128)S(1)} %shard_map.156.packed, f32[24,128]{1,0:T(8,128)S(1)} %get-tuple-element.20.row_force, bf16[9,64,512]{2,1,0:T(8,128)(2,1)S(1)} %get-tuple-element.21.down, s32[128]{0:T(128)S(1)} %get-tuple-element.22.own_list, s32[2]{0:T(128)S(1)} %get-tuple-element.19.tallies, ...), custom_call_target="tpu_custom_call" | custom-call | tf_op jit(solution)/shard_map/pallas_call | solution.py:560
  42.4 3.6 %collective-permute-done.3.from_below = f32[24,128]{1,0:T(8,128)S(1)} collective-permute-done((f32[24,128]{1,0:T(8,128)S(1)}, f32[24,128]{1,0:T(8,128)S(1)}, u32[]{:S(2)}, u32[]{:S(2)}) %collective-permute-start.3) | collective-permute-done | bytes 12320 | tf_op jit(solution)/shard_map/ppermute | solution.py:559
  46.0 0.7 %copy-done.10 = s32[2,64]{1,0:T(2,128)S(1)} copy-done((s32[2,64]{1,0:T(2,128)S(1)}, s32[2,64]{1,0:T(2,128)}, u32[]{:S(2)}) %copy-start.10) | copy-done | bytes 536
  46.7 0.6 %shard_map.160 = (f32[24,128]{1,0:T(8,128)}, f32[24,128]{1,0:T(8,128)}, f32[24,128]{1,0:T(8,128)}, f32[6,1,128]{2,1,0:T(1,128)S(1)}, f32[6,1,128]{2,1,0:T(1,128)S(1)}) custom-call(f32[24,128]{1,0:T(8,128)S(1)} %shard_map.159.force, f32[24,128]{1,0:T(8,128)S(1)} %collective-permute-done.2.from_above, f32[24,128]{1,0:T(8,128)S(1)} %collective-permute-done.3.from_below, ...), custom_call_target="tpu_custom_call" | custom-call | tf_op jit(solution)/shard_map/pallas_call | solution.py:577
  47.3 4.4 %collective-permute-start.6 = (f32[6,1,128]{2,1,0:T(1,128)S(1)}, f32[6,1,128]{2,1,0:T(1,128)S(1)}, u32[]{:S(2)}, u32[]{:S(2)}) collective-permute-start(f32[6,1,128]{2,1,0:T(1,128)S(1)} %get-tuple-element.28), channel_id=1, source_target_pairs={{0,1},{1,2},{2,3},{3,0},{4,5},{5,6},{6,7},{7,4},{8,9},{9,10},{10,1... | collective-permute-start | bytes 9224 | tf_op jit(solution)/shard_map/ppermute | solution.py:595
  51.8 0.8 %collective-permute-start.7 = (f32[6,1,128]{2,1,0:T(1,128)S(1)}, f32[6,1,128]{2,1,0:T(1,128)S(1)}, u32[]{:S(2)}, u32[]{:S(2)}) collective-permute-start(f32[6,1,128]{2,1,0:T(1,128)S(1)} %get-tuple-element.29), channel_id=1, source_target_pairs={{0,3},{1,0},{2,1},{3,2},{4,7},{5,4},{6,5},{7,6},{8,11},{9,8},{10,9... | collective-permute-start | bytes 9224 | tf_op jit(solution)/shard_map/ppermute | solution.py:595
  52.6 1.6 %collective-permute-done.6 = f32[6,1,128]{2,1,0:T(1,128)S(1)} collective-permute-done((f32[6,1,128]{2,1,0:T(1,128)S(1)}, f32[6,1,128]{2,1,0:T(1,128)S(1)}, u32[]{:S(2)}, u32[]{:S(2)}) %collective-permute-start.6) | collective-permute-done | bytes 3104 | tf_op jit(solution)/shard_map/ppermute | solution.py:595
  54.2 1.2 %collective-permute-done.7 = f32[6,1,128]{2,1,0:T(1,128)S(1)} collective-permute-done((f32[6,1,128]{2,1,0:T(1,128)S(1)}, f32[6,1,128]{2,1,0:T(1,128)S(1)}, u32[]{:S(2)}, u32[]{:S(2)}) %collective-permute-start.7) | collective-permute-done | bytes 3104 | tf_op jit(solution)/shard_map/ppermute | solution.py:595
  55.4 0.6 %add_bitcast_fusion = f32[1,6,128]{2,0,1:T(1,128)} fusion(f32[6,1,128]{2,1,0:T(1,128)S(1)} %collective-permute-done.6, f32[6,1,128]{2,1,0:T(1,128)S(1)} %collective-permute-done.7), kind=kLoop, calls=%fused_computation | loop fusion | flops 768 | bytes 9216 | tf_op jit(solution)/shard_map/reshape | solution.py:599
  (22 shorter events, 0.0 us)
Async XLA Ops:
  0.6 0.7 %copy-start.8 = (s32[8]{0:T(128)S(1)}, s32[8]{0:T(128)}, u32[]{:S(2)}) copy-start(s32[8]{0:T(128)} %counts.3) | copy-start | bytes 100
  1.3 0.9 %copy-start.1 = (f32[64,1024]{1,0:T(8,128)S(1)}, f32[64,1024]{1,0:T(8,128)}, u32[]{:S(2)}) copy-start(f32[64,1024]{1,0:T(8,128)} %features.1) | copy-start | bytes 786436
  2.2 0.7 %copy-start.2 = (f32[1,3,1024]{2,0,1:T(1,128)S(1)}, f32[1,3,1024]{2,0,1:T(1,128)}, u32[]{:S(2)}) copy-start(f32[1,3,1024]{2,0,1:T(1,128)} %param.13) | copy-start | bytes 36868
  2.9 9.1 %copy-start = (bf16[4,64,64]{2,1,0:T(8,128)(2,1)S(1)}, bf16[4,64,64]{2,1,0:T(8,128)(2,1)}, u32[]{:S(2)}) copy-start(bf16[4,64,64]{2,1,0:T(8,128)(2,1)} %param.18) | copy-start | bytes 98308
  3.5 13.0 %collective-permute-start = (f32[8,72,128]{2,1,0:T(8,128)S(1)}, f32[8,72,128]{2,1,0:T(8,128)S(1)}, u32[]{:S(2)}, u32[]{:S(2)}) collective-permute-start(f32[8,72,128]{2,1,0:T(8,128)S(1)} %shard_map.156.packed), channel_id=1, source_target_pairs={{0,1},{1,2},{2,3},{3,0},{4,5},{5,6},{6,7},{7,4},{8,9},{9,10},{10,1... | collective-permute-start | bytes 884744 | tf_op jit(solution)/shard_map/ppermute | solution.py:494
  6.6 14.8 %collective-permute-start.1 = (f32[8,72,128]{2,1,0:T(8,128)S(1)}, f32[8,72,128]{2,1,0:T(8,128)S(1)}, u32[]{:S(2)}, u32[]{:S(2)}) collective-permute-start(f32[8,72,128]{2,1,0:T(8,128)S(1)} %shard_map.156.packed), channel_id=1, source_target_pairs={{0,3},{1,0},{2,1},{3,2},{4,7},{5,4},{6,5},{7,6},{8,11},{9,8},{10,9... | collective-permute-start | bytes 884744 | tf_op jit(solution)/shard_map/ppermute | solution.py:495
  8.7 33.7 %collective-permute-start.4 = (f32[24,128]{1,0:T(8,128)S(1)}, f32[24,128]{1,0:T(8,128)S(1)}, u32[]{:S(2)}, u32[]{:S(2)}) collective-permute-start(f32[24,128]{1,0:T(8,128)S(1)} %bitcast.13), channel_id=1, source_target_pairs={{0,4},{4,8},{8,12},{12,16},{16,20},{20,24},{24,28},{28,0},{1,5},{5... | collective-permute-start | bytes 36872 | tf_op jit(solution)/shard_map/ppermute | solution.py:496
  8.7 33.7 %collective-permute-start.5 = (f32[24,128]{1,0:T(8,128)S(1)}, f32[24,128]{1,0:T(8,128)S(1)}, u32[]{:S(2)}, u32[]{:S(2)}) collective-permute-start(f32[24,128]{1,0:T(8,128)S(1)} %bitcast.14), channel_id=1, source_target_pairs={{0,28},{4,0},{8,4},{12,8},{16,12},{20,16},{24,20},{28,24},{1,29},{... | collective-permute-start | bytes 36872 | tf_op jit(solution)/shard_map/ppermute | solution.py:497
  12.0 0.7 %copy-start.6 = (f32[4]{0:T(128)S(1)}, f32[4]{0:T(128)}, u32[]{:S(2)}) copy-start(f32[4]{0:T(128)} %radial_width.5) | copy-start | bytes 52
  12.0 0.7 %copy-start.9 = (s32[2,120]{1,0:T(2,128)S(1)}, s32[2,120]{1,0:T(2,128)}, u32[]{:S(2)}) copy-start(s32[2,120]{1,0:T(2,128)} %pairs.1) | copy-start | bytes 2884
  12.7 8.7 %copy-start.3 = (bf16[64,64]{1,0:T(8,128)(2,1)S(1)}, bf16[64,64]{1,0:T(8,128)(2,1)}, u32[]{:S(2)}) copy-start(bf16[64,64]{1,0:T(8,128)(2,1)} %update_weight.1) | copy-start | bytes 24580
  12.7 8.7 %copy-start.4 = (bf16[64,64]{1,0:T(8,128)(2,1)S(1)}, bf16[64,64]{1,0:T(8,128)(2,1)}, u32[]{:S(2)}) copy-start(bf16[64,64]{1,0:T(8,128)(2,1)} %mix_weight.1) | copy-start | bytes 24580
  21.4 0.7 %copy-start.11 = (bf16[64]{0:T(256)(128)(2,1)S(1)}, bf16[64]{0:T(256)(128)(2,1)}, u32[]{:S(2)}) copy-start(bf16[64]{0:T(256)(128)(2,1)} %param.21) | copy-start | bytes 388
  32.5 9.9 %collective-permute-start.2 = (f32[24,128]{1,0:T(8,128)S(1)}, f32[24,128]{1,0:T(8,128)S(1)}, u32[]{:S(2)}, u32[]{:S(2)}) collective-permute-start(f32[24,128]{1,0:T(8,128)S(1)} %get-tuple-element.23), channel_id=1, source_target_pairs={{0,3},{1,0},{2,1},{3,2},{4,7},{5,4},{6,5},{7,6},{8,11},{9,8},{10,9... | collective-permute-start | bytes 36872 | tf_op jit(solution)/shard_map/ppermute | solution.py:558
  39.7 6.3 %collective-permute-start.3 = (f32[24,128]{1,0:T(8,128)S(1)}, f32[24,128]{1,0:T(8,128)S(1)}, u32[]{:S(2)}, u32[]{:S(2)}) collective-permute-start(f32[24,128]{1,0:T(8,128)S(1)} %get-tuple-element.24), channel_id=1, source_target_pairs={{0,1},{1,2},{2,3},{3,0},{4,5},{5,6},{6,7},{7,4},{8,9},{9,10},{10,1... | collective-permute-start | bytes 36872 | tf_op jit(solution)/shard_map/ppermute | solution.py:559
  39.7 6.3 %copy-start.5 = (f32[1,3,1024]{2,0,1:T(1,128)S(1)}, f32[1,3,1024]{2,0,1:T(1,128)}, u32[]{:S(2)}) copy-start(f32[1,3,1024]{2,0,1:T(1,128)} %param.14) | copy-start | bytes 36868
  39.7 6.3 %copy-start.7 = (f32[1024]{0:T(1024)S(1)}, f32[1024]{0:T(1024)}, u32[]{:S(2)}) copy-start(f32[1024]{0:T(1024)} %param.16) | copy-start | bytes 12292
  46.0 0.7 %copy-start.10 = (s32[2,64]{1,0:T(2,128)S(1)}, s32[2,64]{1,0:T(2,128)}, u32[]{:S(2)}) copy-start(s32[2,64]{1,0:T(2,128)} %leaving.1) | copy-start | bytes 1540
  47.3 6.9 %collective-permute-start.6 = (f32[6,1,128]{2,1,0:T(1,128)S(1)}, f32[6,1,128]{2,1,0:T(1,128)S(1)}, u32[]{:S(2)}, u32[]{:S(2)}) collective-permute-start(f32[6,1,128]{2,1,0:T(1,128)S(1)} %get-tuple-element.28), channel_id=1, source_target_pairs={{0,1},{1,2},{2,3},{3,0},{4,5},{5,6},{6,7},{7,4},{8,9},{9,10},{10,1... | collective-permute-start | bytes 9224 | tf_op jit(solution)/shard_map/ppermute | solution.py:595
  51.8 3.6 %collective-permute-start.7 = (f32[6,1,128]{2,1,0:T(1,128)S(1)}, f32[6,1,128]{2,1,0:T(1,128)S(1)}, u32[]{:S(2)}, u32[]{:S(2)}) collective-permute-start(f32[6,1,128]{2,1,0:T(1,128)S(1)} %get-tuple-element.29), channel_id=1, source_target_pairs={{0,3},{1,0},{2,1},{3,2},{4,7},{5,4},{6,5},{7,6},{8,11},{9,8},{10,9... | collective-permute-start | bytes 9224 | tf_op jit(solution)/shard_map/ppermute | solution.py:595

commit v3 on v2

--- a/solution.py
+++ b/solution.py
@@ -13,7 +13,8 @@
 MIG = 64
 CELLS = 8
 ATOMS_DEV = CELLS * BLK
-PACK = 72
+PLACES = 3 * CELLS
+SMALL = PLACES + CELLS
 
 CUTOFF_SQUARE = 36.0
 CELL_SIDE = 10.0
@@ -44,13 +45,15 @@
     return x[:, b * BLK : (b + 1) * BLK]
 
 
-def pack_kernel(features, positions, counts, packed):
+def pack_kernel(positions, counts, small):
     lane = lax.broadcasted_iota(jnp.int32, (1, BLK), 1)
+    small[0:PLACES, :] = positions[...]
     for b in range(CELLS):
-        keep = (lane < counts[b]).astype(f32)
-        packed[b, 0:F, :] = features[:, b * BLK : (b + 1) * BLK] * keep
-        place = [positions[c * CELLS + b : c * CELLS + b + 1, :] for c in range(3)]
-        packed[b, F:PACK, :] = jnp.concatenate(place + [jnp.zeros((5, BLK), f32)], axis=0)
+        small[PLACES + b : PLACES + b + 1, :] = (lane < counts[b]).astype(f32)
+
+
+def occupancy(small):
+    return jnp.concatenate([small[PLACES + b : PLACES + b + 1, :] for b in range(CELLS)], axis=1)
 
 
 def split_lists(pairs, npairs, own_list, ghost_list, tallies):
@@ -74,14 +77,9 @@
     tallies[1] = ghost
 
 
-def feature_rows(packed):
-    return jnp.concatenate([packed[b, 0:F, :] for b in range(CELLS)], axis=1)
-
-
-def fill_tables(packed, weight, tables, base):
-    high, low = halves(feature_rows(packed))
-    stacked = jnp.concatenate([high, low], axis=0)
-    result = dot(weight, stacked)
+def fill_tables(masked, weight, tables, base):
+    high, low = halves(masked)
+    result = dot(weight, jnp.concatenate([high, low], axis=0))
     for b in range(CELLS):
         for k in range(RAD):
             tables[base + b, :, k * BLK : (k + 1) * BLK] = block_lanes(
@@ -89,32 +87,21 @@
             ).astype(bf16)
 
 
-def fill_transposed(packed, turned, base):
+def fill_transposed(masked, turned, base):
+    high = masked.astype(bf16).astype(f32)
+    stacked = jnp.concatenate([high, masked - high], axis=0)
     for b in range(CELLS):
-        x = packed[b, 0:F, :]
-        high = x.astype(bf16).astype(f32)
-        stacked = jnp.concatenate([high, x - high], axis=0)
-        turned[base + b] = stacked.T.astype(bf16)
-
-
-def fill_columns(sources, columns):
-    pieces = []
-    for packed, shift in sources:
-        for b in range(CELLS):
-            piece = packed[b, F:PACK, :]
-            if shift:
-                third = lax.broadcasted_iota(jnp.int32, (PACK - F, BLK), 0) == 2
-                piece = piece + jnp.where(third, shift, 0.0)
-            pieces.append(piece)
-    blocks = len(pieces)
-    width = PACK - F
-    if width * blocks < BLK:
-        pieces.append(jnp.zeros((BLK - width * blocks, BLK), f32))
-    turned = jnp.concatenate(pieces, axis=0).T
-    for b in range(blocks):
+        turned[base + b] = block_lanes(stacked, b).T.astype(bf16)
+
+
+def fill_columns(small, shift, columns, base):
+    third = lax.broadcasted_iota(jnp.int32, (PLACES, BLK), 0) >= 2 * CELLS
+    places = small[0:PLACES, :] + jnp.where(third, shift, 0.0)
+    turned = jnp.concatenate([places, jnp.zeros((BLK - PLACES, BLK), f32)], axis=0).T
+    for b in range(CELLS):
         for c in range(3):
-            n = width * b + c
-            columns[b, c] = jnp.broadcast_to(turned[:, n : n + 1], (BLK, BLK))
+            n = CELLS * c + b
+            columns[base + b, c] = jnp.broadcast_to(turned[:, n : n + 1], (BLK, BLK))
 
 
 def fill_penalty(penalty):
@@ -134,8 +121,8 @@
     return lax.shift_right_logical(code, 4), lax.bitwise_and(code, 15)
 
 
-def separation(packed, columns, penalty, i, j, place):
-    parts = [packed[i & 7, F + c : F + c + 1, :] - columns[j, c, place, :] for c in range(3)]
+def separation(rows, columns, penalty, i, j, place):
+    parts = [rows[i & 7, c : c + 1, :] - columns[j, c, place, :] for c in range(3)]
     squared = parts[0] * parts[0] + parts[1] * parts[1] + parts[2] * parts[2]
     if penalty is not None:
         squared = squared + penalty[(i == j).astype(jnp.int32), place, :]
@@ -143,12 +130,12 @@
     return parts, squared, remain
 
 
-def message_pass(pair_list, count, packed, columns, penalty, rates, tables, amps, message):
+def message_pass(pair_list, count, rows, columns, penalty, rates, tables, amps, message):
     def amplitudes(p, amp):
         i, j = decode(pair_list, p)
         for r in range(BLK // CHUNK):
             place = slice(r * CHUNK, (r + 1) * CHUNK)
-            _, squared, remain = separation(packed, columns, penalty, i, j, place)
+            _, squared, remain = separation(rows, columns, penalty, i, j, place)
             cutoff = remain * remain
             for k in range(RAD):
                 value = jnp.exp2(squared * rates[k]) * cutoff
@@ -174,7 +161,7 @@
 
 
 def force_pass(
-    pair_list, count, packed, columns, penalty, rates, doubled, turned, down, grads, row_sum, column_sum
+    pair_list, count, rows, columns, penalty, rates, doubled, turned, down, grads, row_sum, column_sum
 ):
     lane = lax.broadcasted_iota(jnp.int32, (CHUNK, BLK), 1)
 
@@ -189,7 +176,7 @@
         sums = [jnp.zeros((CHUNK, BLK), f32) for _ in range(3)]
         for r in range(BLK // CHUNK):
             place = slice(r * CHUNK, (r + 1) * CHUNK)
-            parts, squared, remain = separation(packed, columns, penalty, i, j, place)
+            parts, squared, remain = separation(rows, columns, penalty, i, j, place)
             plain = None
             scaled = None
             for k in range(RAD):
@@ -234,27 +221,45 @@
 
 
 def own_message_kernel(
-    packed,
+    features,
+    small,
+    small_below,
+    small_above,
     pairs,
     npairs,
     radial_width,
     weight,
+    out_weight,
     message,
     own_list,
     ghost_list,
     tallies,
+    rows,
+    columns,
+    ghost_columns,
+    penalty,
+    turned,
+    out_column,
     tables,
-    columns,
-    penalty,
     *amps,
 ):
     split_lists(pairs, npairs, own_list, ghost_list, tallies)
-    fill_tables(packed, jnp.concatenate([weight[...], weight[...]], axis=1), tables, 0)
-    fill_columns([(packed, 0.0)], columns)
+    for b in range(CELLS):
+        for c in range(3):
+            n = CELLS * c + b
+            rows[b, c : c + 1, :] = small[n : n + 1, :]
+        rows[b, 3:8, :] = jnp.zeros((5, BLK), f32)
+    masked = features[...] * occupancy(small)
+    fill_tables(masked, jnp.concatenate([weight[...], weight[...]], axis=1), tables, 0)
+    fill_transposed(masked, turned, 0)
+    fill_columns(small, 0.0, columns, 0)
+    fill_columns(small_below, -CELL_SIDE, ghost_columns, 0)
+    fill_columns(small_above, CELL_SIDE, ghost_columns, CELLS)
     fill_penalty(penalty)
+    out_column[...] = jnp.broadcast_to(as_column(out_weight[...].astype(f32)), (F, BLK))
     message[...] = jnp.zeros(message.shape, f32)
     rates = [-LOG2E * inverse for inverse in inverse_widths(radial_width)]
-    message_pass(own_list, tallies[0], packed, columns, penalty, rates, tables, amps, message)
+    message_pass(own_list, tallies[0], rows, columns, penalty, rates, tables, amps, message)
 
 
 def as_column(row):
@@ -264,19 +269,17 @@
 
 
 def node_backward(
-    message, packed, counts, weight, update_weight, mix_weight, out_weight, down
+    message, masked, occupied, weight, update_weight, mix_weight, out_column, down
 ):
     whole = jnp.concatenate([message[b] for b in range(CELLS)], axis=1)
     scaled = (whole * MESSAGE_SCALE).astype(bf16)
     first_pre = dot(update_weight[...], scaled)
     first_gate = jax.nn.sigmoid(first_pre)
-    updated = (feature_rows(packed) + first_pre * first_gate).astype(bf16)
+    updated = (masked + first_pre * first_gate).astype(bf16)
     second_pre = dot(mix_weight[...], updated)
     second_gate = jax.nn.sigmoid(second_pre)
-    lane = lax.broadcasted_iota(jnp.int32, (1, BLK), 1)
-    occupied = jnp.concatenate([(lane < counts[b]).astype(f32) for b in range(CELLS)], axis=1)
     second_grad = (
-        as_column(out_weight[...].astype(f32))
+        jnp.concatenate([out_column[...]] * CELLS, axis=1)
         * second_gate
         * (1.0 + second_pre * (1.0 - second_gate))
         * occupied
@@ -306,18 +309,22 @@
 
 
 def ghost_kernel(
-    packed,
+    features,
+    small,
     below,
     above,
+    small_below,
+    small_above,
     own_message,
+    rows,
+    columns,
     ghost_list,
     tallies,
-    counts,
     radial_width,
     weight,
     update_weight,
     mix_weight,
-    out_weight,
+    out_column,
     row_force,
     ghost_below,
     ghost_above,
@@ -325,30 +332,40 @@
     message,
     tables,
     turned,
-    columns,
     row_sum,
     column_sum,
     *buffers,
 ):
     amps, grads = buffers[:GROUP], buffers[GROUP:]
     doubled_weight = jnp.concatenate([weight[...], weight[...]], axis=1)
-    fill_tables(below, doubled_weight, tables, 0)
-    fill_tables(above, doubled_weight, tables, CELLS)
-    fill_columns([(below, -CELL_SIDE), (above, CELL_SIDE)], columns)
+    masked_below = below[...] * occupancy(small_below)
+    masked_above = above[...] * occupancy(small_above)
+    fill_tables(masked_below, doubled_weight, tables, 0)
+    fill_tables(masked_above, doubled_weight, tables, CELLS)
     message[...] = own_message[...]
     inverse = inverse_widths(radial_width)
     rates = [-LOG2E * value for value in inverse]
     count = tallies[1]
-    message_pass(ghost_list, count, packed, columns, None, rates, tables, amps, message)
-    fill_transposed(below, turned, 0)
-    fill_transposed(above, turned, CELLS)
-    node_backward(message, packed, counts, weight, update_weight, mix_weight, out_weight, down)
+    message_pass(ghost_list, count, rows, columns, None, rates, tables, amps, message)
+    fill_transposed(below[...] * occupancy(small_below), turned, 0)
+    fill_transposed(above[...] * occupancy(small_above), turned, CELLS)
+    occupied = occupancy(small)
+    node_backward(
+        message,
+        features[...] * occupied,
+        occupied,
+        weight,
+        update_weight,
+        mix_weight,
+        out_column,
+        down,
+    )
     row_sum[...] = jnp.zeros(row_sum.shape, f32)
     column_sum[...] = jnp.zeros(column_sum.shape, f32)
     force_pass(
         ghost_list,
         count,
-        packed,
+        rows,
         columns,
         None,
         rates,
@@ -366,23 +383,20 @@
 
 
 def own_force_kernel(
-    packed,
+    rows,
+    columns,
+    penalty,
+    turned,
     row_force,
     down,
     own_list,
     tallies,
     radial_width,
     force,
-    turned,
-    columns,
-    penalty,
     row_sum,
     column_sum,
     *grads,
 ):
-    fill_columns([(packed, 0.0)], columns)
-    fill_penalty(penalty)
-    fill_transposed(packed, turned, 0)
     row_sum[...] = jnp.zeros(row_sum.shape, f32)
     column_sum[...] = jnp.zeros(column_sum.shape, f32)
     inverse = inverse_widths(radial_width)
@@ -390,7 +404,7 @@
     force_pass(
         own_list,
         tallies[0],
-        packed,
+        rows,
         columns,
         penalty,
         rates,
@@ -415,11 +429,11 @@
     force,
     from_above,
     from_below,
-    positions,
+    small,
     momenta,
+    masses,
     before,
     after,
-    masses,
     leaving,
     forces,
     positions_new,
@@ -430,7 +444,7 @@
 ):
     physical = force[...] - by_component(from_above[...] + from_below[...])
     mass = jnp.concatenate([masses[...]] * 3, axis=0)
-    current = positions[...]
+    current = small[0:PLACES, :]
     spring = -SPRING_RATE * mass * (2.0 * current - before[...] - after[...])
     total = physical + spring
     moved = momenta[...] + total
@@ -459,6 +473,14 @@
         downward[q] = down[q : q + 1, :]
 
 
+def effort(microseconds):
+    return pl.CostEstimate(
+        flops=int(microseconds * 1.0e9),
+        transcendentals=0,
+        bytes_accessed=int(microseconds * 3.0e6),
+    )
+
+
 def shape(dims, kind=f32):
     return jax.ShapeDtypeStruct(dims, kind)
 
@@ -482,17 +504,22 @@
         count = lax.axis_size(axis)
         return [(i, (i + step) % count) for i in range(count)]
 
+    up = ring("dom", 1)
+    down_ring = ring("dom", -1)
+    below = lax.ppermute(features, "dom", up)
+    above = lax.ppermute(features, "dom", down_ring)
     weight = msg_weight.reshape(RAD * F, F)
-    current = positions.reshape(3 * CELLS, BLK)
-    packed = pl.pallas_call(
+    current = positions.reshape(PLACES, BLK)
+    small = pl.pallas_call(
         pack_kernel,
-        out_shape=shape((CELLS, PACK, BLK)),
-        in_specs=[VMEM, VMEM, SMEM],
+        out_shape=shape((SMALL, BLK)),
+        in_specs=[VMEM, SMEM],
         out_specs=VMEM,
         compiler_params=PARAMS,
-    )(features, current, counts)
-    below = lax.ppermute(packed, "dom", ring("dom", 1))
-    above = lax.ppermute(packed, "dom", ring("dom", -1))
+        cost_estimate=effort(5),
+    )(current, counts)
+    small_below = lax.ppermute(small, "dom", up)
+    small_above = lax.ppermute(small, "dom", down_ring)
     before = lax.ppermute(current, "bead", ring("bead", 1))
     after = lax.ppermute(current, "bead", ring("bead", -1))
 
@@ -500,41 +527,65 @@
     grad = pltpu.VMEM((BLK, RAD * BLK), f32)
     row_sum = pltpu.VMEM((CELLS + 1, 3, CHUNK, BLK), f32)
     column_sum = pltpu.VMEM((BLK, BLK), f32)
-    penalty = pltpu.VMEM((2, BLK, BLK), f32)
     listed = shape((pairs.shape[1] + 8,), jnp.int32)
-
-    def columns(blocks):
-        return pltpu.VMEM((blocks, 3, BLK, BLK), f32)
 
     def tables(blocks):
         return pltpu.VMEM((blocks, F, RAD * BLK), bf16)
 
-    def turned(blocks):
-        return pltpu.VMEM((blocks, BLK, BLK), bf16)
-
-    own_message, own_list, ghost_list, tallies = pl.pallas_call(
+    (
+        own_message,
+        own_list,
+        ghost_list,
+        tallies,
+        rows,
+        columns,
+        ghost_columns,
+        penalty,
+        turned,
+        out_column,
+    ) = pl.pallas_call(
         own_message_kernel,
-        out_shape=(shape((CELLS + 1, F, BLK)), listed, listed, shape((2,), jnp.int32)),
-        in_specs=[VMEM, SMEM, SMEM, SMEM, VMEM],
-        out_specs=(VMEM, SMEM, SMEM, SMEM),
-        scratch_shapes=[tables(CELLS), columns(CELLS), penalty] + [amp] * GROUP,
+        out_shape=(
+            shape((CELLS + 1, F, BLK)),
+            listed,
+            listed,
+            shape((2,), jnp.int32),
+            shape((CELLS, 8, BLK)),
+            shape((CELLS, 3, BLK, BLK)),
+            shape((2 * CELLS, 3, BLK, BLK)),
+            shape((2, BLK, BLK)),
+            shape((CELLS, BLK, BLK), bf16),
+            shape((F, BLK)),
+        ),
+        in_specs=[VMEM] * 4 + [SMEM] * 3 + [VMEM] * 2,
+        out_specs=(VMEM, SMEM, SMEM, SMEM) + (VMEM,) * 6,
+        scratch_shapes=[tables(CELLS)] + [amp] * GROUP,
         compiler_params=PARAMS,
-    )(packed, pairs, npairs, radial_width, weight)
+    )(
+        features,
+        small,
+        small_below,
+        small_above,
+        pairs,
+        npairs,
+        radial_width,
+        weight,
+        out_weight.reshape(1, F),
+    )
     row_force, ghost_below, ghost_above, down = pl.pallas_call(
         ghost_kernel,
         out_shape=(
-            shape((24, BLK)),
-            shape((24, BLK)),
-            shape((24, BLK)),
+            shape((PLACES, BLK)),
+            shape((PLACES, BLK)),
+            shape((PLACES, BLK)),
             shape((CELLS + 1, F, RAD * BLK), bf16),
         ),
-        in_specs=[VMEM] * 4 + [SMEM] * 4 + [VMEM] * 4,
+        in_specs=[VMEM] * 9 + [SMEM] * 3 + [VMEM] * 4,
         out_specs=(VMEM,) * 4,
         scratch_shapes=[
             pltpu.VMEM((CELLS + 1, F, BLK), f32),
             tables(2 * CELLS),
-            turned(2 * CELLS),
-            columns(2 * CELLS),
+            pltpu.VMEM((2 * CELLS, BLK, BLK), bf16),
             row_sum,
             column_sum,
         ]
@@ -542,37 +593,34 @@
         + [grad] * GROUP,
         compiler_params=PARAMS,
     )(
-        packed,
+        features,
+        small,
         below,
         above,
+        small_below,
+        small_above,
         own_message,
+        rows,
+        ghost_columns,
         ghost_list,
         tallies,
-        counts,
         radial_width,
         weight,
         update_weight,
         mix_weight,
-        out_weight.reshape(1, F),
-    )
-    from_above = lax.ppermute(ghost_below, "dom", ring("dom", -1))
-    from_below = lax.ppermute(ghost_above, "dom", ring("dom", 1))
+        out_column,
+    )
+    from_above = lax.ppermute(ghost_below, "dom", down_ring)
+    from_below = lax.ppermute(ghost_above, "dom", up)
     force = pl.pallas_call(
         own_force_kernel,
-        out_shape=shape((24, BLK)),
-        in_specs=[VMEM] * 3 + [SMEM] * 3,
+        out_shape=shape((PLACES, BLK)),
+        in_specs=[VMEM] * 6 + [SMEM] * 3,
         out_specs=VMEM,
-        scratch_shapes=[
-            turned(CELLS),
-            columns(CELLS),
-            penalty,
-            row_sum,
-            column_sum,
-        ]
-        + [grad] * GROUP,
+        scratch_shapes=[row_sum, column_sum] + [grad] * GROUP,
         compiler_params=PARAMS,
-    )(packed, row_force, down, own_list, tallies, radial_width)
-    whole = shape((3 * CELLS, BLK))
+    )(rows, columns, penalty, turned, row_force, down, own_list, tallies, radial_width)
+    whole = shape((PLACES, BLK))
     packet = shape((6, 1, 2 * MIG))
     forces, positions_new, momenta_new, upward, downward = pl.pallas_call(
         finish_kernel,
@@ -585,16 +633,14 @@
         force,
         from_above,
         from_below,
-        current,
-        momenta.reshape(3 * CELLS, BLK),
+        small,
+        momenta.reshape(PLACES, BLK),
+        masses.reshape(CELLS, BLK),
         before,
         after,
-        masses.reshape(CELLS, BLK),
         leaving,
     )
-    arrivals = lax.ppermute(upward, "dom", ring("dom", 1)) + lax.ppermute(
-        downward, "dom", ring("dom", -1)
-    )
+    arrivals = lax.ppermute(upward, "dom", up) + lax.ppermute(downward, "dom", down_ring)
     result = tuple(x.reshape(1, 3, ATOMS_DEV) for x in (forces, positions_new, momenta_new))
     return result + (arrivals.reshape(1, 6, 2 * MIG),)
 

time: 56.2 us -> 58.7 us (1.044)
  local copies, waits for them, and re-layouts: 4.32 us -> 0.7 us
  starting transfers between devices: 20.3 us -> 22.6 us
  Pallas kernels: 17.4 us -> 19.5 us
  waiting for transfers between devices: 11.9 us -> 13.6 us
    ppermute x6 -> x8, starting transfers between devices: 17.6 us -> 22.1 us  [the longest x1 8.19 us: body(): from_above = lax.ppermute(ghost_below, 'dom', down_ring)]
    unnamed x24 -> x22, local copies, waits for them, and re-layouts: 4.32 us -> 0.7 us
    ppermute x1, starting transfers between devices: 2.64 us -> 0.51 us  [body(): after = lax.ppermute(current, 'bead', ring('bead', -1))]
    ppermute x6 -> x8, waiting for transfers between devices: 11.9 us -> 13.6 us  [the longest x1 6.74 us: body(): small_below = lax.ppermute(small, 'dom', up)]
    pallas_call x1, Pallas kernels: 3.13 us -> 4.6 us  [body(): pl.pallas_call(own_message_kernel, out_shape=(shape((CELLS + 1, F, BLK)),...]
    pallas_call x3, Pallas kernels: 13.7 us -> 14.3 us  [the longest x1 11 us: body(): pl.pallas_call(ghost_kernel, out_shape=(shape((PLACES, BLK)), shape((PLAC...]
  transfers between devices with their start and end apart: 8 -> 10, of which waited for: 5 -> 4; matrix products, arithmetic and copies ran while one was open for 0% -> 0% of each run, Pallas kernels for 29% -> 32%
where the time goes in v3:
time: 58.7 us; the launch traced here: 58.5 us
  starting transfers between devices  22.6 us (39%)
  Pallas kernels  19.5 us (33%)
  waiting for transfers between devices  13.6 us (23%)
  between operations  1.46 us (2%)
  local copies, waits for them, and re-layouts  0.7 us (1%)
    pallas_call x1, Pallas kernels, body(): pl.pallas_call(ghost_kernel, out_shape=(shape((PLACES, BLK)), shape((PLAC...  11 us
    ppermute x1, starting transfers between devices, body(): from_above = lax.ppermute(ghost_below, 'dom', down_ring)  8.19 us
    ppermute x1, waiting for transfers between devices, body(): small_below = lax.ppermute(small, 'dom', up)  6.74 us
    pallas_call x1, Pallas kernels, body(): pl.pallas_call(own_message_kernel, out_shape=(shape((CELLS + 1, F, BLK)),...  4.6 us
    ppermute x1, waiting for transfers between devices, body(): from_below = lax.ppermute(ghost_above, 'dom', up)  4.07 us
    ppermute x1, starting transfers between devices, body(): lax.ppermute(upward, 'dom', up) + lax.ppermute(downward, 'dom', down_ring)  4.02 us
    ppermute x1, starting transfers between devices, body(): small_above = lax.ppermute(small, 'dom', down_ring)  3.81 us
    ppermute x1, starting transfers between devices, body(): below = lax.ppermute(features, 'dom', up)  3.08 us
  transfers between devices with their start and end apart: 10, of which 4 were waited for; matrix products, arithmetic and copies ran while one was open for 0% of the time, Pallas kernels for 32%

profile of v3, /device:TPU:0, one launch (start us, length us, event | category | flops | bytes accessed | tf_op | source)
XLA Modules:
  0.0 58.5 jit_solution(4060243653194476615)
XLA Ops:
  0.6 3.1 %collective-permute-start.2 = (f32[64,1024]{1,0:T(8,128)}, f32[64,1024]{1,0:T(8,128)S(1)}, u32[]{:S(2)}, u32[]{:S(2)}) collective-permute-start(f32[64,1024]{1,0:T(8,128)} %features.3), channel_id=1, source_target_pairs={{0,1},{1,2},{2,3},{3,0},{4,5},{5,6},{6,7},{7,4},{8,9},{9,10},{10,1... | collective-permute-start | bytes 786440 | tf_op jit(solution)/shard_map/ppermute | solution.py:509
  3.7 2.1 %collective-permute-start.3 = (f32[64,1024]{1,0:T(8,128)}, f32[64,1024]{1,0:T(8,128)S(1)}, u32[]{:S(2)}, u32[]{:S(2)}) collective-permute-start(f32[64,1024]{1,0:T(8,128)} %features.3), channel_id=1, source_target_pairs={{0,3},{1,0},{2,1},{3,2},{4,7},{5,4},{6,5},{7,6},{8,11},{9,8},{10,9... | collective-permute-start | bytes 786440 | tf_op jit(solution)/shard_map/ppermute | solution.py:510
  5.8 0.7 %copy-done.10 = s32[8]{0:T(128)S(1)} copy-done((s32[8]{0:T(128)S(1)}, s32[8]{0:T(128)}, u32[]{:S(2)}) %copy-start.10) | copy-done | bytes 56
  6.5 0.8 %shard_map.156.small = f32[32,128]{1,0:T(8,128)S(1)} custom-call(f32[24,128]{1,0:T(8,128)} %bitcast.positions, s32[8]{0:T(128)S(1)} %copy-done.10), custom_call_target="tpu_custom_call" | custom-call | flops 5000000000 | bytes 15000000 | tf_op jit(solution)/shard_map/pallas_call | solution.py:513
  7.3 0.1 collective-permute-start
  7.3 3.8 %collective-permute-start.1 = (f32[32,128]{1,0:T(8,128)S(1)}, f32[32,128]{1,0:T(8,128)S(1)}, u32[]{:S(2)}, u32[]{:S(2)}) collective-permute-start(f32[32,128]{1,0:T(8,128)S(1)} %shard_map.156.small), channel_id=1, source_target_pairs={{0,3},{1,0},{2,1},{3,2},{4,7},{5,4},{6,5},{7,6},{8,11},{9,8},{10,9... | collective-permute-start | bytes 49160 | tf_op jit(solution)/shard_map/ppermute | solution.py:522
  11.1 0.0 collective-permute-start.6
  11.8 6.7 %collective-permute-done.small_below = f32[32,128]{1,0:T(8,128)S(1)} collective-permute-done((f32[32,128]{1,0:T(8,128)S(1)}, f32[32,128]{1,0:T(8,128)S(1)}, u32[]{:S(2)}, u32[]{:S(2)}) %collective-permute-start) | collective-permute-done | bytes 16416 | tf_op jit(solution)/shard_map/ppermute | solution.py:521
  18.5 0.5 collective-permute-start.7
  19.1 4.6 %shard_map.157 = (f32[9,64,128]{2,1,0:T(8,128)S(1)}, s32[128]{0:T(128)S(1)}, s32[128]{0:T(128)S(1)}, s32[2]{0:T(128)S(1)}, f32[8,8,128]{2,1,0:T(8,128)S(1)}, /*i...) custom-call(f32[64,1024]{1,0:T(8,128)S(1)} %copy-done, ...), custom_call_target="tpu_custom_call" | custom-call | tf_op jit(solution)/shard_map/pallas_call | solution.py:546
  23.7 0.0 collective-permute-done.2.below
  23.8 0.0 copy-start.4
  23.8 0.0 copy-start.6
  23.8 0.0 copy-start.8
  23.8 11.0 %shard_map.158 = (f32[24,128]{1,0:T(8,128)S(1)}, f32[24,128]{1,0:T(8,128)S(1)}, f32[24,128]{1,0:T(8,128)S(1)}, bf16[9,64,512]{2,1,0:T(8,128)(2,1)S(1)}) custom-call(f32[64,1024]{1,0:T(8,128)S(1)} %copy-done, f32[32,128]{1,0:T(8,128)S(1)} %shard_map.156.small, f32[64,1024]{1,0:T(8,128)S(1)} %collective-permute-done.2.below, ...), custom_call_target="tpu_custom_call" | custom-call | tf_op jit(solution)/shard_map/pallas_call | solution.py:575
  34.7 8.2 %collective-permute-start.4 = (f32[24,128]{1,0:T(8,128)S(1)}, f32[24,128]{1,0:T(8,128)S(1)}, u32[]{:S(2)}, u32[]{:S(2)}) collective-permute-start(f32[24,128]{1,0:T(8,128)S(1)} %get-tuple-element.35), channel_id=1, source_target_pairs={{0,3},{1,0},{2,1},{3,2},{4,7},{5,4},{6,5},{7,6},{8,11},{9,8},{10,9... | collective-permute-start | bytes 36872 | tf_op jit(solution)/shard_map/ppermute | solution.py:613
  42.9 2.6 %shard_map.159.force = f32[24,128]{1,0:T(8,128)S(1)} custom-call(f32[8,8,128]{2,1,0:T(8,128)S(1)} %get-tuple-element.23.rows, f32[8,3,128,128]{3,2,1,0:T(8,128)S(1)} %get-tuple-element.24.columns, f32[2,128,128]{2,1,0:T(8,128)S(1)} %get-tuple-element.25.penalty, bf16[8,128,128]{2,1,0:T(8,128)(2,1)S(1)} %get-tuple-element.26.turned, ...), custom_call_target="tpu_custom_call" | custom-call | tf_op jit(solution)/shard_map/pallas_call | solution.py:615
  45.6 4.1 %collective-permute-done.5.from_below = f32[24,128]{1,0:T(8,128)S(1)} collective-permute-done((f32[24,128]{1,0:T(8,128)S(1)}, f32[24,128]{1,0:T(8,128)S(1)}, u32[]{:S(2)}, u32[]{:S(2)}) %collective-permute-start.5) | collective-permute-done | bytes 12320 | tf_op jit(solution)/shard_map/ppermute | solution.py:614
  49.6 0.6 %shard_map.160 = (f32[24,128]{1,0:T(8,128)}, f32[24,128]{1,0:T(8,128)}, f32[24,128]{1,0:T(8,128)}, f32[6,1,128]{2,1,0:T(1,128)S(1)}, f32[6,1,128]{2,1,0:T(1,128)S(1)}) custom-call(f32[24,128]{1,0:T(8,128)S(1)} %shard_map.159.force, f32[24,128]{1,0:T(8,128)S(1)} %collective-permute-done.4.from_above, f32[24,128]{1,0:T(8,128)S(1)} %collective-permute-done.5.from_below, ...), custom_call_target="tpu_custom_call" | custom-call | tf_op jit(solution)/shard_map/pallas_call | solution.py:625
  50.3 4.0 %collective-permute-start.8 = (f32[6,1,128]{2,1,0:T(1,128)S(1)}, f32[6,1,128]{2,1,0:T(1,128)S(1)}, u32[]{:S(2)}, u32[]{:S(2)}) collective-permute-start(f32[6,1,128]{2,1,0:T(1,128)S(1)} %get-tuple-element.40), channel_id=1, source_target_pairs={{0,1},{1,2},{2,3},{3,0},{4,5},{5,6},{6,7},{7,4},{8,9},{9,10},{10,1... | collective-permute-start | bytes 9224 | tf_op jit(solution)/shard_map/ppermute | solution.py:643
  54.3 0.8 %collective-permute-start.9 = (f32[6,1,128]{2,1,0:T(1,128)S(1)}, f32[6,1,128]{2,1,0:T(1,128)S(1)}, u32[]{:S(2)}, u32[]{:S(2)}) collective-permute-start(f32[6,1,128]{2,1,0:T(1,128)S(1)} %get-tuple-element.41), channel_id=1, source_target_pairs={{0,3},{1,0},{2,1},{3,2},{4,7},{5,4},{6,5},{7,6},{8,11},{9,8},{10,9... | collective-permute-start | bytes 9224 | tf_op jit(solution)/shard_map/ppermute | solution.py:643
  55.1 1.6 %collective-permute-done.8 = f32[6,1,128]{2,1,0:T(1,128)S(1)} collective-permute-done((f32[6,1,128]{2,1,0:T(1,128)S(1)}, f32[6,1,128]{2,1,0:T(1,128)S(1)}, u32[]{:S(2)}, u32[]{:S(2)}) %collective-permute-start.8) | collective-permute-done | bytes 3104 | tf_op jit(solution)/shard_map/ppermute | solution.py:643
  56.7 1.2 %collective-permute-done.9 = f32[6,1,128]{2,1,0:T(1,128)S(1)} collective-permute-done((f32[6,1,128]{2,1,0:T(1,128)S(1)}, f32[6,1,128]{2,1,0:T(1,128)S(1)}, u32[]{:S(2)}, u32[]{:S(2)}) %collective-permute-start.9) | collective-permute-done | bytes 3104 | tf_op jit(solution)/shard_map/ppermute | solution.py:643
  57.9 0.6 add_bitcast_fusion
  (24 shorter events, 0.1 us)
Async XLA Ops:
  0.6 23.1 %collective-permute-start.2 = (f32[64,1024]{1,0:T(8,128)}, f32[64,1024]{1,0:T(8,128)S(1)}, u32[]{:S(2)}, u32[]{:S(2)}) collective-permute-start(f32[64,1024]{1,0:T(8,128)} %features.3), channel_id=1, source_target_pairs={{0,1},{1,2},{2,3},{3,0},{4,5},{5,6},{6,7},{7,4},{8,9},{9,10},{10,1... | collective-permute-start | bytes 786440 | tf_op jit(solution)/shard_map/ppermute | solution.py:509
  3.7 20.0 %collective-permute-start.3 = (f32[64,1024]{1,0:T(8,128)}, f32[64,1024]{1,0:T(8,128)S(1)}, u32[]{:S(2)}, u32[]{:S(2)}) collective-permute-start(f32[64,1024]{1,0:T(8,128)} %features.3), channel_id=1, source_target_pairs={{0,3},{1,0},{2,1},{3,2},{4,7},{5,4},{6,5},{7,6},{8,11},{9,8},{10,9... | collective-permute-start | bytes 786440 | tf_op jit(solution)/shard_map/ppermute | solution.py:510
  5.8 0.7 %copy-start.10 = (s32[8]{0:T(128)S(1)}, s32[8]{0:T(128)}, u32[]{:S(2)}) copy-start(s32[8]{0:T(128)} %counts.1) | copy-start | bytes 100
  6.5 12.6 %copy-start = (f32[64,1024]{1,0:T(8,128)S(1)}, f32[64,1024]{1,0:T(8,128)}, u32[]{:S(2)}) copy-start(f32[64,1024]{1,0:T(8,128)} %features.3) | copy-start | bytes 786436
  6.5 12.6 %copy-start.1 = (bf16[4,64,64]{2,1,0:T(8,128)(2,1)S(1)}, bf16[4,64,64]{2,1,0:T(8,128)(2,1)}, u32[]{:S(2)}) copy-start(bf16[4,64,64]{2,1,0:T(8,128)(2,1)} %param.18) | copy-start | bytes 98308
  6.5 12.6 %copy-start.5 = (f32[4]{0:T(128)S(1)}, f32[4]{0:T(128)}, u32[]{:S(2)}) copy-start(f32[4]{0:T(128)} %radial_width.5) | copy-start | bytes 52
  6.5 12.6 %copy-start.7 = (s32[2,120]{1,0:T(2,128)S(1)}, s32[2,120]{1,0:T(2,128)}, u32[]{:S(2)}) copy-start(s32[2,120]{1,0:T(2,128)} %pairs.1) | copy-start | bytes 2884
  6.5 12.6 %copy-start.9 = (bf16[64]{0:T(256)(128)(2,1)S(1)}, bf16[64]{0:T(256)(128)(2,1)}, u32[]{:S(2)}) copy-start(bf16[64]{0:T(256)(128)(2,1)} %param.21) | copy-start | bytes 388
  6.5 17.3 %copy-start.2 = (bf16[64,64]{1,0:T(8,128)(2,1)S(1)}, bf16[64,64]{1,0:T(8,128)(2,1)}, u32[]{:S(2)}) copy-start(bf16[64,64]{1,0:T(8,128)(2,1)} %update_weight.1) | copy-start | bytes 24580
  6.5 17.3 %copy-start.3 = (bf16[64,64]{1,0:T(8,128)(2,1)S(1)}, bf16[64,64]{1,0:T(8,128)(2,1)}, u32[]{:S(2)}) copy-start(bf16[64,64]{1,0:T(8,128)(2,1)} %mix_weight.1) | copy-start | bytes 24580
  7.3 11.3 %collective-permute-start = (f32[32,128]{1,0:T(8,128)S(1)}, f32[32,128]{1,0:T(8,128)S(1)}, u32[]{:S(2)}, u32[]{:S(2)}) collective-permute-start(f32[32,128]{1,0:T(8,128)S(1)} %shard_map.156.small), channel_id=1, source_target_pairs={{0,1},{1,2},{2,3},{3,0},{4,5},{5,6},{6,7},{7,4},{8,9},{9,10},{10,1... | collective-permute-start | bytes 49160 | tf_op jit(solution)/shard_map/ppermute | solution.py:521
  7.3 11.7 %collective-permute-start.1 = (f32[32,128]{1,0:T(8,128)S(1)}, f32[32,128]{1,0:T(8,128)S(1)}, u32[]{:S(2)}, u32[]{:S(2)}) collective-permute-start(f32[32,128]{1,0:T(8,128)S(1)} %shard_map.156.small), channel_id=1, source_target_pairs={{0,3},{1,0},{2,1},{3,2},{4,7},{5,4},{6,5},{7,6},{8,11},{9,8},{10,9... | collective-permute-start | bytes 49160 | tf_op jit(solution)/shard_map/ppermute | solution.py:522
  11.1 34.4 %collective-permute-start.6 = (f32[24,128]{1,0:T(8,128)}, f32[24,128]{1,0:T(8,128)S(1)}, u32[]{:S(2)}, u32[]{:S(2)}) collective-permute-start(f32[24,128]{1,0:T(8,128)} %bitcast.positions), channel_id=1, source_target_pairs={{0,4},{4,8},{8,12},{12,16},{16,20},{20,24},{24,28},{28,0},{1,5},{5... | collective-permute-start | bytes 36872 | tf_op jit(solution)/shard_map/ppermute | solution.py:523
  18.5 27.0 %collective-permute-start.7 = (f32[24,128]{1,0:T(8,128)}, f32[24,128]{1,0:T(8,128)S(1)}, u32[]{:S(2)}, u32[]{:S(2)}) collective-permute-start(f32[24,128]{1,0:T(8,128)} %bitcast.positions), channel_id=1, source_target_pairs={{0,28},{4,0},{8,4},{12,8},{16,12},{20,16},{24,20},{28,24},{1,29},{... | collective-permute-start | bytes 36872 | tf_op jit(solution)/shard_map/ppermute | solution.py:524
  23.8 25.9 %copy-start.4 = (f32[1,3,1024]{2,0,1:T(1,128)S(1)}, f32[1,3,1024]{2,0,1:T(1,128)}, u32[]{:S(2)}) copy-start(f32[1,3,1024]{2,0,1:T(1,128)} %param.14) | copy-start | bytes 36868
  23.8 25.9 %copy-start.6 = (f32[1024]{0:T(1024)S(1)}, f32[1024]{0:T(1024)}, u32[]{:S(2)}) copy-start(f32[1024]{0:T(1024)} %param.16) | copy-start | bytes 12292
  23.8 25.9 %copy-start.8 = (s32[2,64]{1,0:T(2,128)S(1)}, s32[2,64]{1,0:T(2,128)}, u32[]{:S(2)}) copy-start(s32[2,64]{1,0:T(2,128)} %leaving.1) | copy-start | bytes 1540
  34.7 10.8 %collective-permute-start.4 = (f32[24,128]{1,0:T(8,128)S(1)}, f32[24,128]{1,0:T(8,128)S(1)}, u32[]{:S(2)}, u32[]{:S(2)}) collective-permute-start(f32[24,128]{1,0:T(8,128)S(1)} %get-tuple-element.35), channel_id=1, source_target_pairs={{0,3},{1,0},{2,1},{3,2},{4,7},{5,4},{6,5},{7,6},{8,11},{9,8},{10,9... | collective-permute-start | bytes 36872 | tf_op jit(solution)/shard_map/ppermute | solution.py:613
  42.9 6.7 %collective-permute-start.5 = (f32[24,128]{1,0:T(8,128)S(1)}, f32[24,128]{1,0:T(8,128)S(1)}, u32[]{:S(2)}, u32[]{:S(2)}) collective-permute-start(f32[24,128]{1,0:T(8,128)S(1)} %get-tuple-element.36), channel_id=1, source_target_pairs={{0,1},{1,2},{2,3},{3,0},{4,5},{5,6},{6,7},{7,4},{8,9},{9,10},{10,1... | collective-permute-start | bytes 36872 | tf_op jit(solution)/shard_map/ppermute | solution.py:614
  50.3 6.4 %collective-permute-start.8 = (f32[6,1,128]{2,1,0:T(1,128)S(1)}, f32[6,1,128]{2,1,0:T(1,128)S(1)}, u32[]{:S(2)}, u32[]{:S(2)}) collective-permute-start(f32[6,1,128]{2,1,0:T(1,128)S(1)} %get-tuple-element.40), channel_id=1, source_target_pairs={{0,1},{1,2},{2,3},{3,0},{4,5},{5,6},{6,7},{7,4},{8,9},{9,10},{10,1... | collective-permute-start | bytes 9224 | tf_op jit(solution)/shard_map/ppermute | solution.py:643
  54.3 3.6 %collective-permute-start.9 = (f32[6,1,128]{2,1,0:T(1,128)S(1)}, f32[6,1,128]{2,1,0:T(1,128)S(1)}, u32[]{:S(2)}, u32[]{:S(2)}) collective-permute-start(f32[6,1,128]{2,1,0:T(1,128)S(1)} %get-tuple-element.41), channel_id=1, source_target_pairs={{0,3},{1,0},{2,1},{3,2},{4,7},{5,4},{6,5},{7,6},{8,11},{9,8},{10,9... | collective-permute-start | bytes 9224 | tf_op jit(solution)/shard_map/ppermute | solution.py:643

commit v4 on v3

--- a/solution.py
+++ b/solution.py
@@ -223,8 +223,6 @@
 def own_message_kernel(
     features,
     small,
-    small_below,
-    small_above,
     pairs,
     npairs,
     radial_width,
@@ -236,7 +234,6 @@
     tallies,
     rows,
     columns,
-    ghost_columns,
     penalty,
     turned,
     out_column,
@@ -253,8 +250,6 @@
     fill_tables(masked, jnp.concatenate([weight[...], weight[...]], axis=1), tables, 0)
     fill_transposed(masked, turned, 0)
     fill_columns(small, 0.0, columns, 0)
-    fill_columns(small_below, -CELL_SIDE, ghost_columns, 0)
-    fill_columns(small_above, CELL_SIDE, ghost_columns, CELLS)
     fill_penalty(penalty)
     out_column[...] = jnp.broadcast_to(as_column(out_weight[...].astype(f32)), (F, BLK))
     message[...] = jnp.zeros(message.shape, f32)
@@ -317,7 +312,6 @@
     small_above,
     own_message,
     rows,
-    columns,
     ghost_list,
     tallies,
     radial_width,
@@ -332,11 +326,14 @@
     message,
     tables,
     turned,
+    columns,
     row_sum,
     column_sum,
     *buffers,
 ):
     amps, grads = buffers[:GROUP], buffers[GROUP:]
+    fill_columns(small_below, -CELL_SIDE, columns, 0)
+    fill_columns(small_above, CELL_SIDE, columns, CELLS)
     doubled_weight = jnp.concatenate([weight[...], weight[...]], axis=1)
     masked_below = below[...] * occupancy(small_below)
     masked_above = above[...] * occupancy(small_above)
@@ -520,8 +517,6 @@
     )(current, counts)
     small_below = lax.ppermute(small, "dom", up)
     small_above = lax.ppermute(small, "dom", down_ring)
-    before = lax.ppermute(current, "bead", ring("bead", 1))
-    after = lax.ppermute(current, "bead", ring("bead", -1))
 
     amp = pltpu.VMEM((RAD * BLK, BLK), bf16)
     grad = pltpu.VMEM((BLK, RAD * BLK), f32)
@@ -539,7 +534,6 @@
         tallies,
         rows,
         columns,
-        ghost_columns,
         penalty,
         turned,
         out_column,
@@ -552,26 +546,26 @@
             shape((2,), jnp.int32),
             shape((CELLS, 8, BLK)),
             shape((CELLS, 3, BLK, BLK)),
-            shape((2 * CELLS, 3, BLK, BLK)),
             shape((2, BLK, BLK)),
             shape((CELLS, BLK, BLK), bf16),
             shape((F, BLK)),
         ),
-        in_specs=[VMEM] * 4 + [SMEM] * 3 + [VMEM] * 2,
-        out_specs=(VMEM, SMEM, SMEM, SMEM) + (VMEM,) * 6,
+        in_specs=[VMEM] * 2 + [SMEM] * 3 + [VMEM] * 2,
+        out_specs=(VMEM, SMEM, SMEM, SMEM) + (VMEM,) * 5,
         scratch_shapes=[tables(CELLS)] + [amp] * GROUP,
         compiler_params=PARAMS,
     )(
         features,
         small,
-        small_below,
-        small_above,
         pairs,
         npairs,
         radial_width,
         weight,
         out_weight.reshape(1, F),
     )
+    late, own_message = lax.optimization_barrier((current, own_message))
+    before = lax.ppermute(late, "bead", ring("bead", 1))
+    after = lax.ppermute(late, "bead", ring("bead", -1))
     row_force, ghost_below, ghost_above, down = pl.pallas_call(
         ghost_kernel,
         out_shape=(
@@ -580,12 +574,13 @@
             shape((PLACES, BLK)),
             shape((CELLS + 1, F, RAD * BLK), bf16),
         ),
-        in_specs=[VMEM] * 9 + [SMEM] * 3 + [VMEM] * 4,
+        in_specs=[VMEM] * 8 + [SMEM] * 3 + [VMEM] * 4,
         out_specs=(VMEM,) * 4,
         scratch_shapes=[
             pltpu.VMEM((CELLS + 1, F, BLK), f32),
             tables(2 * CELLS),
             pltpu.VMEM((2 * CELLS, BLK, BLK), bf16),
+            pltpu.VMEM((2 * CELLS, 3, BLK, BLK), f32),
             row_sum,
             column_sum,
         ]
@@ -601,7 +596,6 @@
         small_above,
         own_message,
         rows,
-        ghost_columns,
         ghost_list,
         tallies,
         radial_width,

time: 58.7 us -> 51.4 us (0.88)
  waiting for transfers between devices: 13.6 us -> 6.69 us
  starting transfers between devices: 22.6 us -> 19.7 us
  Pallas kernels: 19.5 us -> 21.5 us
  local copies, waits for them, and re-layouts: 0.7 us -> 1.41 us
    ppermute x1, waiting for transfers between devices: 6.74 us -> 0.78 us  [body(): small_below = lax.ppermute(small, 'dom', up)]
    pallas_call x1, Pallas kernels: 11 us -> 13.1 us  [body(): pl.pallas_call(ghost_kernel, out_shape=(shape((PLACES, BLK)), shape((PLAC...]
    ppermute x1, waiting for transfers between devices: 0.01 us -> 2.01 us  [body(): small_above = lax.ppermute(small, 'dom', down_ring)]
    ppermute x1, starting transfers between devices: 8.19 us -> 6.34 us  [body(): from_above = lax.ppermute(ghost_below, 'dom', down_ring)]
    ppermute x1, starting transfers between devices: 3.81 us -> 2.01 us  [body(): small_above = lax.ppermute(small, 'dom', down_ring)]
    ppermute x1, waiting for transfers between devices: 4.07 us -> 2.31 us  [body(): from_below = lax.ppermute(ghost_above, 'dom', up)]
    ppermute x1, starting transfers between devices: 0.83 us -> 2.29 us  [body(): lax.ppermute(downward, 'dom', down_ring)]
    ppermute x1, starting transfers between devices: 4.02 us -> 2.7 us  [body(): lax.ppermute(upward, 'dom', up) + lax.ppermute(downward, 'dom', down_ring)]
  transfers between devices with their start and end apart: 10 -> 10, of which waited for: 4 -> 4; matrix products, arithmetic and copies ran while one was open for 0% -> 0% of each run, Pallas kernels for 32% -> 41%
where the time goes in v4:
time: 51.4 us; the launch traced here: 51.3 us
  Pallas kernels  21.5 us (42%)
  starting transfers between devices  19.7 us (38%)
  waiting for transfers between devices  6.69 us (13%)
  between operations  1.46 us (3%)
  local copies, waits for them, and re-layouts  1.41 us (3%)
  other arithmetic  0.58 us (1%)
    pallas_call x1, Pallas kernels, body(): pl.pallas_call(ghost_kernel, out_shape=(shape((PLACES, BLK)), shape((PLAC...  13.1 us
    ppermute x1, starting transfers between devices, body(): from_above = lax.ppermute(ghost_below, 'dom', down_ring)  6.34 us
    pallas_call x1, Pallas kernels, body(): pl.pallas_call(own_message_kernel, out_shape=(shape((CELLS + 1, F, BLK)),...  4.15 us
    pallas_call x1, Pallas kernels, body(): pl.pallas_call(own_force_kernel, out_shape=shape((PLACES, BLK)), in_specs...  3.14 us
    ppermute x1, starting transfers between devices, body(): below = lax.ppermute(features, 'dom', up)  3.08 us
    ppermute x1, starting transfers between devices, body(): lax.ppermute(upward, 'dom', up) + lax.ppermute(downward, 'dom', down_ring)  2.7 us
    ppermute x1, waiting for transfers between devices, body(): from_below = lax.ppermute(ghost_above, 'dom', up)  2.31 us
    ppermute x1, starting transfers between devices, body(): lax.ppermute(downward, 'dom', down_ring)  2.29 us
  transfers between devices with their start and end apart: 10, of which 4 were waited for; matrix products, arithmetic and copies ran while one was open for 0% of the time, Pallas kernels for 41%

profile of v4, /device:TPU:0, one launch (start us, length us, event | category | flops | bytes accessed | tf_op | source)
XLA Modules:
  0.0 51.3 jit_solution(14755564896543319188)
XLA Ops:
  0.6 3.1 %collective-permute-start = (f32[64,1024]{1,0:T(8,128)}, f32[64,1024]{1,0:T(8,128)S(1)}, u32[]{:S(2)}, u32[]{:S(2)}) collective-permute-start(f32[64,1024]{1,0:T(8,128)} %features.3), channel_id=1, source_target_pairs={{0,1},{1,2},{2,3},{3,0},{4,5},{5,6},{6,7},{7,4},{8,9},{9,10},{10,1... | collective-permute-start | bytes 786440 | tf_op jit(solution)/shard_map/ppermute | solution.py:506
  3.7 2.1 %collective-permute-start.1 = (f32[64,1024]{1,0:T(8,128)}, f32[64,1024]{1,0:T(8,128)S(1)}, u32[]{:S(2)}, u32[]{:S(2)}) collective-permute-start(f32[64,1024]{1,0:T(8,128)} %features.3), channel_id=1, source_target_pairs={{0,3},{1,0},{2,1},{3,2},{4,7},{5,4},{6,5},{7,6},{8,11},{9,8},{10,9... | collective-permute-start | bytes 786440 | tf_op jit(solution)/shard_map/ppermute | solution.py:507
  5.8 0.7 %copy-done.10 = f32[1,3,1024]{2,0,1:T(1,128)S(1)} copy-done((f32[1,3,1024]{2,0,1:T(1,128)S(1)}, f32[1,3,1024]{2,0,1:T(1,128)}, u32[]{:S(2)}) %copy-start.10) | copy-done | bytes 12312
  6.5 0.7 %copy-done.12 = s32[8]{0:T(128)S(1)} copy-done((s32[8]{0:T(128)S(1)}, s32[8]{0:T(128)}, u32[]{:S(2)}) %copy-start.12) | copy-done | bytes 56
  7.2 0.5 %shard_map.156.small = f32[32,128]{1,0:T(8,128)S(1)} custom-call(f32[24,128]{1,0:T(8,128)S(1)} %bitcast.15, s32[8]{0:T(128)S(1)} %copy-done.12), custom_call_target="tpu_custom_call" | custom-call | flops 5000000000 | bytes 15000000 | tf_op jit(solution)/shard_map/pallas_call | solution.py:510
  7.8 2.0 %collective-permute-start.3 = (f32[32,128]{1,0:T(8,128)S(1)}, f32[32,128]{1,0:T(8,128)S(1)}, u32[]{:S(2)}, u32[]{:S(2)}) collective-permute-start(f32[32,128]{1,0:T(8,128)S(1)} %shard_map.156.small), channel_id=1, source_target_pairs={{0,3},{1,0},{2,1},{3,2},{4,7},{5,4},{6,5},{7,6},{8,11},{9,8},{10,9... | collective-permute-start | bytes 49160 | tf_op jit(solution)/shard_map/ppermute | solution.py:519
  9.8 0.1 collective-permute-start.2
  10.6 4.2 %shard_map.157 = (f32[9,64,128]{2,1,0:T(8,128)S(1)}, s32[128]{0:T(128)S(1)}, s32[128]{0:T(128)S(1)}, s32[2]{0:T(128)S(1)}, f32[8,8,128]{2,1,0:T(8,128)S(1)}, /*i...) custom-call(f32[64,1024]{1,0:T(8,128)S(1)} %copy-done, ...), custom_call_target="tpu_custom_call" | custom-call | tf_op jit(solution)/shard_map/pallas_call | solution.py:540
  14.7 1.1 %collective-permute-start.7 = (f32[24,128]{1,0:T(8,128)S(1)}, f32[24,128]{1,0:T(8,128)S(1)}, u32[]{:S(2)}, u32[]{:S(2)}) collective-permute-start(f32[24,128]{1,0:T(8,128)S(1)} %bitcast.16), channel_id=1, source_target_pairs={{0,28},{4,0},{8,4},{12,8},{16,12},{20,16},{24,20},{28,24},{1,29},{... | collective-permute-start | bytes 36872 | tf_op jit(solution)/shard_map/ppermute | solution.py:568
  15.8 2.0 %collective-permute-done.3.small_above = f32[32,128]{1,0:T(8,128)S(1)} collective-permute-done((f32[32,128]{1,0:T(8,128)S(1)}, f32[32,128]{1,0:T(8,128)S(1)}, u32[]{:S(2)}, u32[]{:S(2)}) %collective-permute-start.3) | collective-permute-done | bytes 16416 | tf_op jit(solution)/shard_map/ppermute | solution.py:519
  17.8 0.0 collective-permute-start.6
  17.8 0.8 %collective-permute-done.2.small_below = f32[32,128]{1,0:T(8,128)S(1)} collective-permute-done((f32[32,128]{1,0:T(8,128)S(1)}, f32[32,128]{1,0:T(8,128)S(1)}, u32[]{:S(2)}, u32[]{:S(2)}) %collective-permute-start.2) | collective-permute-done | bytes 16416 | tf_op jit(solution)/shard_map/ppermute | solution.py:518
  18.6 0.0 collective-permute-done.below
  18.6 13.1 %shard_map.158 = (f32[24,128]{1,0:T(8,128)S(1)}, f32[24,128]{1,0:T(8,128)S(1)}, f32[24,128]{1,0:T(8,128)S(1)}, bf16[9,64,512]{2,1,0:T(8,128)(2,1)S(1)}) custom-call(f32[64,1024]{1,0:T(8,128)S(1)} %copy-done, f32[32,128]{1,0:T(8,128)S(1)} %shard_map.156.small, f32[64,1024]{1,0:T(8,128)S(1)} %collective-permute-done.below, ...), custom_call_target="tpu_custom_call" | custom-call | tf_op jit(solution)/shard_map/pallas_call | solution.py:569
  31.7 0.0 copy-start.6
  31.7 0.0 copy-start.8
  31.7 6.3 %collective-permute-start.4 = (f32[24,128]{1,0:T(8,128)S(1)}, f32[24,128]{1,0:T(8,128)S(1)}, u32[]{:S(2)}, u32[]{:S(2)}) collective-permute-start(f32[24,128]{1,0:T(8,128)S(1)} %get-tuple-element.36), channel_id=1, source_target_pairs={{0,3},{1,0},{2,1},{3,2},{4,7},{5,4},{6,5},{7,6},{8,11},{9,8},{10,9... | collective-permute-start | bytes 36872 | tf_op jit(solution)/shard_map/ppermute | solution.py:607
  38.1 3.1 %shard_map.159.force = f32[24,128]{1,0:T(8,128)S(1)} custom-call(f32[8,8,128]{2,1,0:T(8,128)S(1)} %get-tuple-element.24.rows, f32[8,3,128,128]{3,2,1,0:T(8,128)S(1)} %get-tuple-element.25.columns, f32[2,128,128]{2,1,0:T(8,128)S(1)} %get-tuple-element.26.penalty, bf16[8,128,128]{2,1,0:T(8,128)(2,1)S(1)} %get-tuple-element.27.turned, ...), custom_call_target="tpu_custom_call" | custom-call | tf_op jit(solution)/shard_map/pallas_call | solution.py:609
  41.3 2.3 %collective-permute-done.5.from_below = f32[24,128]{1,0:T(8,128)S(1)} collective-permute-done((f32[24,128]{1,0:T(8,128)S(1)}, f32[24,128]{1,0:T(8,128)S(1)}, u32[]{:S(2)}, u32[]{:S(2)}) %collective-permute-start.5) | collective-permute-done | bytes 12320 | tf_op jit(solution)/shard_map/ppermute | solution.py:608
  43.6 0.6 %shard_map.160 = (f32[24,128]{1,0:T(8,128)}, f32[24,128]{1,0:T(8,128)}, f32[24,128]{1,0:T(8,128)}, f32[6,1,128]{2,1,0:T(1,128)S(1)}, f32[6,1,128]{2,1,0:T(1,128)S(1)}) custom-call(f32[24,128]{1,0:T(8,128)S(1)} %shard_map.159.force, f32[24,128]{1,0:T(8,128)S(1)} %collective-permute-done.4.from_above, f32[24,128]{1,0:T(8,128)S(1)} %collective-permute-done.5.from_below, ...), custom_call_target="tpu_custom_call" | custom-call | tf_op jit(solution)/shard_map/pallas_call | solution.py:619
  44.2 2.7 %collective-permute-start.8 = (f32[6,1,128]{2,1,0:T(1,128)S(1)}, f32[6,1,128]{2,1,0:T(1,128)S(1)}, u32[]{:S(2)}, u32[]{:S(2)}) collective-permute-start(f32[6,1,128]{2,1,0:T(1,128)S(1)} %get-tuple-element.42), channel_id=1, source_target_pairs={{0,1},{1,2},{2,3},{3,0},{4,5},{5,6},{6,7},{7,4},{8,9},{9,10},{10,1... | collective-permute-start | bytes 9224 | tf_op jit(solution)/shard_map/ppermute | solution.py:637
  46.9 2.3 %collective-permute-start.9 = (f32[6,1,128]{2,1,0:T(1,128)S(1)}, f32[6,1,128]{2,1,0:T(1,128)S(1)}, u32[]{:S(2)}, u32[]{:S(2)}) collective-permute-start(f32[6,1,128]{2,1,0:T(1,128)S(1)} %get-tuple-element.43), channel_id=1, source_target_pairs={{0,3},{1,0},{2,1},{3,2},{4,7},{5,4},{6,5},{7,6},{8,11},{9,8},{10,9... | collective-permute-start | bytes 9224 | tf_op jit(solution)/shard_map/ppermute | solution.py:637
  49.2 1.6 %collective-permute-done.8 = f32[6,1,128]{2,1,0:T(1,128)S(1)} collective-permute-done((f32[6,1,128]{2,1,0:T(1,128)S(1)}, f32[6,1,128]{2,1,0:T(1,128)S(1)}, u32[]{:S(2)}, u32[]{:S(2)}) %collective-permute-start.8) | collective-permute-done | bytes 3104 | tf_op jit(solution)/shard_map/ppermute | solution.py:637
  50.8 0.6 %add_bitcast_fusion = f32[1,6,128]{2,0,1:T(1,128)} fusion(f32[6,1,128]{2,1,0:T(1,128)S(1)} %collective-permute-done.8, f32[6,1,128]{2,1,0:T(1,128)S(1)} %collective-permute-done.9), kind=kLoop, calls=%fused_computation | loop fusion | flops 768 | bytes 9216 | tf_op jit(solution)/shard_map/reshape | solution.py:639
  (28 shorter events, 0.1 us)
Async XLA Ops:
  0.6 18.0 %collective-permute-start = (f32[64,1024]{1,0:T(8,128)}, f32[64,1024]{1,0:T(8,128)S(1)}, u32[]{:S(2)}, u32[]{:S(2)}) collective-permute-start(f32[64,1024]{1,0:T(8,128)} %features.3), channel_id=1, source_target_pairs={{0,1},{1,2},{2,3},{3,0},{4,5},{5,6},{6,7},{7,4},{8,9},{9,10},{10,1... | collective-permute-start | bytes 786440 | tf_op jit(solution)/shard_map/ppermute | solution.py:506
  3.7 14.9 %collective-permute-start.1 = (f32[64,1024]{1,0:T(8,128)}, f32[64,1024]{1,0:T(8,128)S(1)}, u32[]{:S(2)}, u32[]{:S(2)}) collective-permute-start(f32[64,1024]{1,0:T(8,128)} %features.3), channel_id=1, source_target_pairs={{0,3},{1,0},{2,1},{3,2},{4,7},{5,4},{6,5},{7,6},{8,11},{9,8},{10,9... | collective-permute-start | bytes 786440 | tf_op jit(solution)/shard_map/ppermute | solution.py:507
  5.8 0.7 %copy-start.10 = (f32[1,3,1024]{2,0,1:T(1,128)S(1)}, f32[1,3,1024]{2,0,1:T(1,128)}, u32[]{:S(2)}) copy-start(f32[1,3,1024]{2,0,1:T(1,128)} %param.13) | copy-start | bytes 36868
  6.5 0.7 %copy-start.12 = (s32[8]{0:T(128)S(1)}, s32[8]{0:T(128)}, u32[]{:S(2)}) copy-start(s32[8]{0:T(128)} %counts.1) | copy-start | bytes 100
  7.2 3.3 %copy-start = (f32[64,1024]{1,0:T(8,128)S(1)}, f32[64,1024]{1,0:T(8,128)}, u32[]{:S(2)}) copy-start(f32[64,1024]{1,0:T(8,128)} %features.3) | copy-start | bytes 786436
  7.2 3.3 %copy-start.1 = (bf16[4,64,64]{2,1,0:T(8,128)(2,1)S(1)}, bf16[4,64,64]{2,1,0:T(8,128)(2,1)}, u32[]{:S(2)}) copy-start(bf16[4,64,64]{2,1,0:T(8,128)(2,1)} %param.18) | copy-start | bytes 98308
  7.2 3.4 %copy-start.5 = (f32[4]{0:T(128)S(1)}, f32[4]{0:T(128)}, u32[]{:S(2)}) copy-start(f32[4]{0:T(128)} %radial_width.5) | copy-start | bytes 52
  7.2 3.4 %copy-start.7 = (s32[2,120]{1,0:T(2,128)S(1)}, s32[2,120]{1,0:T(2,128)}, u32[]{:S(2)}) copy-start(s32[2,120]{1,0:T(2,128)} %pairs.1) | copy-start | bytes 2884
  7.2 3.4 %copy-start.9 = (bf16[64]{0:T(256)(128)(2,1)S(1)}, bf16[64]{0:T(256)(128)(2,1)}, u32[]{:S(2)}) copy-start(bf16[64]{0:T(256)(128)(2,1)} %param.21) | copy-start | bytes 388
  7.2 7.5 %copy-start.11 = (f32[1,3,1024]{2,0,1:T(1,128)S(1)}, f32[1,3,1024]{2,0,1:T(1,128)}, u32[]{:S(2)}) copy-start(f32[1,3,1024]{2,0,1:T(1,128)} %param.13) | copy-start | bytes 36868
  7.2 11.4 %copy-start.2 = (bf16[64,64]{1,0:T(8,128)(2,1)S(1)}, bf16[64,64]{1,0:T(8,128)(2,1)}, u32[]{:S(2)}) copy-start(bf16[64,64]{1,0:T(8,128)(2,1)} %update_weight.1) | copy-start | bytes 24580
  7.2 11.4 %copy-start.3 = (bf16[64,64]{1,0:T(8,128)(2,1)S(1)}, bf16[64,64]{1,0:T(8,128)(2,1)}, u32[]{:S(2)}) copy-start(bf16[64,64]{1,0:T(8,128)(2,1)} %mix_weight.1) | copy-start | bytes 24580
  7.8 10.1 %collective-permute-start.3 = (f32[32,128]{1,0:T(8,128)S(1)}, f32[32,128]{1,0:T(8,128)S(1)}, u32[]{:S(2)}, u32[]{:S(2)}) collective-permute-start(f32[32,128]{1,0:T(8,128)S(1)} %shard_map.156.small), channel_id=1, source_target_pairs={{0,3},{1,0},{2,1},{3,2},{4,7},{5,4},{6,5},{7,6},{8,11},{9,8},{10,9... | collective-permute-start | bytes 49160 | tf_op jit(solution)/shard_map/ppermute | solution.py:519
  9.8 8.8 %collective-permute-start.2 = (f32[32,128]{1,0:T(8,128)S(1)}, f32[32,128]{1,0:T(8,128)S(1)}, u32[]{:S(2)}, u32[]{:S(2)}) collective-permute-start(f32[32,128]{1,0:T(8,128)S(1)} %shard_map.156.small), channel_id=1, source_target_pairs={{0,1},{1,2},{2,3},{3,0},{4,5},{5,6},{6,7},{7,4},{8,9},{9,10},{10,1... | collective-permute-start | bytes 49160 | tf_op jit(solution)/shard_map/ppermute | solution.py:518
  14.7 26.5 %collective-permute-start.7 = (f32[24,128]{1,0:T(8,128)S(1)}, f32[24,128]{1,0:T(8,128)S(1)}, u32[]{:S(2)}, u32[]{:S(2)}) collective-permute-start(f32[24,128]{1,0:T(8,128)S(1)} %bitcast.16), channel_id=1, source_target_pairs={{0,28},{4,0},{8,4},{12,8},{16,12},{20,16},{24,20},{28,24},{1,29},{... | collective-permute-start | bytes 36872 | tf_op jit(solution)/shard_map/ppermute | solution.py:568
  17.8 23.4 %collective-permute-start.6 = (f32[24,128]{1,0:T(8,128)S(1)}, f32[24,128]{1,0:T(8,128)S(1)}, u32[]{:S(2)}, u32[]{:S(2)}) collective-permute-start(f32[24,128]{1,0:T(8,128)S(1)} %bitcast.17), channel_id=1, source_target_pairs={{0,4},{4,8},{8,12},{12,16},{16,20},{20,24},{24,28},{28,0},{1,5},{5... | collective-permute-start | bytes 36872 | tf_op jit(solution)/shard_map/ppermute | solution.py:567
  31.7 11.9 %copy-start.4 = (f32[1,3,1024]{2,0,1:T(1,128)S(1)}, f32[1,3,1024]{2,0,1:T(1,128)}, u32[]{:S(2)}) copy-start(f32[1,3,1024]{2,0,1:T(1,128)} %param.14) | copy-start | bytes 36868
  31.7 11.9 %copy-start.6 = (f32[1024]{0:T(1024)S(1)}, f32[1024]{0:T(1024)}, u32[]{:S(2)}) copy-start(f32[1024]{0:T(1024)} %param.16) | copy-start | bytes 12292
  31.7 11.8 %copy-start.8 = (s32[2,64]{1,0:T(2,128)S(1)}, s32[2,64]{1,0:T(2,128)}, u32[]{:S(2)}) copy-start(s32[2,64]{1,0:T(2,128)} %leaving.1) | copy-start | bytes 1540
  31.7 9.5 %collective-permute-start.4 = (f32[24,128]{1,0:T(8,128)S(1)}, f32[24,128]{1,0:T(8,128)S(1)}, u32[]{:S(2)}, u32[]{:S(2)}) collective-permute-start(f32[24,128]{1,0:T(8,128)S(1)} %get-tuple-element.36), channel_id=1, source_target_pairs={{0,3},{1,0},{2,1},{3,2},{4,7},{5,4},{6,5},{7,6},{8,11},{9,8},{10,9... | collective-permute-start | bytes 36872 | tf_op jit(solution)/shard_map/ppermute | solution.py:607
  38.1 5.5 %collective-permute-start.5 = (f32[24,128]{1,0:T(8,128)S(1)}, f32[24,128]{1,0:T(8,128)S(1)}, u32[]{:S(2)}, u32[]{:S(2)}) collective-permute-start(f32[24,128]{1,0:T(8,128)S(1)} %get-tuple-element.37), channel_id=1, source_target_pairs={{0,1},{1,2},{2,3},{3,0},{4,5},{5,6},{6,7},{7,4},{8,9},{9,10},{10,1... | collective-permute-start | bytes 36872 | tf_op jit(solution)/shard_map/ppermute | solution.py:608
  44.2 6.6 %collective-permute-start.8 = (f32[6,1,128]{2,1,0:T(1,128)S(1)}, f32[6,1,128]{2,1,0:T(1,128)S(1)}, u32[]{:S(2)}, u32[]{:S(2)}) collective-permute-start(f32[6,1,128]{2,1,0:T(1,128)S(1)} %get-tuple-element.42), channel_id=1, source_target_pairs={{0,1},{1,2},{2,3},{3,0},{4,5},{5,6},{6,7},{7,4},{8,9},{9,10},{10,1... | collective-permute-start | bytes 9224 | tf_op jit(solution)/shard_map/ppermute | solution.py:637
  46.9 3.9 %collective-permute-start.9 = (f32[6,1,128]{2,1,0:T(1,128)S(1)}, f32[6,1,128]{2,1,0:T(1,128)S(1)}, u32[]{:S(2)}, u32[]{:S(2)}) collective-permute-start(f32[6,1,128]{2,1,0:T(1,128)S(1)} %get-tuple-element.43), channel_id=1, source_target_pairs={{0,3},{1,0},{2,1},{3,2},{4,7},{5,4},{6,5},{7,6},{8,11},{9,8},{10,9... | collective-permute-start | bytes 9224 | tf_op jit(solution)/shard_map/ppermute | solution.py:637

commit v5 on v4

--- a/solution.py
+++ b/solution.py
@@ -16,20 +16,24 @@
 PLACES = 3 * CELLS
 SMALL = PLACES + CELLS
 
-CUTOFF_SQUARE = 36.0
+CUTOFF = 6.0
+CUTOFF_SQUARE = CUTOFF * CUTOFF
 CELL_SIDE = 10.0
 MESSAGE_SCALE = 0.25
 SPRING_RATE = 0.2
 LOG2E = 1.4426950408889634
 FAR = 1.0e9
+REACH = 1.001
+FEWER = 96
 CHUNK = 16
-GROUP = 4
+GROUP = 8
+BATCH = 8
 
 f32 = jnp.float32
 bf16 = jnp.bfloat16
 VMEM = pl.BlockSpec(memory_space=pltpu.VMEM)
 SMEM = pl.BlockSpec(memory_space=pltpu.SMEM)
-PARAMS = pltpu.CompilerParams(vmem_limit_bytes=48 * 1024 * 1024)
+PARAMS = pltpu.CompilerParams(vmem_limit_bytes=32 * 1024 * 1024)
 
 
 def dot(a, b, dims=((1,), (0,))):
@@ -70,7 +74,7 @@
         return own + taken, ghost + 1 - taken
 
     own, ghost = lax.fori_loop(0, npairs[0], step, (jnp.int32(0), jnp.int32(0)))
-    for extra in range(2 * GROUP):
+    for extra in range(2 * BATCH):
         own_list[own + extra] = CELLS * 16
         ghost_list[ghost + extra] = CELLS * 16
     tallies[0] = own
@@ -96,7 +100,7 @@
 
 def fill_columns(small, shift, columns, base):
     third = lax.broadcasted_iota(jnp.int32, (PLACES, BLK), 0) >= 2 * CELLS
-    places = small[0:PLACES, :] + jnp.where(third, shift, 0.0)
+    places = (small[0:PLACES, :] + jnp.where(third, shift, 0.0)) * (1.0 / CUTOFF)
     turned = jnp.concatenate([places, jnp.zeros((BLK - PLACES, BLK), f32)], axis=0).T
     for b in range(CELLS):
         for c in range(3):
@@ -104,6 +108,79 @@
             columns[base + b, c] = jnp.broadcast_to(turned[:, n : n + 1], (BLK, BLK))
 
 
+def near_first(smalls, shifts, small, places):
+    pieces = []
+    for part, shift in zip(smalls, shifts):
+        third = lax.broadcasted_iota(jnp.int32, (PLACES, BLK), 0) >= 2 * CELLS
+        moved = (part[0:PLACES, :] + jnp.where(third, shift, 0.0)) * (1.0 / CUTOFF)
+        pieces += [moved, part[PLACES:SMALL, :]]
+    pieces.append(jnp.zeros((BLK - 2 * SMALL, BLK), f32))
+    flat = jnp.concatenate(pieces, axis=0)
+    places[...] = flat
+    turned = flat.T
+    heights = small[2 * CELLS : PLACES, :] * (1.0 / CUTOFF)
+    held = small[PLACES:SMALL, :] > 0.5
+    lowest = jnp.min(jnp.where(held, heights, FAR))
+    highest = jnp.max(jnp.where(held, heights, -FAR))
+    inside = jnp.logical_and(turned > lowest - REACH, turned < highest + REACH)
+    present = pltpu.roll(turned, BLK - CELLS, 1) > 0.5
+    near = jnp.where(jnp.logical_and(inside, present), 1.0, 0.0)
+    ahead = lax.broadcasted_iota(jnp.int32, (BLK, BLK), 1) < lax.broadcasted_iota(
+        jnp.int32, (BLK, BLK), 0
+    )
+    rank = dot(jnp.where(ahead, 1.0, 0.0).astype(bf16), near.astype(bf16))
+    lane = lax.broadcasted_iota(jnp.int32, (1, BLK), 1)
+    height_lane = jnp.bitwise_and(lax.shift_right_logical(lane, 3), 3) == 2
+    height_lane = jnp.logical_and(height_lane, lane < 2 * SMALL)
+    total = jnp.sum(near, axis=0, keepdims=True)
+    most = jnp.max(jnp.where(height_lane, total, 0.0))
+    return jnp.where(near > 0.5, rank, -1.0), most
+
+
+def fill_ghosts(smalls, features, slots, places, weight, chosen, tables, turned, columns):
+    lane = lax.broadcasted_iota(jnp.int32, (BLK, BLK), 1).astype(f32)
+    for side in range(2):
+        masked = features[side][...] * occupancy(smalls[side])
+        high = masked.astype(bf16).astype(f32)
+        low = masked - high
+        for b in range(CELLS):
+            n = side * CELLS + b
+            place = side * SMALL + 2 * CELLS + b
+            slot = jnp.broadcast_to(slots[:, place : place + 1], (BLK, BLK))
+            pick = jnp.where(slot == lane, 1.0, 0.0).astype(bf16)
+            chosen[n] = pick
+            three = [
+                places[side * SMALL + CELLS * c + b : side * SMALL + CELLS * c + b + 1, :]
+                for c in range(3)
+            ]
+            here = jnp.concatenate(three + [jnp.zeros((5, BLK), f32)], axis=0)
+            first = here.astype(bf16).astype(f32)
+            second = (here - first).astype(bf16).astype(f32)
+            parts = [block_lanes(high, b), block_lanes(low, b)]
+            parts += [first, second, here - first - second]
+            moved = dot(jnp.concatenate(parts, axis=0).astype(bf16), pick)
+            spots = moved[2 * F : 2 * F + 8] + moved[2 * F + 8 : 2 * F + 16] + moved[2 * F + 16 :]
+            for c in range(3):
+                columns[n, c] = jnp.broadcast_to(spots[c : c + 1, :], (BLK, BLK)).T
+            halved = moved[0 : 2 * F]
+            result = dot(weight, halved.astype(bf16))
+            for k in range(RAD):
+                tables[n, :, k * BLK : (k + 1) * BLK] = result[k * F : (k + 1) * F].astype(bf16)
+            turned[n] = halved.T.astype(bf16)
+
+
+def return_ghosts(column_sum, chosen, outs):
+    flat = column_sum[...].T
+    for side in range(2):
+        for b in range(CELLS):
+            n = side * CELLS + b
+            piece = jnp.concatenate([flat[3 * n : 3 * n + 3], jnp.zeros((5, BLK), f32)], axis=0)
+            first = piece.astype(bf16).astype(f32)
+            both = jnp.concatenate([first, piece - first], axis=0).astype(bf16)
+            back = dot(both, chosen[n], ((1,), (1,)))
+            outs[side][3 * b : 3 * b + 3, :] = back[0:3] + back[8:11]
+
+
 def fill_penalty(penalty):
     same = lax.broadcasted_iota(jnp.int32, (BLK, BLK), 0) == lax.broadcasted_iota(
         jnp.int32, (BLK, BLK), 1
@@ -114,6 +191,10 @@
 
 def inverse_widths(radial_width):
     return [1.0 / (radial_width[k] * radial_width[k]) for k in range(RAD)]
+
+
+def decay_rates(inverse):
+    return [value * (-LOG2E * CUTOFF_SQUARE) for value in inverse]
 
 
 def decode(pair_list, p):
@@ -126,19 +207,22 @@
     squared = parts[0] * parts[0] + parts[1] * parts[1] + parts[2] * parts[2]
     if penalty is not None:
         squared = squared + penalty[(i == j).astype(jnp.int32), place, :]
-    remain = jnp.maximum(1.0 - squared * (1.0 / CUTOFF_SQUARE), 0.0)
+    remain = jnp.maximum(1.0 - squared, 0.0)
     return parts, squared, remain
 
 
-def message_pass(pair_list, count, rows, columns, penalty, rates, tables, amps, message):
+def message_pass(
+    pair_list, count, rows, columns, penalty, rates, tables, amps, message, used=BLK
+):
     def amplitudes(p, amp):
         i, j = decode(pair_list, p)
-        for r in range(BLK // CHUNK):
+        for r in range(used // CHUNK):
             place = slice(r * CHUNK, (r + 1) * CHUNK)
             _, squared, remain = separation(rows, columns, penalty, i, j, place)
             cutoff = remain * remain
             for k in range(RAD):
-                value = jnp.exp2(squared * rates[k]) * cutoff
+                decay = jnp.exp2(squared * rates[k])
+                value = decay * cutoff
                 amp[k * BLK + r * CHUNK : k * BLK + (r + 1) * CHUNK, :] = value.astype(bf16)
 
     def multiply(p, amp):
@@ -152,35 +236,37 @@
 
     def step(t, carry):
         for u, amp in enumerate(amps):
-            multiply(GROUP * t + u, amp)
+            multiply(BATCH * t + u, amp)
         for u, amp in enumerate(amps):
-            amplitudes(GROUP * t + GROUP + u, amp)
+            amplitudes(BATCH * t + BATCH + u, amp)
         return carry
 
-    lax.fori_loop(0, (count + GROUP - 1) // GROUP, step, 0)
+    lax.fori_loop(0, (count + BATCH - 1) // BATCH, step, 0)
 
 
 def force_pass(
-    pair_list, count, rows, columns, penalty, rates, doubled, turned, down, grads, row_sum, column_sum
+    pair_list, count, rows, columns, penalty, rates, doubled, turned, down, grads, row_sum, column_sum,
+    used=BLK,
 ):
     lane = lax.broadcasted_iota(jnp.int32, (CHUNK, BLK), 1)
 
     def products(p, grad):
         i, j = decode(pair_list, p)
         right = down[i]
-        grad[...] = dot(turned[j], jnp.concatenate([right, right], axis=0))
+        grad[0:used, :] = dot(turned[j, 0:used, :], jnp.concatenate([right, right], axis=0))
 
     def apply(p, grad):
         i, j = decode(pair_list, p)
         marks = [lane == 3 * j + c for c in range(3)]
         sums = [jnp.zeros((CHUNK, BLK), f32) for _ in range(3)]
-        for r in range(BLK // CHUNK):
+        for r in range(used // CHUNK):
             place = slice(r * CHUNK, (r + 1) * CHUNK)
             parts, squared, remain = separation(rows, columns, penalty, i, j, place)
+            decays = [jnp.exp2(squared * rates[k]) for k in range(RAD)]
             plain = None
             scaled = None
             for k in range(RAD):
-                term = jnp.exp2(squared * rates[k]) * grad[place, k * BLK : (k + 1) * BLK]
+                term = decays[k] * grad[place, k * BLK : (k + 1) * BLK]
                 plain = term if plain is None else plain + term
                 term = term * doubled[k]
                 scaled = term if scaled is None else scaled + term
@@ -244,7 +330,7 @@
     for b in range(CELLS):
         for c in range(3):
             n = CELLS * c + b
-            rows[b, c : c + 1, :] = small[n : n + 1, :]
+            rows[b, c : c + 1, :] = small[n : n + 1, :] * (1.0 / CUTOFF)
         rows[b, 3:8, :] = jnp.zeros((5, BLK), f32)
     masked = features[...] * occupancy(small)
     fill_tables(masked, jnp.concatenate([weight[...], weight[...]], axis=1), tables, 0)
@@ -253,7 +339,7 @@
     fill_penalty(penalty)
     out_column[...] = jnp.broadcast_to(as_column(out_weight[...].astype(f32)), (F, BLK))
     message[...] = jnp.zeros(message.shape, f32)
-    rates = [-LOG2E * inverse for inverse in inverse_widths(radial_width)]
+    rates = decay_rates(inverse_widths(radial_width))
     message_pass(own_list, tallies[0], rows, columns, penalty, rates, tables, amps, message)
 
 
@@ -284,7 +370,7 @@
     downstream = (MESSAGE_SCALE * dot(update_weight[...], first_grad, ((0,), (0,)))).astype(bf16)
     for k in range(RAD):
         mixed = dot(weight[k * F : (k + 1) * F, :], downstream, ((0,), (0,)))
-        mixed = (mixed * (4.0 / CUTOFF_SQUARE)).astype(bf16)
+        mixed = (mixed * (4.0 * CUTOFF / CUTOFF_SQUARE)).astype(bf16)
         for b in range(CELLS):
             down[b, :, k * BLK : (k + 1) * BLK] = block_lanes(mixed, b)
     down[CELLS] = jnp.zeros((F, RAD * BLK), bf16)
@@ -327,25 +413,32 @@
     tables,
     turned,
     columns,
+    chosen,
+    places,
     row_sum,
     column_sum,
     *buffers,
 ):
-    amps, grads = buffers[:GROUP], buffers[GROUP:]
-    fill_columns(small_below, -CELL_SIDE, columns, 0)
-    fill_columns(small_above, CELL_SIDE, columns, CELLS)
+    amps, grads = buffers[:BATCH], buffers[BATCH:]
     doubled_weight = jnp.concatenate([weight[...], weight[...]], axis=1)
-    masked_below = below[...] * occupancy(small_below)
-    masked_above = above[...] * occupancy(small_above)
-    fill_tables(masked_below, doubled_weight, tables, 0)
-    fill_tables(masked_above, doubled_weight, tables, CELLS)
+    smalls = (small_below, small_above)
+    slots, most = near_first(smalls, (-CELL_SIDE, CELL_SIDE), small, places)
+    fill_ghosts(
+        smalls, (below, above), slots, places, doubled_weight, chosen, tables, turned, columns
+    )
     message[...] = own_message[...]
     inverse = inverse_widths(radial_width)
-    rates = [-LOG2E * value for value in inverse]
+    rates = decay_rates(inverse)
     count = tallies[1]
-    message_pass(ghost_list, count, rows, columns, None, rates, tables, amps, message)
-    fill_transposed(below[...] * occupancy(small_below), turned, 0)
-    fill_transposed(above[...] * occupancy(small_above), turned, CELLS)
+    for amp in amps:
+        amp[...] = jnp.zeros(amp.shape, bf16)
+    few = most <= FEWER
+
+    def messages(used):
+        message_pass(ghost_list, count, rows, columns, None, rates, tables, amps, message, used)
+
+    pl.when(few)(partial(messages, FEWER))
+    pl.when(jnp.logical_not(few))(partial(messages, BLK))
     occupied = occupancy(small)
     node_backward(
         message,
@@ -359,24 +452,28 @@
     )
     row_sum[...] = jnp.zeros(row_sum.shape, f32)
     column_sum[...] = jnp.zeros(column_sum.shape, f32)
-    force_pass(
-        ghost_list,
-        count,
-        rows,
-        columns,
-        None,
-        rates,
-        doubled_rates(inverse),
-        turned,
-        down,
-        grads,
-        row_sum,
-        column_sum,
-    )
+
+    def pulls(used):
+        force_pass(
+            ghost_list,
+            count,
+            rows,
+            columns,
+            None,
+            rates,
+            doubled_rates(inverse),
+            turned,
+            down,
+            grads,
+            row_sum,
+            column_sum,
+            used,
+        )
+
+    pl.when(few)(partial(pulls, FEWER))
+    pl.when(jnp.logical_not(few))(partial(pulls, BLK))
     collect_rows(row_sum, row_force)
-    flat = column_sum[...].T
-    ghost_below[...] = flat[0:24]
-    ghost_above[...] = flat[24:48]
+    return_ghosts(column_sum, chosen, (ghost_below, ghost_above))
 
 
 def own_force_kernel(
@@ -397,7 +494,7 @@
     row_sum[...] = jnp.zeros(row_sum.shape, f32)
     column_sum[...] = jnp.zeros(column_sum.shape, f32)
     inverse = inverse_widths(radial_width)
-    rates = [-LOG2E * value for value in inverse]
+    rates = decay_rates(inverse)
     force_pass(
         own_list,
         tallies[0],
@@ -522,7 +619,7 @@
     grad = pltpu.VMEM((BLK, RAD * BLK), f32)
     row_sum = pltpu.VMEM((CELLS + 1, 3, CHUNK, BLK), f32)
     column_sum = pltpu.VMEM((BLK, BLK), f32)
-    listed = shape((pairs.shape[1] + 8,), jnp.int32)
+    listed = shape((pairs.shape[1] + 2 * BATCH,), jnp.int32)
 
     def tables(blocks):
         return pltpu.VMEM((blocks, F, RAD * BLK), bf16)
@@ -552,7 +649,7 @@
         ),
         in_specs=[VMEM] * 2 + [SMEM] * 3 + [VMEM] * 2,
         out_specs=(VMEM, SMEM, SMEM, SMEM) + (VMEM,) * 5,
-        scratch_shapes=[tables(CELLS)] + [amp] * GROUP,
+        scratch_shapes=[tables(CELLS)] + [amp] * BATCH,
         compiler_params=PARAMS,
     )(
         features,
@@ -581,10 +678,12 @@
             tables(2 * CELLS),
             pltpu.VMEM((2 * CELLS, BLK, BLK), bf16),
             pltpu.VMEM((2 * CELLS, 3, BLK, BLK), f32),
+            pltpu.VMEM((2 * CELLS, BLK, BLK), bf16),
+            pltpu.VMEM((BLK, BLK), f32),
             row_sum,
             column_sum,
         ]
-        + [amp] * GROUP
+        + [amp] * BATCH
         + [grad] * GROUP,
         compiler_params=PARAMS,
     )(

time: 51.4 us -> 47.6 us (0.926)
  Pallas kernels: 21.5 us -> 15.9 us
  waiting for transfers between devices: 6.69 us -> 8.64 us
    pallas_call x1, Pallas kernels: 13.1 us -> 9.31 us  [body(): pl.pallas_call(ghost_kernel, out_shape=(shape((PLACES, BLK)), shape((PLAC...]
    ppermute x1, waiting for transfers between devices: 2.31 us -> 3.47 us  [body(): from_below = lax.ppermute(ghost_above, 'dom', up)]
    pallas_call x1, Pallas kernels: 3.14 us -> 1.98 us  [body(): pl.pallas_call(own_force_kernel, out_shape=shape((PLACES, BLK)), in_specs...]
    ppermute x1, waiting for transfers between devices: 2.01 us -> 2.76 us  [body(): small_above = lax.ppermute(small, 'dom', down_ring)]
    pallas_call x1, Pallas kernels: 4.15 us -> 3.41 us  [body(): pl.pallas_call(own_message_kernel, out_shape=(shape((CELLS + 1, F, BLK)),...]
  transfers between devices with their start and end apart: 10 -> 10, of which waited for: 4 -> 4; matrix products, arithmetic and copies ran while one was open for 0% -> 0% of each run, Pallas kernels for 41% -> 32%
where the time goes in v5:
time: 47.6 us; the launch traced here: 47.4 us
  starting transfers between devices  19.4 us (41%)
  Pallas kernels  15.9 us (33%)
  waiting for transfers between devices  8.64 us (18%)
  between operations  1.46 us (3%)
  local copies, waits for them, and re-layouts  1.42 us (3%)
  other arithmetic  0.58 us (1%)
    pallas_call x1, Pallas kernels, body(): pl.pallas_call(ghost_kernel, out_shape=(shape((PLACES, BLK)), shape((PLAC...  9.31 us
    ppermute x1, starting transfers between devices, body(): from_above = lax.ppermute(ghost_below, 'dom', down_ring)  6.52 us
    ppermute x1, waiting for transfers between devices, body(): from_below = lax.ppermute(ghost_above, 'dom', up)  3.47 us
    pallas_call x1, Pallas kernels, body(): pl.pallas_call(own_message_kernel, out_shape=(shape((CELLS + 1, F, BLK)),...  3.41 us
    ppermute x1, starting transfers between devices, body(): below = lax.ppermute(features, 'dom', up)  3.08 us
    ppermute x1, waiting for transfers between devices, body(): small_above = lax.ppermute(small, 'dom', down_ring)  2.76 us
    ppermute x1, starting transfers between devices, body(): lax.ppermute(upward, 'dom', up) + lax.ppermute(downward, 'dom', down_ring)  2.58 us
    ppermute x1, starting transfers between devices, body(): above = lax.ppermute(features, 'dom', down_ring)  2.09 us
  transfers between devices with their start and end apart: 10, of which 4 were waited for; matrix products, arithmetic and copies ran while one was open for 0% of the time, Pallas kernels for 32%

profile of v5, /device:TPU:0, one launch (start us, length us, event | category | flops | bytes accessed | tf_op | source)
XLA Modules:
  0.0 47.4 jit_solution(15100117021429830466)
XLA Ops:
  0.6 3.1 %collective-permute-start = (f32[64,1024]{1,0:T(8,128)}, f32[64,1024]{1,0:T(8,128)S(1)}, u32[]{:S(2)}, u32[]{:S(2)}) collective-permute-start(f32[64,1024]{1,0:T(8,128)} %features.3), channel_id=1, source_target_pairs={{0,1},{1,2},{2,3},{3,0},{4,5},{5,6},{6,7},{7,4},{8,9},{9,10},{10,1... | collective-permute-start | bytes 786440 | tf_op jit(solution)/shard_map/ppermute | solution.py:603
  3.7 2.1 %collective-permute-start.1 = (f32[64,1024]{1,0:T(8,128)}, f32[64,1024]{1,0:T(8,128)S(1)}, u32[]{:S(2)}, u32[]{:S(2)}) collective-permute-start(f32[64,1024]{1,0:T(8,128)} %features.3), channel_id=1, source_target_pairs={{0,3},{1,0},{2,1},{3,2},{4,7},{5,4},{6,5},{7,6},{8,11},{9,8},{10,9... | collective-permute-start | bytes 786440 | tf_op jit(solution)/shard_map/ppermute | solution.py:604
  5.8 0.7 %copy-done.10 = f32[1,3,1024]{2,0,1:T(1,128)S(1)} copy-done((f32[1,3,1024]{2,0,1:T(1,128)S(1)}, f32[1,3,1024]{2,0,1:T(1,128)}, u32[]{:S(2)}) %copy-start.10) | copy-done | bytes 12312
  6.5 0.7 %copy-done.12 = s32[8]{0:T(128)S(1)} copy-done((s32[8]{0:T(128)S(1)}, s32[8]{0:T(128)}, u32[]{:S(2)}) %copy-start.12) | copy-done | bytes 56
  7.2 0.5 %shard_map.156.small = f32[32,128]{1,0:T(8,128)S(1)} custom-call(f32[24,128]{1,0:T(8,128)S(1)} %bitcast.15, s32[8]{0:T(128)S(1)} %copy-done.12), custom_call_target="tpu_custom_call" | custom-call | flops 5000000000 | bytes 15000000 | tf_op jit(solution)/shard_map/pallas_call | solution.py:607
  7.8 2.0 %collective-permute-start.3 = (f32[32,128]{1,0:T(8,128)S(1)}, f32[32,128]{1,0:T(8,128)S(1)}, u32[]{:S(2)}, u32[]{:S(2)}) collective-permute-start(f32[32,128]{1,0:T(8,128)S(1)} %shard_map.156.small), channel_id=1, source_target_pairs={{0,3},{1,0},{2,1},{3,2},{4,7},{5,4},{6,5},{7,6},{8,11},{9,8},{10,9... | collective-permute-start | bytes 49160 | tf_op jit(solution)/shard_map/ppermute | solution.py:616
  9.8 0.1 collective-permute-start.2
  10.6 3.4 %shard_map.157 = (f32[9,64,128]{2,1,0:T(8,128)S(1)}, s32[136]{0:T(256)S(1)}, s32[136]{0:T(256)S(1)}, s32[2]{0:T(128)S(1)}, f32[8,8,128]{2,1,0:T(8,128)S(1)}, /*i...) custom-call(f32[64,1024]{1,0:T(8,128)S(1)} %copy-done, ...), custom_call_target="tpu_custom_call" | custom-call | tf_op jit(solution)/shard_map/pallas_call | solution.py:637
  14.0 1.1 %collective-permute-start.7 = (f32[24,128]{1,0:T(8,128)S(1)}, f32[24,128]{1,0:T(8,128)S(1)}, u32[]{:S(2)}, u32[]{:S(2)}) collective-permute-start(f32[24,128]{1,0:T(8,128)S(1)} %bitcast.16), channel_id=1, source_target_pairs={{0,28},{4,0},{8,4},{12,8},{16,12},{20,16},{24,20},{28,24},{1,29},{... | collective-permute-start | bytes 36872 | tf_op jit(solution)/shard_map/ppermute | solution.py:665
  15.1 2.8 %collective-permute-done.3.small_above = f32[32,128]{1,0:T(8,128)S(1)} collective-permute-done((f32[32,128]{1,0:T(8,128)S(1)}, f32[32,128]{1,0:T(8,128)S(1)}, u32[]{:S(2)}, u32[]{:S(2)}) %collective-permute-start.3) | collective-permute-done | bytes 16416 | tf_op jit(solution)/shard_map/ppermute | solution.py:616
  17.8 0.0 collective-permute-start.6
  17.8 0.8 %collective-permute-done.2.small_below = f32[32,128]{1,0:T(8,128)S(1)} collective-permute-done((f32[32,128]{1,0:T(8,128)S(1)}, f32[32,128]{1,0:T(8,128)S(1)}, u32[]{:S(2)}, u32[]{:S(2)}) %collective-permute-start.2) | collective-permute-done | bytes 16416 | tf_op jit(solution)/shard_map/ppermute | solution.py:615
  18.6 0.0 collective-permute-done.below
  18.6 9.3 %shard_map.158 = (f32[24,128]{1,0:T(8,128)S(1)}, f32[24,128]{1,0:T(8,128)S(1)}, f32[24,128]{1,0:T(8,128)S(1)}, bf16[9,64,512]{2,1,0:T(8,128)(2,1)S(1)}) custom-call(f32[64,1024]{1,0:T(8,128)S(1)} %copy-done, f32[32,128]{1,0:T(8,128)S(1)} %shard_map.156.small, f32[64,1024]{1,0:T(8,128)S(1)} %collective-permute-done.below, ...), custom_call_target="tpu_custom_call" | custom-call | tf_op jit(solution)/shard_map/pallas_call | solution.py:666
  28.0 0.0 copy-start.8
  28.0 6.5 %collective-permute-start.4 = (f32[24,128]{1,0:T(8,128)S(1)}, f32[24,128]{1,0:T(8,128)S(1)}, u32[]{:S(2)}, u32[]{:S(2)}) collective-permute-start(f32[24,128]{1,0:T(8,128)S(1)} %get-tuple-element.36), channel_id=1, source_target_pairs={{0,3},{1,0},{2,1},{3,2},{4,7},{5,4},{6,5},{7,6},{8,11},{9,8},{10,9... | collective-permute-start | bytes 36872 | tf_op jit(solution)/shard_map/ppermute | solution.py:706
  34.5 2.0 %shard_map.159.force = f32[24,128]{1,0:T(8,128)S(1)} custom-call(f32[8,8,128]{2,1,0:T(8,128)S(1)} %get-tuple-element.24.rows, f32[8,3,128,128]{3,2,1,0:T(8,128)S(1)} %get-tuple-element.25.columns, f32[2,128,128]{2,1,0:T(8,128)S(1)} %get-tuple-element.26.penalty, bf16[8,128,128]{2,1,0:T(8,128)(2,1)S(1)} %get-tuple-element.27.turned, ...), custom_call_target="tpu_custom_call" | custom-call | tf_op jit(solution)/shard_map/pallas_call | solution.py:708
  36.5 3.5 %collective-permute-done.5.from_below = f32[24,128]{1,0:T(8,128)S(1)} collective-permute-done((f32[24,128]{1,0:T(8,128)S(1)}, f32[24,128]{1,0:T(8,128)S(1)}, u32[]{:S(2)}, u32[]{:S(2)}) %collective-permute-start.5) | collective-permute-done | bytes 12320 | tf_op jit(solution)/shard_map/ppermute | solution.py:707
  40.0 0.6 %shard_map.160 = (f32[24,128]{1,0:T(8,128)}, f32[24,128]{1,0:T(8,128)}, f32[24,128]{1,0:T(8,128)}, f32[6,1,128]{2,1,0:T(1,128)S(1)}, f32[6,1,128]{2,1,0:T(1,128)S(1)}) custom-call(f32[24,128]{1,0:T(8,128)S(1)} %shard_map.159.force, f32[24,128]{1,0:T(8,128)S(1)} %collective-permute-done.4.from_above, f32[24,128]{1,0:T(8,128)S(1)} %collective-permute-done.5.from_below, ...), custom_call_target="tpu_custom_call" | custom-call | tf_op jit(solution)/shard_map/pallas_call | solution.py:718
  40.6 2.6 %collective-permute-start.8 = (f32[6,1,128]{2,1,0:T(1,128)S(1)}, f32[6,1,128]{2,1,0:T(1,128)S(1)}, u32[]{:S(2)}, u32[]{:S(2)}) collective-permute-start(f32[6,1,128]{2,1,0:T(1,128)S(1)} %get-tuple-element.42), channel_id=1, source_target_pairs={{0,1},{1,2},{2,3},{3,0},{4,5},{5,6},{6,7},{7,4},{8,9},{9,10},{10,1... | collective-permute-start | bytes 9224 | tf_op jit(solution)/shard_map/ppermute | solution.py:736
  43.2 2.0 %collective-permute-start.9 = (f32[6,1,128]{2,1,0:T(1,128)S(1)}, f32[6,1,128]{2,1,0:T(1,128)S(1)}, u32[]{:S(2)}, u32[]{:S(2)}) collective-permute-start(f32[6,1,128]{2,1,0:T(1,128)S(1)} %get-tuple-element.43), channel_id=1, source_target_pairs={{0,3},{1,0},{2,1},{3,2},{4,7},{5,4},{6,5},{7,6},{8,11},{9,8},{10,9... | collective-permute-start | bytes 9224 | tf_op jit(solution)/shard_map/ppermute | solution.py:736
  45.2 1.6 %collective-permute-done.8 = f32[6,1,128]{2,1,0:T(1,128)S(1)} collective-permute-done((f32[6,1,128]{2,1,0:T(1,128)S(1)}, f32[6,1,128]{2,1,0:T(1,128)S(1)}, u32[]{:S(2)}, u32[]{:S(2)}) %collective-permute-start.8) | collective-permute-done | bytes 3104 | tf_op jit(solution)/shard_map/ppermute | solution.py:736
  46.8 0.1 collective-permute-done.9
  46.8 0.6 %add_bitcast_fusion = f32[1,6,128]{2,0,1:T(1,128)} fusion(f32[6,1,128]{2,1,0:T(1,128)S(1)} %collective-permute-done.8, f32[6,1,128]{2,1,0:T(1,128)S(1)} %collective-permute-done.9), kind=kLoop, calls=%fused_computation | loop fusion | flops 768 | bytes 9216 | tf_op jit(solution)/shard_map/reshape | solution.py:738
  (28 shorter events, 0.1 us)
Async XLA Ops:
  0.6 18.0 %collective-permute-start = (f32[64,1024]{1,0:T(8,128)}, f32[64,1024]{1,0:T(8,128)S(1)}, u32[]{:S(2)}, u32[]{:S(2)}) collective-permute-start(f32[64,1024]{1,0:T(8,128)} %features.3), channel_id=1, source_target_pairs={{0,1},{1,2},{2,3},{3,0},{4,5},{5,6},{6,7},{7,4},{8,9},{9,10},{10,1... | collective-permute-start | bytes 786440 | tf_op jit(solution)/shard_map/ppermute | solution.py:603
  3.7 14.9 %collective-permute-start.1 = (f32[64,1024]{1,0:T(8,128)}, f32[64,1024]{1,0:T(8,128)S(1)}, u32[]{:S(2)}, u32[]{:S(2)}) collective-permute-start(f32[64,1024]{1,0:T(8,128)} %features.3), channel_id=1, source_target_pairs={{0,3},{1,0},{2,1},{3,2},{4,7},{5,4},{6,5},{7,6},{8,11},{9,8},{10,9... | collective-permute-start | bytes 786440 | tf_op jit(solution)/shard_map/ppermute | solution.py:604
  5.8 0.7 %copy-start.10 = (f32[1,3,1024]{2,0,1:T(1,128)S(1)}, f32[1,3,1024]{2,0,1:T(1,128)}, u32[]{:S(2)}) copy-start(f32[1,3,1024]{2,0,1:T(1,128)} %param.13) | copy-start | bytes 36868
  6.5 0.7 %copy-start.12 = (s32[8]{0:T(128)S(1)}, s32[8]{0:T(128)}, u32[]{:S(2)}) copy-start(s32[8]{0:T(128)} %counts.1) | copy-start | bytes 100
  7.2 3.3 %copy-start = (f32[64,1024]{1,0:T(8,128)S(1)}, f32[64,1024]{1,0:T(8,128)}, u32[]{:S(2)}) copy-start(f32[64,1024]{1,0:T(8,128)} %features.3) | copy-start | bytes 786436
  7.2 3.3 %copy-start.1 = (bf16[4,64,64]{2,1,0:T(8,128)(2,1)S(1)}, bf16[4,64,64]{2,1,0:T(8,128)(2,1)}, u32[]{:S(2)}) copy-start(bf16[4,64,64]{2,1,0:T(8,128)(2,1)} %param.18) | copy-start | bytes 98308
  7.2 3.4 %copy-start.5 = (f32[4]{0:T(128)S(1)}, f32[4]{0:T(128)}, u32[]{:S(2)}) copy-start(f32[4]{0:T(128)} %radial_width.5) | copy-start | bytes 52
  7.2 3.4 %copy-start.7 = (s32[2,120]{1,0:T(2,128)S(1)}, s32[2,120]{1,0:T(2,128)}, u32[]{:S(2)}) copy-start(s32[2,120]{1,0:T(2,128)} %pairs.1) | copy-start | bytes 2884
  7.2 3.4 %copy-start.9 = (bf16[64]{0:T(256)(128)(2,1)S(1)}, bf16[64]{0:T(256)(128)(2,1)}, u32[]{:S(2)}) copy-start(bf16[64]{0:T(256)(128)(2,1)} %param.21) | copy-start | bytes 388
  7.2 6.8 %copy-start.11 = (f32[1,3,1024]{2,0,1:T(1,128)S(1)}, f32[1,3,1024]{2,0,1:T(1,128)}, u32[]{:S(2)}) copy-start(f32[1,3,1024]{2,0,1:T(1,128)} %param.13) | copy-start | bytes 36868
  7.2 11.4 %copy-start.2 = (bf16[64,64]{1,0:T(8,128)(2,1)S(1)}, bf16[64,64]{1,0:T(8,128)(2,1)}, u32[]{:S(2)}) copy-start(bf16[64,64]{1,0:T(8,128)(2,1)} %update_weight.1) | copy-start | bytes 24580
  7.2 11.4 %copy-start.3 = (bf16[64,64]{1,0:T(8,128)(2,1)S(1)}, bf16[64,64]{1,0:T(8,128)(2,1)}, u32[]{:S(2)}) copy-start(bf16[64,64]{1,0:T(8,128)(2,1)} %mix_weight.1) | copy-start | bytes 24580
  7.8 10.1 %collective-permute-start.3 = (f32[32,128]{1,0:T(8,128)S(1)}, f32[32,128]{1,0:T(8,128)S(1)}, u32[]{:S(2)}, u32[]{:S(2)}) collective-permute-start(f32[32,128]{1,0:T(8,128)S(1)} %shard_map.156.small), channel_id=1, source_target_pairs={{0,3},{1,0},{2,1},{3,2},{4,7},{5,4},{6,5},{7,6},{8,11},{9,8},{10,9... | collective-permute-start | bytes 49160 | tf_op jit(solution)/shard_map/ppermute | solution.py:616
  9.8 8.8 %collective-permute-start.2 = (f32[32,128]{1,0:T(8,128)S(1)}, f32[32,128]{1,0:T(8,128)S(1)}, u32[]{:S(2)}, u32[]{:S(2)}) collective-permute-start(f32[32,128]{1,0:T(8,128)S(1)} %shard_map.156.small), channel_id=1, source_target_pairs={{0,1},{1,2},{2,3},{3,0},{4,5},{5,6},{6,7},{7,4},{8,9},{9,10},{10,1... | collective-permute-start | bytes 49160 | tf_op jit(solution)/shard_map/ppermute | solution.py:615
  14.0 22.5 %collective-permute-start.7 = (f32[24,128]{1,0:T(8,128)S(1)}, f32[24,128]{1,0:T(8,128)S(1)}, u32[]{:S(2)}, u32[]{:S(2)}) collective-permute-start(f32[24,128]{1,0:T(8,128)S(1)} %bitcast.16), channel_id=1, source_target_pairs={{0,28},{4,0},{8,4},{12,8},{16,12},{20,16},{24,20},{28,24},{1,29},{... | collective-permute-start | bytes 36872 | tf_op jit(solution)/shard_map/ppermute | solution.py:665
  17.8 18.7 %collective-permute-start.6 = (f32[24,128]{1,0:T(8,128)S(1)}, f32[24,128]{1,0:T(8,128)S(1)}, u32[]{:S(2)}, u32[]{:S(2)}) collective-permute-start(f32[24,128]{1,0:T(8,128)S(1)} %bitcast.17), channel_id=1, source_target_pairs={{0,4},{4,8},{8,12},{12,16},{16,20},{20,24},{24,28},{28,0},{1,5},{5... | collective-permute-start | bytes 36872 | tf_op jit(solution)/shard_map/ppermute | solution.py:664
  27.9 12.1 %copy-start.4 = (f32[1,3,1024]{2,0,1:T(1,128)S(1)}, f32[1,3,1024]{2,0,1:T(1,128)}, u32[]{:S(2)}) copy-start(f32[1,3,1024]{2,0,1:T(1,128)} %param.14) | copy-start | bytes 36868
  27.9 12.1 %copy-start.6 = (f32[1024]{0:T(1024)S(1)}, f32[1024]{0:T(1024)}, u32[]{:S(2)}) copy-start(f32[1024]{0:T(1024)} %param.16) | copy-start | bytes 12292
  28.0 12.0 %copy-start.8 = (s32[2,64]{1,0:T(2,128)S(1)}, s32[2,64]{1,0:T(2,128)}, u32[]{:S(2)}) copy-start(s32[2,64]{1,0:T(2,128)} %leaving.1) | copy-start | bytes 1540
  28.0 8.5 %collective-permute-start.4 = (f32[24,128]{1,0:T(8,128)S(1)}, f32[24,128]{1,0:T(8,128)S(1)}, u32[]{:S(2)}, u32[]{:S(2)}) collective-permute-start(f32[24,128]{1,0:T(8,128)S(1)} %get-tuple-element.36), channel_id=1, source_target_pairs={{0,3},{1,0},{2,1},{3,2},{4,7},{5,4},{6,5},{7,6},{8,11},{9,8},{10,9... | collective-permute-start | bytes 36872 | tf_op jit(solution)/shard_map/ppermute | solution.py:706
  34.5 5.5 %collective-permute-start.5 = (f32[24,128]{1,0:T(8,128)S(1)}, f32[24,128]{1,0:T(8,128)S(1)}, u32[]{:S(2)}, u32[]{:S(2)}) collective-permute-start(f32[24,128]{1,0:T(8,128)S(1)} %get-tuple-element.37), channel_id=1, source_target_pairs={{0,1},{1,2},{2,3},{3,0},{4,5},{5,6},{6,7},{7,4},{8,9},{9,10},{10,1... | collective-permute-start | bytes 36872 | tf_op jit(solution)/shard_map/ppermute | solution.py:707
  40.6 6.1 %collective-permute-start.8 = (f32[6,1,128]{2,1,0:T(1,128)S(1)}, f32[6,1,128]{2,1,0:T(1,128)S(1)}, u32[]{:S(2)}, u32[]{:S(2)}) collective-permute-start(f32[6,1,128]{2,1,0:T(1,128)S(1)} %get-tuple-element.42), channel_id=1, source_target_pairs={{0,1},{1,2},{2,3},{3,0},{4,5},{5,6},{6,7},{7,4},{8,9},{9,10},{10,1... | collective-permute-start | bytes 9224 | tf_op jit(solution)/shard_map/ppermute | solution.py:736
  43.2 3.6 %collective-permute-start.9 = (f32[6,1,128]{2,1,0:T(1,128)S(1)}, f32[6,1,128]{2,1,0:T(1,128)S(1)}, u32[]{:S(2)}, u32[]{:S(2)}) collective-permute-start(f32[6,1,128]{2,1,0:T(1,128)S(1)} %get-tuple-element.43), channel_id=1, source_target_pairs={{0,3},{1,0},{2,1},{3,2},{4,7},{5,4},{6,5},{7,6},{8,11},{9,8},{10,9... | collective-permute-start | bytes 9224 | tf_op jit(solution)/shard_map/ppermute | solution.py:736

commit v6 on v5

--- a/solution.py
+++ b/solution.py
@@ -101,11 +101,10 @@
 def fill_columns(small, shift, columns, base):
     third = lax.broadcasted_iota(jnp.int32, (PLACES, BLK), 0) >= 2 * CELLS
     places = (small[0:PLACES, :] + jnp.where(third, shift, 0.0)) * (1.0 / CUTOFF)
-    turned = jnp.concatenate([places, jnp.zeros((BLK - PLACES, BLK), f32)], axis=0).T
     for b in range(CELLS):
         for c in range(3):
             n = CELLS * c + b
-            columns[base + b, c] = jnp.broadcast_to(turned[:, n : n + 1], (BLK, BLK))
+            columns[base + b, c] = jnp.broadcast_to(places[n : n + 1, :], (BLK, BLK)).T
 
 
 def near_first(smalls, shifts, small, places):
@@ -241,7 +240,13 @@
             amplitudes(BATCH * t + BATCH + u, amp)
         return carry
 
-    lax.fori_loop(0, (count + BATCH - 1) // BATCH, step, 0)
+    groups = (count + BATCH - 1) // BATCH
+    lax.fori_loop(0, groups - 1, step, 0)
+
+    @pl.when(count > 0)
+    def _():
+        for u, amp in enumerate(amps):
+            multiply(BATCH * (groups - 1) + u, amp)
 
 
 def force_pass(
@@ -320,10 +325,10 @@
     tallies,
     rows,
     columns,
-    penalty,
     turned,
     out_column,
     tables,
+    penalty,
     *amps,
 ):
     split_lists(pairs, npairs, own_list, ghost_list, tallies)
@@ -479,7 +484,6 @@
 def own_force_kernel(
     rows,
     columns,
-    penalty,
     turned,
     row_force,
     down,
@@ -500,7 +504,7 @@
         tallies[0],
         rows,
         columns,
-        penalty,
+        None,
         rates,
         doubled_rates(inverse),
         turned,
@@ -631,7 +635,6 @@
         tallies,
         rows,
         columns,
-        penalty,
         turned,
         out_column,
     ) = pl.pallas_call(
@@ -643,13 +646,12 @@
             shape((2,), jnp.int32),
             shape((CELLS, 8, BLK)),
             shape((CELLS, 3, BLK, BLK)),
-            shape((2, BLK, BLK)),
             shape((CELLS, BLK, BLK), bf16),
             shape((F, BLK)),
         ),
         in_specs=[VMEM] * 2 + [SMEM] * 3 + [VMEM] * 2,
-        out_specs=(VMEM, SMEM, SMEM, SMEM) + (VMEM,) * 5,
-        scratch_shapes=[tables(CELLS)] + [amp] * BATCH,
+        out_specs=(VMEM, SMEM, SMEM, SMEM) + (VMEM,) * 4,
+        scratch_shapes=[tables(CELLS), pltpu.VMEM((2, BLK, BLK), f32)] + [amp] * BATCH,
         compiler_params=PARAMS,
     )(
         features,
@@ -708,11 +710,11 @@
     force = pl.pallas_call(
         own_force_kernel,
         out_shape=shape((PLACES, BLK)),
-        in_specs=[VMEM] * 6 + [SMEM] * 3,
+        in_specs=[VMEM] * 5 + [SMEM] * 3,
         out_specs=VMEM,
         scratch_shapes=[row_sum, column_sum] + [grad] * GROUP,
         compiler_params=PARAMS,
-    )(rows, columns, penalty, turned, row_force, down, own_list, tallies, radial_width)
+    )(rows, columns, turned, row_force, down, own_list, tallies, radial_width)
     whole = shape((PLACES, BLK))
     packet = shape((6, 1, 2 * MIG))
     forces, positions_new, momenta_new, upward, downward = pl.pallas_call(

time: 47.6 us -> 47.5 us (level)
  Pallas kernels: 15.9 us -> 12.9 us
  waiting for transfers between devices: 8.64 us -> 10.9 us
  starting transfers between devices: 19.4 us -> 20 us
    pallas_call x1, Pallas kernels: 9.31 us -> 6.88 us  [body(): pl.pallas_call(ghost_kernel, out_shape=(shape((PLACES, BLK)), shape((PLAC...]
    ppermute x1, starting transfers between devices: 1.98 us -> 0.86 us  [body(): lax.ppermute(downward, 'dom', down_ring)]
    ppermute x1, waiting for transfers between devices: 0.05 us -> 1.17 us  [body(): lax.ppermute(downward, 'dom', down_ring)]
    ppermute x1, starting transfers between devices: 2.58 us -> 3.56 us  [body(): lax.ppermute(upward, 'dom', up) + lax.ppermute(downward, 'dom', down_ring)]
    ppermute x1, starting transfers between devices: 6.52 us -> 7.23 us  [body(): from_above = lax.ppermute(ghost_below, 'dom', down_ring)]
    ppermute x1, waiting for transfers between devices: 3.47 us -> 4.06 us  [body(): from_below = lax.ppermute(ghost_above, 'dom', up)]
    pallas_call x1, Pallas kernels: 3.41 us -> 2.84 us  [body(): pl.pallas_call(own_message_kernel, out_shape=(shape((CELLS + 1, F, BLK)),...]
    ppermute x1, waiting for transfers between devices: 2.76 us -> 3.32 us  [body(): small_above = lax.ppermute(small, 'dom', down_ring)]
  transfers between devices with their start and end apart: 10 -> 10, of which waited for: 4 -> 5; matrix products, arithmetic and copies ran while one was open for 0% -> 0% of each run, Pallas kernels for 32% -> 26%
where the time goes in v6:
time: 47.5 us; the launch traced here: 47.2 us
  starting transfers between devices  20 us (42%)
  Pallas kernels  12.9 us (27%)
  waiting for transfers between devices  10.9 us (23%)
  between operations  1.46 us (3%)
  local copies, waits for them, and re-layouts  1.42 us (3%)
  other arithmetic  0.58 us (1%)
    ppermute x1, starting transfers between devices, body(): from_above = lax.ppermute(ghost_below, 'dom', down_ring)  7.23 us
    pallas_call x1, Pallas kernels, body(): pl.pallas_call(ghost_kernel, out_shape=(shape((PLACES, BLK)), shape((PLAC...  6.88 us
    ppermute x1, waiting for transfers between devices, body(): from_below = lax.ppermute(ghost_above, 'dom', up)  4.06 us
    ppermute x1, starting transfers between devices, body(): lax.ppermute(upward, 'dom', up) + lax.ppermute(downward, 'dom', down_ring)  3.56 us
    ppermute x1, waiting for transfers between devices, body(): small_above = lax.ppermute(small, 'dom', down_ring)  3.32 us
    ppermute x1, starting transfers between devices, body(): below = lax.ppermute(features, 'dom', up)  3.08 us
    pallas_call x1, Pallas kernels, body(): pl.pallas_call(own_message_kernel, out_shape=(shape((CELLS + 1, F, BLK)),...  2.84 us
    ppermute x1, starting transfers between devices, body(): above = lax.ppermute(features, 'dom', down_ring)  2.09 us
  transfers between devices with their start and end apart: 10, of which 5 were waited for; matrix products, arithmetic and copies ran while one was open for 0% of the time, Pallas kernels for 26%

profile of v6, /device:TPU:0, one launch (start us, length us, event | category | flops | bytes accessed | tf_op | source)
XLA Modules:
  0.0 47.2 jit_solution(6206515882639528976)
XLA Ops:
  0.6 3.1 %collective-permute-start = (f32[64,1024]{1,0:T(8,128)}, f32[64,1024]{1,0:T(8,128)S(1)}, u32[]{:S(2)}, u32[]{:S(2)}) collective-permute-start(f32[64,1024]{1,0:T(8,128)} %features.3), channel_id=1, source_target_pairs={{0,1},{1,2},{2,3},{3,0},{4,5},{5,6},{6,7},{7,4},{8,9},{9,10},{10,1... | collective-permute-start | bytes 786440 | tf_op jit(solution)/shard_map/ppermute | solution.py:607
  3.7 2.1 %collective-permute-start.1 = (f32[64,1024]{1,0:T(8,128)}, f32[64,1024]{1,0:T(8,128)S(1)}, u32[]{:S(2)}, u32[]{:S(2)}) collective-permute-start(f32[64,1024]{1,0:T(8,128)} %features.3), channel_id=1, source_target_pairs={{0,3},{1,0},{2,1},{3,2},{4,7},{5,4},{6,5},{7,6},{8,11},{9,8},{10,9... | collective-permute-start | bytes 786440 | tf_op jit(solution)/shard_map/ppermute | solution.py:608
  5.8 0.7 %copy-done.10 = f32[1,3,1024]{2,0,1:T(1,128)S(1)} copy-done((f32[1,3,1024]{2,0,1:T(1,128)S(1)}, f32[1,3,1024]{2,0,1:T(1,128)}, u32[]{:S(2)}) %copy-start.10) | copy-done | bytes 12312
  6.5 0.7 %copy-done.12 = s32[8]{0:T(128)S(1)} copy-done((s32[8]{0:T(128)S(1)}, s32[8]{0:T(128)}, u32[]{:S(2)}) %copy-start.12) | copy-done | bytes 56
  7.2 0.5 %shard_map.156.small = f32[32,128]{1,0:T(8,128)S(1)} custom-call(f32[24,128]{1,0:T(8,128)S(1)} %bitcast.15, s32[8]{0:T(128)S(1)} %copy-done.12), custom_call_target="tpu_custom_call" | custom-call | flops 5000000000 | bytes 15000000 | tf_op jit(solution)/shard_map/pallas_call | solution.py:611
  7.8 2.0 %collective-permute-start.3 = (f32[32,128]{1,0:T(8,128)S(1)}, f32[32,128]{1,0:T(8,128)S(1)}, u32[]{:S(2)}, u32[]{:S(2)}) collective-permute-start(f32[32,128]{1,0:T(8,128)S(1)} %shard_map.156.small), channel_id=1, source_target_pairs={{0,3},{1,0},{2,1},{3,2},{4,7},{5,4},{6,5},{7,6},{8,11},{9,8},{10,9... | collective-permute-start | bytes 49160 | tf_op jit(solution)/shard_map/ppermute | solution.py:620
  9.8 0.1 collective-permute-start.2
  10.6 2.8 %shard_map.157 = (f32[9,64,128]{2,1,0:T(8,128)S(1)}, s32[136]{0:T(256)S(1)}, s32[136]{0:T(256)S(1)}, s32[2]{0:T(128)S(1)}, f32[8,8,128]{2,1,0:T(8,128)S(1)}, /*i...) custom-call(f32[64,1024]{1,0:T(8,128)S(1)} %copy-done, ...), custom_call_target="tpu_custom_call" | custom-call | tf_op jit(solution)/shard_map/pallas_call | solution.py:640
  13.4 1.1 %collective-permute-start.7 = (f32[24,128]{1,0:T(8,128)S(1)}, f32[24,128]{1,0:T(8,128)S(1)}, u32[]{:S(2)}, u32[]{:S(2)}) collective-permute-start(f32[24,128]{1,0:T(8,128)S(1)} %bitcast.16), channel_id=1, source_target_pairs={{0,28},{4,0},{8,4},{12,8},{16,12},{20,16},{24,20},{28,24},{1,29},{... | collective-permute-start | bytes 36872 | tf_op jit(solution)/shard_map/ppermute | solution.py:667
  14.5 3.3 %collective-permute-done.3.small_above = f32[32,128]{1,0:T(8,128)S(1)} collective-permute-done((f32[32,128]{1,0:T(8,128)S(1)}, f32[32,128]{1,0:T(8,128)S(1)}, u32[]{:S(2)}, u32[]{:S(2)}) %collective-permute-start.3) | collective-permute-done | bytes 16416 | tf_op jit(solution)/shard_map/ppermute | solution.py:620
  17.8 0.0 collective-permute-start.6
  17.8 0.8 %collective-permute-done.2.small_below = f32[32,128]{1,0:T(8,128)S(1)} collective-permute-done((f32[32,128]{1,0:T(8,128)S(1)}, f32[32,128]{1,0:T(8,128)S(1)}, u32[]{:S(2)}, u32[]{:S(2)}) %collective-permute-start.2) | collective-permute-done | bytes 16416 | tf_op jit(solution)/shard_map/ppermute | solution.py:619
  18.6 6.9 %shard_map.158 = (f32[24,128]{1,0:T(8,128)S(1)}, f32[24,128]{1,0:T(8,128)S(1)}, f32[24,128]{1,0:T(8,128)S(1)}, bf16[9,64,512]{2,1,0:T(8,128)(2,1)S(1)}) custom-call(f32[64,1024]{1,0:T(8,128)S(1)} %copy-done, f32[32,128]{1,0:T(8,128)S(1)} %shard_map.156.small, f32[64,1024]{1,0:T(8,128)S(1)} %collective-permute-done.below, ...), custom_call_target="tpu_custom_call" | custom-call | tf_op jit(solution)/shard_map/pallas_call | solution.py:668
  25.5 0.0 copy-start.8
  25.5 7.2 %collective-permute-start.4 = (f32[24,128]{1,0:T(8,128)S(1)}, f32[24,128]{1,0:T(8,128)S(1)}, u32[]{:S(2)}, u32[]{:S(2)}) collective-permute-start(f32[24,128]{1,0:T(8,128)S(1)} %get-tuple-element.34), channel_id=1, source_target_pairs={{0,3},{1,0},{2,1},{3,2},{4,7},{5,4},{6,5},{7,6},{8,11},{9,8},{10,9... | collective-permute-start | bytes 36872 | tf_op jit(solution)/shard_map/ppermute | solution.py:708
  32.8 0.0 collective-permute-start.5
  32.8 2.0 %shard_map.159.force = f32[24,128]{1,0:T(8,128)S(1)} custom-call(f32[8,8,128]{2,1,0:T(8,128)S(1)} %get-tuple-element.23.rows, f32[8,3,128,128]{3,2,1,0:T(8,128)S(1)} %get-tuple-element.24.columns, bf16[8,128,128]{2,1,0:T(8,128)(2,1)S(1)} %get-tuple-element.25.turned, f32[24,128]{1,0:T(8,128)S(1)} %get-tuple-element.31.row_force, ...), custom_call_target="tpu_custom_call" | custom-call | tf_op jit(solution)/shard_map/pallas_call | solution.py:710
  34.8 4.1 %collective-permute-done.5.from_below = f32[24,128]{1,0:T(8,128)S(1)} collective-permute-done((f32[24,128]{1,0:T(8,128)S(1)}, f32[24,128]{1,0:T(8,128)S(1)}, u32[]{:S(2)}, u32[]{:S(2)}) %collective-permute-start.5) | collective-permute-done | bytes 12320 | tf_op jit(solution)/shard_map/ppermute | solution.py:709
  38.9 0.6 %shard_map.160 = (f32[24,128]{1,0:T(8,128)}, f32[24,128]{1,0:T(8,128)}, f32[24,128]{1,0:T(8,128)}, f32[6,1,128]{2,1,0:T(1,128)S(1)}, f32[6,1,128]{2,1,0:T(1,128)S(1)}) custom-call(f32[24,128]{1,0:T(8,128)S(1)} %shard_map.159.force, f32[24,128]{1,0:T(8,128)S(1)} %collective-permute-done.4.from_above, f32[24,128]{1,0:T(8,128)S(1)} %collective-permute-done.5.from_below, ...), custom_call_target="tpu_custom_call" | custom-call | tf_op jit(solution)/shard_map/pallas_call | solution.py:720
  39.5 3.6 %collective-permute-start.8 = (f32[6,1,128]{2,1,0:T(1,128)S(1)}, f32[6,1,128]{2,1,0:T(1,128)S(1)}, u32[]{:S(2)}, u32[]{:S(2)}) collective-permute-start(f32[6,1,128]{2,1,0:T(1,128)S(1)} %get-tuple-element.40), channel_id=1, source_target_pairs={{0,1},{1,2},{2,3},{3,0},{4,5},{5,6},{6,7},{7,4},{8,9},{9,10},{10,1... | collective-permute-start | bytes 9224 | tf_op jit(solution)/shard_map/ppermute | solution.py:738
  43.1 0.9 %collective-permute-start.9 = (f32[6,1,128]{2,1,0:T(1,128)S(1)}, f32[6,1,128]{2,1,0:T(1,128)S(1)}, u32[]{:S(2)}, u32[]{:S(2)}) collective-permute-start(f32[6,1,128]{2,1,0:T(1,128)S(1)} %get-tuple-element.41), channel_id=1, source_target_pairs={{0,3},{1,0},{2,1},{3,2},{4,7},{5,4},{6,5},{7,6},{8,11},{9,8},{10,9... | collective-permute-start | bytes 9224 | tf_op jit(solution)/shard_map/ppermute | solution.py:738
  43.9 1.6 %collective-permute-done.8 = f32[6,1,128]{2,1,0:T(1,128)S(1)} collective-permute-done((f32[6,1,128]{2,1,0:T(1,128)S(1)}, f32[6,1,128]{2,1,0:T(1,128)S(1)}, u32[]{:S(2)}, u32[]{:S(2)}) %collective-permute-start.8) | collective-permute-done | bytes 3104 | tf_op jit(solution)/shard_map/ppermute | solution.py:738
  45.5 1.2 %collective-permute-done.9 = f32[6,1,128]{2,1,0:T(1,128)S(1)} collective-permute-done((f32[6,1,128]{2,1,0:T(1,128)S(1)}, f32[6,1,128]{2,1,0:T(1,128)S(1)}, u32[]{:S(2)}, u32[]{:S(2)}) %collective-permute-start.9) | collective-permute-done | bytes 3104 | tf_op jit(solution)/shard_map/ppermute | solution.py:738
  46.6 0.6 %add_bitcast_fusion = f32[1,6,128]{2,0,1:T(1,128)} fusion(f32[6,1,128]{2,1,0:T(1,128)S(1)} %collective-permute-done.8, f32[6,1,128]{2,1,0:T(1,128)S(1)} %collective-permute-done.9), kind=kLoop, calls=%fused_computation | loop fusion | flops 768 | bytes 9216 | tf_op jit(solution)/shard_map/reshape | solution.py:740
  (28 shorter events, 0.1 us)
Async XLA Ops:
  0.6 18.0 %collective-permute-start = (f32[64,1024]{1,0:T(8,128)}, f32[64,1024]{1,0:T(8,128)S(1)}, u32[]{:S(2)}, u32[]{:S(2)}) collective-permute-start(f32[64,1024]{1,0:T(8,128)} %features.3), channel_id=1, source_target_pairs={{0,1},{1,2},{2,3},{3,0},{4,5},{5,6},{6,7},{7,4},{8,9},{9,10},{10,1... | collective-permute-start | bytes 786440 | tf_op jit(solution)/shard_map/ppermute | solution.py:607
  3.7 14.9 %collective-permute-start.1 = (f32[64,1024]{1,0:T(8,128)}, f32[64,1024]{1,0:T(8,128)S(1)}, u32[]{:S(2)}, u32[]{:S(2)}) collective-permute-start(f32[64,1024]{1,0:T(8,128)} %features.3), channel_id=1, source_target_pairs={{0,3},{1,0},{2,1},{3,2},{4,7},{5,4},{6,5},{7,6},{8,11},{9,8},{10,9... | collective-permute-start | bytes 786440 | tf_op jit(solution)/shard_map/ppermute | solution.py:608
  5.8 0.7 %copy-start.10 = (f32[1,3,1024]{2,0,1:T(1,128)S(1)}, f32[1,3,1024]{2,0,1:T(1,128)}, u32[]{:S(2)}) copy-start(f32[1,3,1024]{2,0,1:T(1,128)} %param.13) | copy-start | bytes 36868
  6.5 0.7 %copy-start.12 = (s32[8]{0:T(128)S(1)}, s32[8]{0:T(128)}, u32[]{:S(2)}) copy-start(s32[8]{0:T(128)} %counts.1) | copy-start | bytes 100
  7.2 3.3 %copy-start = (f32[64,1024]{1,0:T(8,128)S(1)}, f32[64,1024]{1,0:T(8,128)}, u32[]{:S(2)}) copy-start(f32[64,1024]{1,0:T(8,128)} %features.3) | copy-start | bytes 786436
  7.2 3.3 %copy-start.1 = (bf16[4,64,64]{2,1,0:T(8,128)(2,1)S(1)}, bf16[4,64,64]{2,1,0:T(8,128)(2,1)}, u32[]{:S(2)}) copy-start(bf16[4,64,64]{2,1,0:T(8,128)(2,1)} %param.18) | copy-start | bytes 98308
  7.2 3.4 %copy-start.5 = (f32[4]{0:T(128)S(1)}, f32[4]{0:T(128)}, u32[]{:S(2)}) copy-start(f32[4]{0:T(128)} %radial_width.5) | copy-start | bytes 52
  7.2 3.4 %copy-start.7 = (s32[2,120]{1,0:T(2,128)S(1)}, s32[2,120]{1,0:T(2,128)}, u32[]{:S(2)}) copy-start(s32[2,120]{1,0:T(2,128)} %pairs.1) | copy-start | bytes 2884
  7.2 3.4 %copy-start.9 = (bf16[64]{0:T(256)(128)(2,1)S(1)}, bf16[64]{0:T(256)(128)(2,1)}, u32[]{:S(2)}) copy-start(bf16[64]{0:T(256)(128)(2,1)} %param.21) | copy-start | bytes 388
  7.2 6.2 %copy-start.11 = (f32[1,3,1024]{2,0,1:T(1,128)S(1)}, f32[1,3,1024]{2,0,1:T(1,128)}, u32[]{:S(2)}) copy-start(f32[1,3,1024]{2,0,1:T(1,128)} %param.13) | copy-start | bytes 36868
  7.2 11.4 %copy-start.2 = (bf16[64,64]{1,0:T(8,128)(2,1)S(1)}, bf16[64,64]{1,0:T(8,128)(2,1)}, u32[]{:S(2)}) copy-start(bf16[64,64]{1,0:T(8,128)(2,1)} %update_weight.1) | copy-start | bytes 24580
  7.2 11.4 %copy-start.3 = (bf16[64,64]{1,0:T(8,128)(2,1)S(1)}, bf16[64,64]{1,0:T(8,128)(2,1)}, u32[]{:S(2)}) copy-start(bf16[64,64]{1,0:T(8,128)(2,1)} %mix_weight.1) | copy-start | bytes 24580
  7.8 10.1 %collective-permute-start.3 = (f32[32,128]{1,0:T(8,128)S(1)}, f32[32,128]{1,0:T(8,128)S(1)}, u32[]{:S(2)}, u32[]{:S(2)}) collective-permute-start(f32[32,128]{1,0:T(8,128)S(1)} %shard_map.156.small), channel_id=1, source_target_pairs={{0,3},{1,0},{2,1},{3,2},{4,7},{5,4},{6,5},{7,6},{8,11},{9,8},{10,9... | collective-permute-start | bytes 49160 | tf_op jit(solution)/shard_map/ppermute | solution.py:620
  9.8 8.8 %collective-permute-start.2 = (f32[32,128]{1,0:T(8,128)S(1)}, f32[32,128]{1,0:T(8,128)S(1)}, u32[]{:S(2)}, u32[]{:S(2)}) collective-permute-start(f32[32,128]{1,0:T(8,128)S(1)} %shard_map.156.small), channel_id=1, source_target_pairs={{0,1},{1,2},{2,3},{3,0},{4,5},{5,6},{6,7},{7,4},{8,9},{9,10},{10,1... | collective-permute-start | bytes 49160 | tf_op jit(solution)/shard_map/ppermute | solution.py:619
  13.4 21.3 %collective-permute-start.7 = (f32[24,128]{1,0:T(8,128)S(1)}, f32[24,128]{1,0:T(8,128)S(1)}, u32[]{:S(2)}, u32[]{:S(2)}) collective-permute-start(f32[24,128]{1,0:T(8,128)S(1)} %bitcast.16), channel_id=1, source_target_pairs={{0,28},{4,0},{8,4},{12,8},{16,12},{20,16},{24,20},{28,24},{1,29},{... | collective-permute-start | bytes 36872 | tf_op jit(solution)/shard_map/ppermute | solution.py:667
  17.8 16.9 %collective-permute-start.6 = (f32[24,128]{1,0:T(8,128)S(1)}, f32[24,128]{1,0:T(8,128)S(1)}, u32[]{:S(2)}, u32[]{:S(2)}) collective-permute-start(f32[24,128]{1,0:T(8,128)S(1)} %bitcast.17), channel_id=1, source_target_pairs={{0,4},{4,8},{8,12},{12,16},{16,20},{20,24},{24,28},{28,0},{1,5},{5... | collective-permute-start | bytes 36872 | tf_op jit(solution)/shard_map/ppermute | solution.py:666
  25.5 13.3 %copy-start.4 = (f32[1,3,1024]{2,0,1:T(1,128)S(1)}, f32[1,3,1024]{2,0,1:T(1,128)}, u32[]{:S(2)}) copy-start(f32[1,3,1024]{2,0,1:T(1,128)} %param.14) | copy-start | bytes 36868
  25.5 13.3 %copy-start.6 = (f32[1024]{0:T(1024)S(1)}, f32[1024]{0:T(1024)}, u32[]{:S(2)}) copy-start(f32[1024]{0:T(1024)} %param.16) | copy-start | bytes 12292
  25.5 13.3 %copy-start.8 = (s32[2,64]{1,0:T(2,128)S(1)}, s32[2,64]{1,0:T(2,128)}, u32[]{:S(2)}) copy-start(s32[2,64]{1,0:T(2,128)} %leaving.1) | copy-start | bytes 1540
  25.5 9.2 %collective-permute-start.4 = (f32[24,128]{1,0:T(8,128)S(1)}, f32[24,128]{1,0:T(8,128)S(1)}, u32[]{:S(2)}, u32[]{:S(2)}) collective-permute-start(f32[24,128]{1,0:T(8,128)S(1)} %get-tuple-element.34), channel_id=1, source_target_pairs={{0,3},{1,0},{2,1},{3,2},{4,7},{5,4},{6,5},{7,6},{8,11},{9,8},{10,9... | collective-permute-start | bytes 36872 | tf_op jit(solution)/shard_map/ppermute | solution.py:708
  32.8 6.1 %collective-permute-start.5 = (f32[24,128]{1,0:T(8,128)S(1)}, f32[24,128]{1,0:T(8,128)S(1)}, u32[]{:S(2)}, u32[]{:S(2)}) collective-permute-start(f32[24,128]{1,0:T(8,128)S(1)} %get-tuple-element.35), channel_id=1, source_target_pairs={{0,1},{1,2},{2,3},{3,0},{4,5},{5,6},{6,7},{7,4},{8,9},{9,10},{10,1... | collective-permute-start | bytes 36872 | tf_op jit(solution)/shard_map/ppermute | solution.py:709
  39.5 6.0 %collective-permute-start.8 = (f32[6,1,128]{2,1,0:T(1,128)S(1)}, f32[6,1,128]{2,1,0:T(1,128)S(1)}, u32[]{:S(2)}, u32[]{:S(2)}) collective-permute-start(f32[6,1,128]{2,1,0:T(1,128)S(1)} %get-tuple-element.40), channel_id=1, source_target_pairs={{0,1},{1,2},{2,3},{3,0},{4,5},{5,6},{6,7},{7,4},{8,9},{9,10},{10,1... | collective-permute-start | bytes 9224 | tf_op jit(solution)/shard_map/ppermute | solution.py:738
  43.1 3.6 %collective-permute-start.9 = (f32[6,1,128]{2,1,0:T(1,128)S(1)}, f32[6,1,128]{2,1,0:T(1,128)S(1)}, u32[]{:S(2)}, u32[]{:S(2)}) collective-permute-start(f32[6,1,128]{2,1,0:T(1,128)S(1)} %get-tuple-element.41), channel_id=1, source_target_pairs={{0,3},{1,0},{2,1},{3,2},{4,7},{5,4},{6,5},{7,6},{8,11},{9,8},{10,9... | collective-permute-start | bytes 9224 | tf_op jit(solution)/shard_map/ppermute | solution.py:738
